TPU v7x, 256 devices: a whole 4x4x8 slice. The times are simulated.
256 devices in a mesh: dom: 32 (over x_hi, z, core), face: 8 (over y, x_lo).
Axes of the slice: x: 4 (x_hi: 2, x_lo: 2; x = x_hi * 2 + x_lo), y: 4, z: 8, core: 2. Of those that a mesh axis runs over, the one named last changes fastest.
Arguments:
- positions: float32 [3, 65536], P(None, ('dom', 'face')), may hold values from 0 to 3
- species: int32 [65536], P(('dom', 'face')), may hold values from 0 to 6
- send_list: int32 [256, 8, 64], P(('dom', 'face')), may hold values from 0 to 255
- edge_src: int32 [256, 1024], P(('dom', 'face')), may hold values from 0 to 255
- edge_dst: int32 [256, 1024], P(('dom', 'face')), may hold values from 0 to 767
- edge_count: int32 [256], P(('dom', 'face')), may hold values from 256 to 1024, as said below
- w_in: float32 [22, 128], replicated, may hold values from -1.25 to 1.25
- w_mid: float32 [128, 128], replicated, may hold values from -0.5 to 0.5
- w_pair: float32 [128, 128], replicated, may hold values from -0.5 to 0.5
- w_mix: float32 [320, 128], replicated, may hold values from -0.3125 to 0.3125
- w_back: float32 [128, 128], replicated, may hold values from -0.5 to 0.5
- w_read: float32 [128], replicated, may hold values from -0.5 to 0.5
Outputs:
- forces: float32 [3, 65536], P(None, ('dom', 'face'))
- energies: float32 [65536], P(('dom', 'face'))
Inputs may be any that keep to these rules, and one draw needn't show every extreme that they name: The first edge_count[g] pairs of domain g are live and the rest are padding; some domain is full in every draw.
All inputs are finite; a program needn't handle non-finite values.
Results may differ from a plain program's by a relative error of at most 0.0003.
Values sent between devices are 32-bit elements; how exact they have to be, the bound alone decides.
A program may use at most 128 MiB of HBM per device.

v0:
```python
import jax
import jax.numpy as jnp
from jax import lax
from jax.sharding import PartitionSpec as P

CHANNELS = 64
BASIS = 8
SPECIES = 7


ENV_SCALE = 0.2
CUTOFF = 6.0


def padded_2(cells, sides, width):
    for axis, dim in sides:
        count = lax.axis_size(axis)
        head = lax.slice_in_dim(cells, 0, width, axis=dim)
        tail = lax.slice_in_dim(cells, cells.shape[dim] - width, cells.shape[dim], axis=dim)
        cells = jnp.concatenate(
            [
                lax.ppermute(tail, axis, [(i, (i + 1) % count) for i in range(count)]),
                cells,
                lax.ppermute(head, axis, [((i + 1) % count, i) for i in range(count)]),
            ],
            axis=dim,
        )
    return cells


def product_of(left, right):
    return jnp.dot(left, right, precision=lax.Precision.HIGHEST, preferred_element_type=jnp.float32)


def harmonics(direction):
    comp_x = direction[:, 0]
    comp_y = direction[:, 1]
    comp_z = direction[:, 2]
    root3 = 3.0**0.5
    root5 = 5.0**0.5
    root15 = 15.0**0.5
    return jnp.stack(
        [
            jnp.ones_like(comp_x),
            root3 * comp_x,
            root3 * comp_y,
            root3 * comp_z,
            root15 * comp_x * comp_y,
            root15 * comp_y * comp_z,
            0.5 * root5 * (2.0 * comp_z * comp_z - comp_x * comp_x - comp_y * comp_y),
            root15 * comp_x * comp_z,
            0.5 * root15 * (comp_x * comp_x - comp_y * comp_y),
        ],
        axis=1,
    )


def pair_features(pos_centre, pos_partner, spec_centre, spec_partner, is_live, w_in, w_mid, w_pair):
    displace = pos_partner - pos_centre
    soft_len = jnp.sqrt(jnp.sum(displace * displace, axis=1) + 1.0)
    direction = displace / soft_len[:, None]
    orders = jnp.arange(1, BASIS + 1).astype(jnp.float32)
    radial = jnp.sin(jnp.pi * orders[None, :] * soft_len[:, None] / CUTOFF) / soft_len[:, None]
    scaled = soft_len / CUTOFF
    envelope = is_live * (1.0 - scaled * scaled) ** 2
    kinds = jnp.arange(SPECIES)
    hot_centre = (spec_centre[:, None] == kinds[None, :]).astype(jnp.float32)
    hot_partner = (spec_partner[:, None] == kinds[None, :]).astype(jnp.float32)
    inputs = jnp.concatenate([hot_centre, hot_partner, radial], axis=1)
    latent = product_of(jax.nn.silu(product_of(inputs, w_in)), w_mid)
    paired = product_of(latent, w_pair)
    return (latent, paired, harmonics(direction), envelope)


def env_terms(paired, angular, envelope):
    weights = paired[:, :CHANNELS] * (envelope * ENV_SCALE)[:, None]
    return jnp.concatenate([weights * angular[:, order : order + 1] for order in range(9)], axis=1)


def edge_energy(latent, paired, angular, envelope, env_rows, w_cat, w_back, w_read):
    values = paired[:, CHANNELS:]
    parts = [
        env_rows[:, order * CHANNELS : (order + 1) * CHANNELS] * angular[:, order : order + 1]
        for order in range(9)
    ]
    degree_zero = parts[0]
    degree_one = parts[1] + parts[2] + parts[3]
    degree_two = parts[4] + parts[5] + parts[6] + parts[7] + parts[8]
    invariant = jnp.concatenate(
        [degree_zero * values, degree_one * values, degree_two * values], axis=1
    )
    mixed_in = jnp.concatenate([latent, invariant], axis=1)
    updated = latent + product_of(jax.nn.silu(product_of(mixed_in, w_cat)), w_back)
    return envelope * product_of(updated, w_read)


def neighbour_swap(outgoing):
    layout = jnp.concatenate([outgoing[:4], jnp.zeros_like(outgoing[:1]), outgoing[4:]], axis=0)
    layout = layout.reshape((3, 3) + outgoing.shape[1:])
    padded = padded_2(layout, (("dom", 0), ("face", 1)), 1)
    picked = padded[::2, ::2].reshape((9,) + outgoing.shape[1:])
    return jnp.concatenate([picked[:4], picked[5:]], axis=0)


def return_ghosts(ghost_data, send_rows, owned):
    arrived = neighbour_swap(ghost_data.reshape((8, send_rows.shape[1], ghost_data.shape[-1])))
    return jax.ops.segment_sum(
        arrived.reshape(-1, ghost_data.shape[-1]), send_rows.reshape(-1), num_segments=owned
    )


def send_ghosts(owned_data, send_rows):
    arrived = neighbour_swap(owned_data[send_rows])
    return arrived.reshape(-1, owned_data.shape[-1])


def per_device(
    positions,
    species,
    send_list,
    edge_src,
    edge_dst,
    edge_count,
    w_in,
    w_mid,
    w_pair,
    w_mix,
    w_back,
    w_read,
):
    owned = positions.shape[1]
    send_rows = send_list[0]
    slots = owned + 8 * send_rows.shape[1]
    hidden_width = w_mid.shape[0]
    channel_rows = w_mix[hidden_width:].reshape(CHANNELS, 3, hidden_width)
    w_cat = jnp.concatenate(
        [
            w_mix[:hidden_width],
            jnp.transpose(channel_rows, (1, 0, 2)).reshape(3 * CHANNELS, hidden_width),
        ],
        axis=0,
    )
    coords = positions.T
    payload = jnp.concatenate([coords, species[:, None].astype(jnp.float32)], axis=1)
    arrived = send_ghosts(payload, send_rows)
    pos_ext = jnp.concatenate([coords, arrived[:, :3]], axis=0)
    spec_ext = jnp.concatenate([species, arrived[:, 3].astype(jnp.int32)], axis=0)
    first = edge_src[0]
    second = edge_dst[0]
    centre = jnp.concatenate([first, second])
    partner = jnp.concatenate([second, first])
    is_live = (jnp.arange(first.shape[0]) < edge_count[0]).astype(jnp.float32)
    alive_both = jnp.concatenate([is_live, is_live])

    def geometry(points):
        return pair_features(
            points[centre],
            points[partner],
            spec_ext[centre],
            spec_ext[partner],
            alive_both,
            w_in,
            w_mid,
            w_pair,
        )

    features, geo_pull = jax.vjp(geometry, pos_ext)
    latent, paired, angular, envelope = features

    def partial_env(paired_in, angular_in, envelope_in):
        return jax.ops.segment_sum(
            env_terms(paired_in, angular_in, envelope_in), centre, num_segments=slots
        )

    partial_value, env_pull = jax.vjp(partial_env, paired, angular, envelope)
    env_owned = partial_value[:owned] + return_ghosts(partial_value[owned:], send_rows, owned)
    env_full = jnp.concatenate([env_owned, send_ghosts(env_owned, send_rows)], axis=0)

    def atom_energy(latent_in, paired_in, angular_in, envelope_in, env_in):
        energy = edge_energy(
            latent_in, paired_in, angular_in, envelope_in, env_in[centre], w_cat, w_back, w_read
        )
        return jax.ops.segment_sum(energy, centre, num_segments=slots)

    energy_ext, energy_pull = jax.vjp(atom_energy, latent, paired, angular, envelope, env_full)
    g_lat, g_pair, g_ang, g_env, g_full = energy_pull(jnp.ones_like(energy_ext))
    g_owned = g_full[:owned] + return_ghosts(g_full[owned:], send_rows, owned)
    g_partial = jnp.concatenate([g_owned, send_ghosts(g_owned, send_rows)], axis=0)
    h_pair, h_ang, h_env = env_pull(g_partial)
    (g_points,) = geo_pull((g_lat, g_pair + h_pair, g_ang + h_ang, g_env + h_env))
    joined = jnp.concatenate([g_points, energy_ext[:, None]], axis=1)
    result = joined[:owned] + return_ghosts(joined[owned:], send_rows, owned)
    return ((-result[:, :3]).T, result[:, 3])


def solution(mesh):
    placed = (
        P(None, ("dom", "face")),
        P(("dom", "face")),
        P(("dom", "face"), None, None),
        P(("dom", "face"), None),
        P(("dom", "face"), None),
        P(("dom", "face")),
        P(),
        P(),
        P(),
        P(),
        P(),
        P(),
    )
    return jax.shard_map(
        per_device,
        mesh=mesh,
        in_specs=placed,
        out_specs=(P(None, ("dom", "face")), P(("dom", "face"))),
        check_vma=False,
    )
```

profile of v0, /device:TPU:1, one launch (start us, length us, event | category | flops | bytes accessed | tf_op | source)
XLA Modules:
  0.0 449.6 jit_solution(8913818088150785834)
XLA Ops:
  14.4 8.6 %gather_fusion.7 = f32[2048]{0:T(1024)S(1)} fusion(f32[768]{0:T(1024)S(1)} %broadcast_in_dim.15, s32[2048]{0:T(1024)S(1)} %get-tuple-element.136), kind=kCustom, calls=%fused_computation.7 | custom fusion | bytes 24576 | tf_op jit(solution)/shard_map/transpose(jvp())/gather | solution.py:183
  34.4 8.6 %gather_fusion.3 = s32[2048]{0:T(1024)S(1)} fusion(s32[768]{0:T(1024)S(1)} %pad_add_fusion.4, s32[2048]{0:T(1024)S(1)} %get-tuple-element.140), kind=kCustom, calls=%fused_computation.3 | custom fusion | bytes 24576 | tf_op jit(solution)/shard_map/jvp()/gather | solution.py:159
  43.0 8.6 %gather_fusion.4 = s32[2048]{0:T(1024)S(1)} fusion(s32[768]{0:T(1024)S(1)} %pad_add_fusion.4, s32[2048]{0:T(1024)S(1)} %broadcast_clamp_fusion.2), kind=kCustom, calls=%fused_computation.4 | custom fusion | bytes 24576 | tf_op jit(solution)/shard_map/jvp()/gather | solution.py:160
  66.8 5.8 %copy.177 = f32[2048,576]{1,0:T(8,128)} copy(f32[2048,576]{0,1:T(8,128)} %multiply_dynamic-update-slice_fusion) | data formatting | bytes 9437184 | tf_op jit(solution)/shard_map/jvp()/concatenate | solution.py:77
  72.6 14.9 %scatter_custom_fusion = f32[768,576]{1,0:T(8,128)S(1)} fusion(s32[2048]{0:T(1024)S(1)} %get-tuple-element.137, f32[2048,576]{1,0:T(8,128)} %copy.177, f32[]{:T(128)} %constant.17.clone.1), kind=kCustom, calls=%fused_computation.69 | custom fusion | flops 1179648 | bytes 1769984 | tf_op jit(solution)/shard_map/jvp()/scatter-add | solution.py:171
  102.6 10.5 %collective-permute-done.6 = f32[5,1,64,576]{3,2,1,0:T(8,128)} collective-permute-done((f32[5,1,64,576]{3,2,1,0:T(8,128)}, f32[5,1,64,576]{3,2,1,0:T(8,128)}, u32[]{:S(2)}, u32[]{:S(2)}) %collective-permute-start.6) | collective-permute-done | bytes 737312 | tf_op jit(solution)/shard_map/ppermute | solution.py:22
  113.1 17.1 %collective-permute-done.7 = f32[5,1,64,576]{3,2,1,0:T(8,128)} collective-permute-done((f32[5,1,64,576]{3,2,1,0:T(8,128)}, f32[5,1,64,576]{3,2,1,0:T(8,128)}, u32[]{:S(2)}, u32[]{:S(2)}) %collective-permute-start.7) | collective-permute-done | bytes 737312 | tf_op jit(solution)/shard_map/ppermute | solution.py:24
  138.4 6.2 %collective-permute-start.8 = (f32[1,3,64,576]{3,2,1,0:T(8,128)S(1)}, f32[1,3,64,576]{3,2,1,0:T(8,128)S(1)}, u32[]{:S(2)}, u32[]{:S(2)}) collective-permute-start(f32[1,3,64,576]{3,2,1,0:T(8,128)S(1)} %bitcast.142), channel_id=1, source_target_pairs={{0,8},{8,16},{16,24},{24,32},{32,40},{40,48},{48,56},{56,64},{64,7... | collective-permute-start | bytes 1327112 | tf_op jit(solution)/shard_map/ppermute | solution.py:22
  162.0 10.6 %collective-permute-done.10 = f32[5,1,64,576]{3,2,1,0:T(8,128)} collective-permute-done((f32[5,1,64,576]{3,2,1,0:T(8,128)}, f32[5,1,64,576]{3,2,1,0:T(8,128)}, u32[]{:S(2)}, u32[]{:S(2)}) %collective-permute-start.10) | collective-permute-done | bytes 737312 | tf_op jit(solution)/shard_map/ppermute | solution.py:22
  172.6 14.0 %collective-permute-done.11 = f32[5,1,64,576]{3,2,1,0:T(8,128)} collective-permute-done((f32[5,1,64,576]{3,2,1,0:T(8,128)}, f32[5,1,64,576]{3,2,1,0:T(8,128)}, u32[]{:S(2)}, u32[]{:S(2)}) %collective-permute-start.11) | collective-permute-done | bytes 737312 | tf_op jit(solution)/shard_map/ppermute | solution.py:24
  188.8 9.7 %gather_fusion.6 = f32[2048,576]{1,0:T(8,128)} fusion(f32[768,576]{1,0:T(8,128)S(1)} %pad_maximum_fusion.4, s32[2048]{0:T(1024)S(1)} %get-tuple-element.140), kind=kCustom, calls=%fused_computation.6 | custom fusion | bytes 9445376 | tf_op jit(solution)/shard_map/jvp()/gather | solution.py:181
  198.5 8.0 %fusion.89 = (f32[2048,64]{1,0:T(8,128)}, f32[2048,64]{1,0:T(8,128)}, f32[2048,64]{1,0:T(8,128)}, f32[2048,64]{1,0:T(8,128)S(1)}, f32[2048,64]{1,0:T(8,128)}, /*...) fusion(f32[2048,576]{1,0:T(8,128)} %gather_fusion.6), kind=kLoop, calls=%fused_computation.264 | loop fusion | bytes 9437184 | tf_op jit(solution)/shard_map/jvp()/slice | solution.py:83
  238.7 5.8 %copy.188 = f32[2048,576]{1,0:T(8,128)} copy(f32[2048,576]{0,1:T(8,128)} %pad_add_fusion) | data formatting | bytes 9437184 | tf_op jit(solution)/shard_map/transpose(jvp())/add_any | solution.py:83
  244.5 14.9 %scatter_custom_fusion.2 = f32[768,576]{1,0:T(8,128)S(1)} fusion(s32[2048]{0:T(1024)} %bitcast.214, f32[2048,576]{1,0:T(8,128)} %copy.188, f32[]{:T(128)} %constant.17.clone.1), kind=kCustom, calls=%fused_computation.67 | custom fusion | flops 1179648 | bytes 1769984 | tf_op jit(solution)/shard_map/transpose(jvp())/scatter-add | solution.py:181
  259.5 7.4 %collective-permute-start.12 = (f32[1,3,64,576]{3,2,1,0:T(8,128)S(1)}, f32[1,3,64,576]{3,2,1,0:T(8,128)S(1)}, u32[]{:S(2)}, u32[]{:S(2)}) collective-permute-start(f32[1,3,64,576]{3,2,1,0:T(8,128)S(1)} %bitcast.143), channel_id=1, source_target_pairs={{0,8},{8,16},{16,24},{24,32},{32,40},{40,48},{48,56},{56,64},{64,7... | collective-permute-start | bytes 1327112 | tf_op jit(solution)/shard_map/ppermute | solution.py:22
  281.6 11.5 %collective-permute-done.14 = f32[5,1,64,576]{3,2,1,0:T(8,128)S(1)} collective-permute-done((f32[5,1,64,576]{3,2,1,0:T(8,128)S(1)}, f32[5,1,64,576]{3,2,1,0:T(8,128)S(1)}, u32[]{:S(2)}, u32[]{:S(2)}) %collective-permute-start.14) | collective-permute-done | bytes 737312 | tf_op jit(solution)/shard_map/ppermute | solution.py:22
  293.1 16.2 %collective-permute-done.15 = f32[5,1,64,576]{3,2,1,0:T(8,128)S(1)} collective-permute-done((f32[5,1,64,576]{3,2,1,0:T(8,128)S(1)}, f32[5,1,64,576]{3,2,1,0:T(8,128)S(1)}, u32[]{:S(2)}, u32[]{:S(2)}) %collective-permute-start.15) | collective-permute-done | bytes 737312 | tf_op jit(solution)/shard_map/ppermute | solution.py:24
  335.6 12.2 %collective-permute-done.18 = f32[5,1,64,576]{3,2,1,0:T(8,128)S(1)} collective-permute-done((f32[5,1,64,576]{3,2,1,0:T(8,128)S(1)}, f32[5,1,64,576]{3,2,1,0:T(8,128)S(1)}, u32[]{:S(2)}, u32[]{:S(2)}) %collective-permute-start.18) | collective-permute-done | bytes 737312 | tf_op jit(solution)/shard_map/ppermute | solution.py:22
  347.8 16.3 %collective-permute-done.19 = f32[5,1,64,576]{3,2,1,0:T(8,128)S(1)} collective-permute-done((f32[5,1,64,576]{3,2,1,0:T(8,128)S(1)}, f32[5,1,64,576]{3,2,1,0:T(8,128)S(1)}, u32[]{:S(2)}, u32[]{:S(2)}) %collective-permute-start.19) | collective-permute-done | bytes 737312 | tf_op jit(solution)/shard_map/ppermute | solution.py:24
  365.5 9.3 %gather_fusion.9 = f32[2048,576]{1,0:T(8,128)} fusion(f32[768,576]{1,0:T(8,128)S(1)} %pad_maximum_fusion.5, s32[2048]{0:T(1024)S(1)} %copy-done.39), kind=kCustom, calls=%fused_computation.9 | custom fusion | bytes 9445376 | tf_op jit(solution)/shard_map/transpose(jvp())/gather | solution.py:171
  374.9 5.8 %copy.189 = f32[2048,576]{0,1:T(8,128)} copy(f32[2048,576]{1,0:T(8,128)} %gather_fusion.9) | data formatting | bytes 9437184 | tf_op jit(solution)/shard_map/transpose(jvp())/gather | solution.py:171
  392.7 12.1 %scatter_custom_fusion.5 = f32[768,3]{1,0:T(8,128)S(1)} fusion(s32[2048]{0:T(1024)} %bitcast.215, f32[2048,3]{1,0:T(8,128)S(1)} %copy.193, f32[]{:T(128)} %constant.17.clone.1), kind=kCustom, calls=%fused_computation.142 | custom fusion | flops 6144 | bytes 9728 | tf_op jit(solution)/shard_map/transpose(jvp())/scatter-add | solution.py:157
  405.2 11.7 %scatter_custom_fusion.4 = f32[768,3]{1,0:T(8,128)S(1)} fusion(s32[2048]{0:T(1024)} %bitcast.217, f32[2048,3]{1,0:T(8,128)S(1)} %copy.192, f32[]{:T(128)} %constant.17.clone.1), kind=kCustom, calls=%fused_computation.144 | custom fusion | flops 6144 | bytes 9728 | tf_op jit(solution)/shard_map/transpose(jvp())/scatter-add | solution.py:158
  417.1 14.8 %scatter_custom_fusion.6 = f32[768]{0:T(1024)S(1)} fusion(s32[2048]{0:T(1024)} %copy-done.61, f32[2048]{0:T(1024)S(1)} %get-tuple-element.125, f32[]{:T(128)} %constant.17.clone.1), kind=kCustom, calls=%fused_computation.245 | custom fusion | flops 2048 | bytes 3584 | tf_op jit(solution)/shard_map/jvp()/scatter-add | solution.py:183
  (343 shorter events, 186.0 us)
Async XLA Ops:
  4.2 5.1 %collective-permute-start = (f32[1,3,64,4]{2,3,1,0:T(4,128)S(1)}, f32[1,3,64,4]{2,3,1,0:T(4,128)S(1)}, u32[]{:S(2)}, u32[]{:S(2)}) collective-permute-start(f32[1,3,64,4]{2,3,1,0:T(4,128)S(1)} %copy.167), channel_id=1, source_target_pairs={{0,8},{8,16},{16,24},{24,32},{32,40},{40,48},{48,56},{56,64},{64,7... | collective-permute-start | bytes 9224 | tf_op jit(solution)/shard_map/ppermute | solution.py:22
  7.3 3.1 collective-permute-start.1
  10.4 12.7 %collective-permute-start.2 = (f32[5,1,64,4]{2,3,1,0:T(4,128)S(1)}, f32[5,1,64,4]{2,3,1,0:T(4,128)S(1)}, u32[]{:S(2)}, u32[]{:S(2)}) collective-permute-start(f32[5,1,64,4]{2,3,1,0:T(4,128)S(1)} %get-tuple-element.119), channel_id=1, source_target_pairs={{0,1},{1,2},{2,3},{3,4},{4,5},{5,6},{6,7},{7,0},{8,9},{9,10},{10,1... | collective-permute-start | bytes 15368 | tf_op jit(solution)/shard_map/ppermute | solution.py:22
  11.7 11.4 %collective-permute-start.3 = (f32[5,1,64,4]{2,3,1,0:T(4,128)S(1)}, f32[5,1,64,4]{2,3,1,0:T(4,128)S(1)}, u32[]{:S(2)}, u32[]{:S(2)}) collective-permute-start(f32[5,1,64,4]{2,3,1,0:T(4,128)S(1)} %get-tuple-element.120), channel_id=1, source_target_pairs={{1,0},{2,1},{3,2},{4,3},{5,4},{6,5},{7,6},{0,7},{9,8},{10,9},{11,1... | collective-permute-start | bytes 15368 | tf_op jit(solution)/shard_map/ppermute | solution.py:24
  87.6 6.7 %collective-permute-start.4 = (f32[1,3,64,576]{3,2,1,0:T(8,128)S(1)}, f32[1,3,64,576]{3,2,1,0:T(8,128)S(1)}, u32[]{:S(2)}, u32[]{:S(2)}) collective-permute-start(f32[1,3,64,576]{3,2,1,0:T(8,128)S(1)} %bitcast.141), channel_id=1, source_target_pairs={{0,8},{8,16},{16,24},{24,32},{32,40},{40,48},{48,56},{56,64},{64,7... | collective-permute-start | bytes 1327112 | tf_op jit(solution)/shard_map/ppermute | solution.py:22
  88.4 8.4 %collective-permute-start.5 = (f32[1,3,64,576]{3,2,1,0:T(8,128)S(1)}, f32[1,3,64,576]{3,2,1,0:T(8,128)S(1)}, u32[]{:S(2)}, u32[]{:S(2)}) collective-permute-start(f32[1,3,64,576]{3,2,1,0:T(8,128)S(1)} %bitcast.137), channel_id=1, source_target_pairs={{8,0},{16,8},{24,16},{32,24},{40,32},{48,40},{56,48},{64,56},{72,6... | collective-permute-start | bytes 1327112 | tf_op jit(solution)/shard_map/ppermute | solution.py:24
  99.0 14.1 %collective-permute-start.6 = (f32[5,1,64,576]{3,2,1,0:T(8,128)}, f32[5,1,64,576]{3,2,1,0:T(8,128)}, u32[]{:S(2)}, u32[]{:S(2)}) collective-permute-start(f32[5,1,64,576]{3,2,1,0:T(8,128)} %get-tuple-element.66), channel_id=1, source_target_pairs={{0,1},{1,2},{2,3},{3,4},{4,5},{5,6},{6,7},{7,0},{8,9},{9,10},{10,1... | collective-permute-start | bytes 2211848 | tf_op jit(solution)/shard_map/ppermute | solution.py:22
  99.0 31.2 %collective-permute-start.7 = (f32[5,1,64,576]{3,2,1,0:T(8,128)}, f32[5,1,64,576]{3,2,1,0:T(8,128)}, u32[]{:S(2)}, u32[]{:S(2)}) collective-permute-start(f32[5,1,64,576]{3,2,1,0:T(8,128)} %get-tuple-element.67), channel_id=1, source_target_pairs={{1,0},{2,1},{3,2},{4,3},{5,4},{6,5},{7,6},{0,7},{9,8},{10,9},{11,1... | collective-permute-start | bytes 2211848 | tf_op jit(solution)/shard_map/ppermute | solution.py:24
  138.4 12.0 %collective-permute-start.8 = (f32[1,3,64,576]{3,2,1,0:T(8,128)S(1)}, f32[1,3,64,576]{3,2,1,0:T(8,128)S(1)}, u32[]{:S(2)}, u32[]{:S(2)}) collective-permute-start(f32[1,3,64,576]{3,2,1,0:T(8,128)S(1)} %bitcast.142), channel_id=1, source_target_pairs={{0,8},{8,16},{16,24},{24,32},{32,40},{40,48},{48,56},{56,64},{64,7... | collective-permute-start | bytes 1327112 | tf_op jit(solution)/shard_map/ppermute | solution.py:22
  144.7 8.3 %collective-permute-start.9 = (f32[1,3,64,576]{3,2,1,0:T(8,128)S(1)}, f32[1,3,64,576]{3,2,1,0:T(8,128)S(1)}, u32[]{:S(2)}, u32[]{:S(2)}) collective-permute-start(f32[1,3,64,576]{3,2,1,0:T(8,128)S(1)} %bitcast.138), channel_id=1, source_target_pairs={{8,0},{16,8},{24,16},{32,24},{40,32},{48,40},{56,48},{64,56},{72,6... | collective-permute-start | bytes 1327112 | tf_op jit(solution)/shard_map/ppermute | solution.py:24
  154.3 18.3 %collective-permute-start.10 = (f32[5,1,64,576]{3,2,1,0:T(8,128)}, f32[5,1,64,576]{3,2,1,0:T(8,128)}, u32[]{:S(2)}, u32[]{:S(2)}) collective-permute-start(f32[5,1,64,576]{3,2,1,0:T(8,128)} %get-tuple-element.64), channel_id=1, source_target_pairs={{0,1},{1,2},{2,3},{3,4},{4,5},{5,6},{6,7},{7,0},{8,9},{9,10},{10,1... | collective-permute-start | bytes 2211848 | tf_op jit(solution)/shard_map/ppermute | solution.py:22
  154.9 31.8 %collective-permute-start.11 = (f32[5,1,64,576]{3,2,1,0:T(8,128)}, f32[5,1,64,576]{3,2,1,0:T(8,128)}, u32[]{:S(2)}, u32[]{:S(2)}) collective-permute-start(f32[5,1,64,576]{3,2,1,0:T(8,128)} %get-tuple-element.65), channel_id=1, source_target_pairs={{1,0},{2,1},{3,2},{4,3},{5,4},{6,5},{7,6},{0,7},{9,8},{10,9},{11,1... | collective-permute-start | bytes 2211848 | tf_op jit(solution)/shard_map/ppermute | solution.py:24
  259.5 13.2 %collective-permute-start.12 = (f32[1,3,64,576]{3,2,1,0:T(8,128)S(1)}, f32[1,3,64,576]{3,2,1,0:T(8,128)S(1)}, u32[]{:S(2)}, u32[]{:S(2)}) collective-permute-start(f32[1,3,64,576]{3,2,1,0:T(8,128)S(1)} %bitcast.143), channel_id=1, source_target_pairs={{0,8},{8,16},{16,24},{24,32},{32,40},{40,48},{48,56},{56,64},{64,7... | collective-permute-start | bytes 1327112 | tf_op jit(solution)/shard_map/ppermute | solution.py:22
  266.9 8.6 %collective-permute-start.13 = (f32[1,3,64,576]{3,2,1,0:T(8,128)S(1)}, f32[1,3,64,576]{3,2,1,0:T(8,128)S(1)}, u32[]{:S(2)}, u32[]{:S(2)}) collective-permute-start(f32[1,3,64,576]{3,2,1,0:T(8,128)S(1)} %bitcast.139), channel_id=1, source_target_pairs={{8,0},{16,8},{24,16},{32,24},{40,32},{48,40},{56,48},{64,56},{72,6... | collective-permute-start | bytes 1327112 | tf_op jit(solution)/shard_map/ppermute | solution.py:24
  275.6 17.5 %collective-permute-start.14 = (f32[5,1,64,576]{3,2,1,0:T(8,128)S(1)}, f32[5,1,64,576]{3,2,1,0:T(8,128)S(1)}, u32[]{:S(2)}, u32[]{:S(2)}) collective-permute-start(f32[5,1,64,576]{3,2,1,0:T(8,128)S(1)} %get-tuple-element.62), channel_id=1, source_target_pairs={{0,1},{1,2},{2,3},{3,4},{4,5},{5,6},{6,7},{7,0},{8,9},{9,10},{10,1... | collective-permute-start | bytes 2211848 | tf_op jit(solution)/shard_map/ppermute | solution.py:22
  275.9 33.3 %collective-permute-start.15 = (f32[5,1,64,576]{3,2,1,0:T(8,128)S(1)}, f32[5,1,64,576]{3,2,1,0:T(8,128)S(1)}, u32[]{:S(2)}, u32[]{:S(2)}) collective-permute-start(f32[5,1,64,576]{3,2,1,0:T(8,128)S(1)} %get-tuple-element.63), channel_id=1, source_target_pairs={{1,0},{2,1},{3,2},{4,3},{5,4},{6,5},{7,6},{0,7},{9,8},{10,9},{11,1... | collective-permute-start | bytes 2211848 | tf_op jit(solution)/shard_map/ppermute | solution.py:24
  316.8 10.6 %collective-permute-start.16 = (f32[1,3,64,576]{3,2,1,0:T(8,128)S(1)}, f32[1,3,64,576]{3,2,1,0:T(8,128)S(1)}, u32[]{:S(2)}, u32[]{:S(2)}) collective-permute-start(f32[1,3,64,576]{3,2,1,0:T(8,128)S(1)} %bitcast.144), channel_id=1, source_target_pairs={{0,8},{8,16},{16,24},{24,32},{32,40},{40,48},{48,56},{56,64},{64,7... | collective-permute-start | bytes 1327112 | tf_op jit(solution)/shard_map/ppermute | solution.py:22
  321.6 8.6 %collective-permute-start.17 = (f32[1,3,64,576]{3,2,1,0:T(8,128)S(1)}, f32[1,3,64,576]{3,2,1,0:T(8,128)S(1)}, u32[]{:S(2)}, u32[]{:S(2)}) collective-permute-start(f32[1,3,64,576]{3,2,1,0:T(8,128)S(1)} %bitcast.140), channel_id=1, source_target_pairs={{8,0},{16,8},{24,16},{32,24},{40,32},{48,40},{56,48},{64,56},{72,6... | collective-permute-start | bytes 1327112 | tf_op jit(solution)/shard_map/ppermute | solution.py:24
  330.2 17.6 %collective-permute-start.18 = (f32[5,1,64,576]{3,2,1,0:T(8,128)S(1)}, f32[5,1,64,576]{3,2,1,0:T(8,128)S(1)}, u32[]{:S(2)}, u32[]{:S(2)}) collective-permute-start(f32[5,1,64,576]{3,2,1,0:T(8,128)S(1)} %get-tuple-element.60), channel_id=1, source_target_pairs={{0,1},{1,2},{2,3},{3,4},{4,5},{5,6},{6,7},{7,0},{8,9},{9,10},{10,1... | collective-permute-start | bytes 2211848 | tf_op jit(solution)/shard_map/ppermute | solution.py:22
  330.6 33.5 %collective-permute-start.19 = (f32[5,1,64,576]{3,2,1,0:T(8,128)S(1)}, f32[5,1,64,576]{3,2,1,0:T(8,128)S(1)}, u32[]{:S(2)}, u32[]{:S(2)}) collective-permute-start(f32[5,1,64,576]{3,2,1,0:T(8,128)S(1)} %get-tuple-element.61), channel_id=1, source_target_pairs={{1,0},{2,1},{3,2},{4,3},{5,4},{6,5},{7,6},{0,7},{9,8},{10,9},{11,1... | collective-permute-start | bytes 2211848 | tf_op jit(solution)/shard_map/ppermute | solution.py:24
  432.3 6.0 %collective-permute-start.20 = (f32[1,3,64,4]{2,1,3,0:T(4,128)S(1)}, f32[1,3,64,4]{2,1,3,0:T(4,128)S(1)}, u32[]{:S(2)}, u32[]{:S(2)}) collective-permute-start(f32[1,3,64,4]{2,1,3,0:T(4,128)S(1)} %slice.408), channel_id=1, source_target_pairs={{0,8},{8,16},{16,24},{24,32},{32,40},{40,48},{48,56},{56,64},{64,7... | collective-permute-start | bytes 9224 | tf_op jit(solution)/shard_map/ppermute | solution.py:22
  436.6 3.1 collective-permute-start.21
  439.7 4.7 %collective-permute-start.22 = (f32[5,1,64,4]{2,3,1,0:T(4,128)S(1)}, f32[5,1,64,4]{2,3,1,0:T(4,128)S(1)}, u32[]{:S(2)}, u32[]{:S(2)}) collective-permute-start(f32[5,1,64,4]{2,3,1,0:T(4,128)S(1)} %get-tuple-element.117), channel_id=1, source_target_pairs={{0,1},{1,2},{2,3},{3,4},{4,5},{5,6},{6,7},{7,0},{8,9},{9,10},{10,1... | collective-permute-start | bytes 15368 | tf_op jit(solution)/shard_map/ppermute | solution.py:22
  440.4 4.1 collective-permute-start.23
  (73 other events, 1048.5 us)
where the time goes:
time: 459 us; the launch traced here: 450 us
  waiting for transfers between devices  138 us (30%)
  local copies, waits for them, and re-layouts  115 us (25%)
  other arithmetic  113 us (25%)
  starting transfers between devices  56.7 us (12%)
  matrix products  24.3 us (5%)
    ppermute x12, waiting for transfers between devices, padded_2(): lax.ppermute(head, axis, [((i + 1) % count, i) for i in range(count)])  76.8 us
    ppermute x12, waiting for transfers between devices, padded_2(): lax.ppermute(tail, axis, [(i, (i + 1) % count) for i in range(count)])  61.5 us
    ppermute x12, starting transfers between devices, padded_2(): lax.ppermute(tail, axis, [(i, (i + 1) % count) for i in range(count)])  30 us
    ppermute x12, starting transfers between devices, padded_2(): lax.ppermute(head, axis, [((i + 1) % count, i) for i in range(count)])  26.7 us
    dot_general x11, matrix products, product_of(): jnp.dot(left, right, precision=lax.Precision.HIGHEST, preferred_element_t...  24.3 us
    unnamed x158, local copies, waits for them, and re-layouts  22.1 us
    gather x2, local copies, waits for them, and re-layouts, partial_env(): jax.ops.segment_sum(env_terms(paired_in, angular_in, envelope_in), centre...  15.1 us
    scatter-add x1, other arithmetic, atom_energy(): env_in[centre]  14.9 us
  transfers between devices with their start and end apart: 24, of which 20 were waited for; matrix products, arithmetic and copies ran while one was open for 4% of the time, Pallas kernels for 0%

commit v1 on v0

v1 whole, which is shorter than its diff:
```python
import functools

import jax
import jax.numpy as jnp
from jax import lax
from jax.experimental import pallas as pl
from jax.experimental.pallas import tpu as pltpu
from jax.sharding import PartitionSpec as P

CH = 64
WIDTH = 128
BASIS = 8
SPECIES = 7
ENV_SCALE = 0.2
CUTOFF = 6.0
PI = 3.141592653589793
DIRECTIONS = ((-1, -1), (-1, 0), (-1, 1), (0, -1), (0, 1), (1, -1), (1, 0), (1, 1))
NBR = 8
ATOM = 256
GHOST = 64
PAIR = 1024
SLOTS = NBR * GHOST
LIST = PAIR + 128
CAP = 10 * PAIR
EB = 512
F32 = jnp.float32
BF16 = jnp.bfloat16
I32 = jnp.int32
MESH = pl.DeviceIdType.MESH
VMEM = pl.BlockSpec(memory_space=pltpu.VMEM)
SMEM = pl.BlockSpec(memory_space=pltpu.SMEM)
ANY = pl.BlockSpec(memory_space=pl.ANY)

RAD, DRAD, ANG, ENVL, DENVL, RINV, DIR, ERAW, DANG, ROWS = 0, 8, 16, 25, 26, 27, 28, 31, 32, 40


def dot(a, b):
    return lax.dot_general(a, b, (((1,), (0,)), ((), ())), preferred_element_type=F32)


def dot_nt(a, b):
    return lax.dot_general(a, b, (((1,), (1,)), ((), ())), preferred_element_type=F32)


def exact(a, b):
    return jnp.dot(a, b, precision=lax.Precision.HIGHEST, preferred_element_type=F32)


def halves(x):
    high = x.astype(BF16)
    return high, (x - high.astype(F32)).astype(BF16)


def thirds(x):
    high = x.astype(BF16).astype(F32)
    rest = x - high
    mid = rest.astype(BF16).astype(F32)
    return high, mid, rest - mid


def one_hot(row, count):
    rows = lax.broadcasted_iota(I32, (count, row.shape[1]), 0)
    return jnp.where(rows == row, 1.0, 0.0).astype(BF16)


def atom_table(coords, kinds):
    parts = thirds(coords)
    pad = jnp.zeros((6, coords.shape[1]), F32)
    return jnp.concatenate([*parts, kinds, pad], axis=0)


def joined(rows):
    return rows[0:3] + rows[3:6] + rows[6:9]


def greet():
    here = [lax.axis_index("dom"), lax.axis_index("face")]
    sizes = [lax.axis_size("dom"), lax.axis_size("face")]
    peers = []
    for shift in DIRECTIONS:
        peers.append(
            tuple(lax.rem(at + by + size, size) for at, by, size in zip(here, shift, sizes))
        )
    barrier = pltpu.get_barrier_semaphore()
    for peer in peers:
        pl.semaphore_signal(barrier, inc=1, device_id=peer, device_id_type=MESH)
    return barrier, peers


def swap(peers, out_ref, in_ref, send_sem, recv_sem):
    copies = []
    for k, peer in enumerate(peers):
        copies.append(
            pltpu.make_async_remote_copy(
                src_ref=out_ref.at[k],
                dst_ref=in_ref.at[NBR - 1 - k],
                send_sem=send_sem.at[k],
                recv_sem=recv_sem.at[NBR - 1 - k],
                device_id=peer,
                device_id_type=MESH,
            )
        )
    for copy in copies:
        copy.start()
    return copies


def share_kernel(
    count_ref, pos_ref, spec_ref, send_ref, src_ref, dst_ref,
    w_in_ref, w_mid_ref, w_pair_ref, w_mix_ref, w_back_ref, w_read_ref,
    own_ref, table_ref, recv_ref, wx_ref, up_ref, upl_ref, dn_ref, dnl_ref,
    mt_ref, mtl_ref, mb_ref, mbl_ref, wr_ref, wrl_ref, ab_ref,
    out_buf, order_buf, send_sem, recv_sem,
):
    barrier, peers = greet()
    table = atom_table(pos_ref[...], spec_ref[...].astype(F32)).astype(BF16)
    table_ref[...] = table
    sends = jnp.concatenate([send_ref[k : k + 1, :] for k in range(NBR)], axis=1)
    ghosts = dot(table, one_hot(sends, ATOM))
    ghost_rows = jnp.concatenate([joined(ghosts), ghosts[9:10]], axis=0)
    src = src_ref[...]
    dst = dst_ref[...]
    lanes = lax.broadcasted_iota(I32, (1, PAIR), 1)
    live = lanes < count_ref[0]
    ghost = dst >= ATOM
    away = dst - ATOM
    bucket = jnp.where(ghost, (away >> 6) + 1, 0)
    bucket = jnp.where(live, bucket, 15)
    place = jnp.where(ghost, away & 63, dst)
    member = jnp.where(lax.broadcasted_iota(I32, (16, PAIR), 0) == bucket, 1.0, 0.0)
    before = lax.broadcasted_iota(I32, (ATOM, ATOM), 0) < lax.broadcasted_iota(I32, (ATOM, ATOM), 1)
    before = jnp.where(before, 1.0, 0.0).astype(BF16)
    pieces = [member[:, i * ATOM : (i + 1) * ATOM] for i in range(PAIR // ATOM)]
    ranks = dot(jnp.concatenate(pieces, axis=0).astype(BF16), before)
    sums = [jnp.sum(piece, axis=1, keepdims=True) for piece in pieces]
    total = sums[0] + sums[1] + sums[2] + sums[3]
    start = jnp.zeros((16, 1), F32)
    index = lax.broadcasted_iota(I32, (16, 1), 0)
    for b in range(NBR + 1):
        start = start + jnp.where(index > b, total[b : b + 1, :], 0.0)
    offset = start
    spots = []
    for i, piece in enumerate(pieces):
        where = ranks[16 * i : 16 * (i + 1)] + offset
        spots.append(jnp.sum(piece * where, axis=0, keepdims=True))
        offset = offset + sums[i]
    spot = jnp.concatenate(spots, axis=1)
    spot = jnp.where(live, spot, -1.0).astype(I32)
    picked = dot(table, one_hot(src, ATOM))
    data = jnp.concatenate(
        [picked[0:10], place.astype(F32), src.astype(F32), jnp.zeros((4, PAIR), F32)], axis=0
    ).astype(BF16)
    for i in range(PAIR // ATOM):
        rows = lax.broadcasted_iota(I32, (ATOM, PAIR), 0) + i * ATOM
        chosen = jnp.where(rows == spot, 1.0, 0.0).astype(BF16)
        order_buf[:, i * ATOM : (i + 1) * ATOM] = dot_nt(data, chosen)
    ordered = order_buf[...]
    entries = jnp.concatenate(
        [joined(ordered), ordered[9:12], jnp.zeros((2, PAIR), F32)], axis=0
    )
    none = jnp.zeros((8, GHOST), F32)
    for k in range(NBR):
        out_buf[k, :, 0:PAIR] = entries
        mine = jnp.concatenate([ghost_rows[:, k * GHOST : (k + 1) * GHOST], none[0:4]], axis=0)
        out_buf[k, :, PAIR:LIST] = jnp.concatenate([mine, none], axis=1)
        out_buf[k, 4:5, PAIR:LIST] = jnp.broadcast_to(total[k + 1 : k + 2, :], (1, 128))
        out_buf[k, 5:6, PAIR:LIST] = jnp.broadcast_to(start[k + 1 : k + 2, :], (1, 128))
    pl.semaphore_wait(barrier, NBR)
    copies = swap(peers, out_buf, recv_ref, send_sem, recv_sem)
    own_ref[:, 0:PAIR] = entries
    own_ref[:, PAIR:LIST] = jnp.zeros((8, 128), F32)
    own_ref[4:5, PAIR:LIST] = jnp.broadcast_to(total[0:1, :], (1, 128))
    w_in = w_in_ref[...]
    w_c = w_in[0:SPECIES].T
    w_p = w_in[SPECIES : 2 * SPECIES].T
    w_r = w_in[2 * SPECIES :]
    gap = jnp.zeros((WIDTH, 1), F32)
    first = jnp.concatenate([w_c, gap, w_p, gap, w_r.T], axis=1)
    first_high = first.astype(BF16).astype(F32)
    first_low = first - first_high
    wx_ref[...] = jnp.concatenate(
        [first_high, first_high[:, 16:24], first_low, jnp.zeros((WIDTH, 8), F32)], axis=1
    ).astype(BF16)
    wr_high, wr_low = halves(jnp.concatenate([w_r, jnp.zeros((8, WIDTH), F32)], axis=0))
    wr_ref[...] = jnp.concatenate([wr_high, wr_high], axis=1)
    wrl_ref[...] = wr_low
    w_mid = w_mid_ref[...]
    w_read = w_read_ref[...]
    down = jnp.concatenate(
        [exact(w_mid, w_pair_ref[...]), exact(w_mid, w_mix_ref[0:WIDTH, :])], axis=1
    )
    a_col = jnp.sum(w_mid * w_read, axis=1, keepdims=True)
    b_col = jnp.sum(w_back_ref[...] * w_read, axis=1, keepdims=True)
    ab_ref[...] = jnp.concatenate([a_col, b_col], axis=1)
    dn_high, dn_low = halves(down)
    dn_ref[...] = dn_high
    dnl_ref[...] = dn_low
    up = down.T
    up_high, up_low = halves(up)
    up_ref[...] = jnp.concatenate([up_high, up_high], axis=1)
    upl_ref[...] = up_low
    mix = jnp.concatenate(
        [w_mix_ref[pl.ds(WIDTH + degree, CH, stride=3), :] for degree in range(3)], axis=0
    )
    mb_ref[...], mbl_ref[...] = halves(mix)
    mt_ref[...], mtl_ref[...] = halves(mix.T)
    for copy in copies:
        copy.wait()


def edge_kernel(
    count_ref, src_ref, dst_ref, send_ref, own_ref, table_ref, recv_ref,
    wx_ref, up_ref, upl_ref, dn_ref, dnl_ref, mt_ref, mtl_ref, mb_ref, mbl_ref,
    wr_ref, wrl_ref, ab_ref,
    msg_ref, force_ref, energy_ref,
    edges, hots, paired, slope, mixed, mixed_low, d_value, geo, env, g_env,
    env_high, env_low, g_high, g_low, at_centre, at_partner,
):
    count = count_ref[0]
    src = src_ref[...]
    dst = dst_ref[...]
    near = jnp.concatenate([recv_ref[k, 0:4, PAIR : PAIR + GHOST] for k in range(NBR)], axis=1)
    ghosts = atom_table(near[0:3], near[3:4]).astype(BF16)
    table = table_ref[...]
    segments = jnp.concatenate([table, ghosts[:, 0:ATOM], ghosts[:, ATOM:SLOTS]], axis=0)
    found = dot(segments, one_hot(dst & 255, ATOM))
    part = dst >> 8
    picked = jnp.where(part == 0, found[0:16], jnp.where(part == 1, found[16:32], found[32:48]))
    edges[:, 0:PAIR] = jnp.concatenate(
        [joined(picked), picked[9:10], src.astype(F32), dst.astype(F32), jnp.zeros((2, PAIR), F32)],
        axis=0,
    )
    lane = lax.broadcasted_iota(I32, (8, 128), 1)
    row = lax.broadcasted_iota(I32, (8, 128), 0)

    def place(ref, size, begin, at, extra, tile):
        base = tile * 128 - at + begin
        first = base >> 7
        turn = base & 127
        low = jnp.clip(first, 0, 8)
        high = jnp.clip(first + 1, 0, 8)
        left = ref[:, pl.ds(pl.multiple_of(low * 128, 128), 128)]
        right = ref[:, pl.ds(pl.multiple_of(high * 128, 128), 128)]
        back = lax.rem(128 - turn, 128)
        taken = jnp.where(
            lane < 128 - turn, pltpu.roll(left, back, 1), pltpu.roll(right, back, 1)
        )
        here = pl.ds(pl.multiple_of(tile * 128, 128), 128)
        spot = tile * 128 + lane
        inside = (spot >= at) & (spot < at + size)
        edges[:, here] = jnp.where(inside, taken + extra, edges[:, here])

    def scalar(ref, which):
        return ref[which : which + 1, PAIR : PAIR + 128][0, 0].astype(I32)

    at = count
    jobs = []
    size = scalar(own_ref, 4)
    jobs.append((own_ref, size, 0, at, jnp.zeros((8, 128), F32), 4))
    at = at + size
    for k in range(NBR):
        ref = recv_ref.at[k]
        size = scalar(ref, 4)
        extra = jnp.where(row == 4, F32(ATOM + GHOST * k), 0.0)
        extra = jnp.where(row == 5, F32(ATOM * (3 + k)), extra)
        jobs.append((ref, size, scalar(ref, 5), at, extra, 2))
        at = at + size
    total = at
    for ref, size, begin, at, extra, usual in jobs:
        for step in range(usual):
            place(ref, size, begin, at, extra, (at >> 7) + step)
    for ref, size, begin, at, extra, usual in jobs:
        last = (at + size + 127) >> 7

        def more(tile, carry, ref=ref, size=size, begin=begin, at=at, extra=extra):
            place(ref, size, begin, at, extra, tile)
            return carry

        lax.fori_loop((at >> 7) + usual, last, more, 0)
    blocks = lax.div(total + EB - 1, EB)

    env[...] = jnp.zeros_like(env)
    g_env[...] = jnp.zeros_like(g_env)
    at_centre[...] = jnp.zeros_like(at_centre)
    at_partner[...] = jnp.zeros_like(at_partner)
    root3, root5, root15 = 3.0**0.5, 5.0**0.5, 15.0**0.5
    sends = jnp.concatenate([send_ref[k : k + 1, :] for k in range(NBR)], axis=1).astype(F32)
    own_index = lax.broadcasted_iota(I32, (1, ATOM), 1).astype(F32)
    codes = jnp.concatenate(
        [own_index, sends[:, 0:ATOM], sends[:, ATOM:SLOTS], jnp.zeros((13, ATOM), F32)], axis=0
    ).astype(BF16)

    def first_pass(block, carry):
        begin = pl.multiple_of(block * EB, EB)
        here = pl.ds(begin, EB)
        valid = begin + lax.broadcasted_iota(I32, (1, EB), 1) < total
        part = jnp.where(valid, edges[:, here], 0.0)
        code = part[4:5].astype(I32)
        seek = dot(codes, one_hot(code & 255, ATOM))
        kind = code >> 8
        centre = jnp.where(kind == 0, seek[0:1], jnp.where(kind == 1, seek[1:2], seek[2:3]))
        hot = one_hot(centre.astype(I32), ATOM)
        hots[:, here] = hot
        held = dot(table, hot)
        delta = part[0:3] - joined(held)
        length2 = delta[0:1] * delta[0:1] + delta[1:2] * delta[1:2] + delta[2:3] * delta[2:3] + 1.0
        soft = jnp.sqrt(length2)
        rinv = 1.0 / soft
        unit = delta * rinv
        ux, uy, uz = unit[0:1], unit[1:2], unit[2:3]
        turn = soft * (PI / CUTOFF) - PI / 2
        t2 = turn * turn
        cosine = -turn * (
            1 + t2 * (-1 / 6 + t2 * (1 / 120 + t2 * (-1 / 5040 + t2 * (1 / 362880 - t2 / 39916800))))
        )
        sine = 1 + t2 * (
            -1 / 2 + t2 * (1 / 24 + t2 * (-1 / 720 + t2 * (1 / 40320 + t2 * (-1 / 3628800 + t2 / 479001600))))
        )
        twice = 2 * cosine
        s_old, s_now = jnp.zeros_like(sine), sine
        c_old, c_now = jnp.ones_like(sine), cosine
        for b in range(BASIS):
            geo[RAD + b : RAD + b + 1, here] = s_now * rinv
            geo[DRAD + b : DRAD + b + 1, here] = (c_now * ((b + 1) * PI / CUTOFF) - s_now * rinv) * rinv
            s_old, s_now = s_now, twice * s_now - s_old
            c_old, c_now = c_now, twice * c_now - c_old
        angular = [
            jnp.ones_like(ux),
            root3 * ux,
            root3 * uy,
            root3 * uz,
            root15 * ux * uy,
            root15 * uy * uz,
            0.5 * root5 * (2.0 * uz * uz - ux * ux - uy * uy),
            root15 * ux * uz,
            0.5 * root15 * (ux * ux - uy * uy),
        ]
        for m in range(9):
            geo[ANG + m : ANG + m + 1, here] = angular[m]
        inner = 1.0 - length2 * (1.0 / (CUTOFF * CUTOFF))
        alive = jnp.where(valid, 1.0, 0.0)
        envelope = alive * inner * inner
        geo[ENVL : ENVL + 1, here] = envelope
        geo[DENVL : DENVL + 1, here] = alive * inner * soft * (-4.0 / (CUTOFF * CUTOFF))
        geo[RINV : RINV + 1, here] = rinv
        geo[DIR : DIR + 3, here] = unit
        radial = geo[RAD : RAD + 8, here]
        radial_low = radial - radial.astype(BF16).astype(F32)
        kinds = lax.broadcasted_iota(I32, (8, EB), 0)
        hot_c = jnp.where(kinds == held[9:10].astype(I32), 1.0, 0.0)
        hot_p = jnp.where(kinds == part[3:4].astype(I32), 1.0, 0.0)
        inputs = jnp.concatenate(
            [hot_c, hot_p, radial, radial_low, hot_c, hot_p, radial, jnp.zeros((8, EB), F32)], axis=0
        ).astype(BF16)
        pre = dot(wx_ref[...], inputs)
        gate = 1.0 / (1.0 + jnp.exp(-pre))
        act = pre * gate
        slope[:, here] = gate + act * (1.0 - gate)
        act_high, act_low = halves(act)
        after = dot(up_ref[...], jnp.concatenate([act_high, act_low], axis=0)) + dot(
            upl_ref[...], act_high
        )
        paired[:, here] = after
        geo[ERAW : ERAW + 1, here] = jnp.sum(act * ab_ref[:, 0:1], axis=0, keepdims=True)
        weights = after[0:CH] * envelope
        for m in range(9):
            term = weights if m == 0 else weights * angular[m]
            high, low = halves(term)
            rows = slice(m * CH, (m + 1) * CH)
            env[rows, :] += dot_nt(high, hot) + dot_nt(low, hot)
        return carry

    lax.fori_loop(0, blocks, first_pass, 0)
    env_high[...], env_low[...] = halves(env[...] * ENV_SCALE)
    degrees = (0, 1, 1, 1, 2, 2, 2, 2, 2)

    def second_pass(block, carry):
        here = pl.ds(pl.multiple_of(block * EB, EB), EB)
        hot = hots[:, here]
        angular = [geo[ANG + m : ANG + m + 1, here] for m in range(9)]
        envelope = geo[ENVL : ENVL + 1, here]
        around = []
        sums = [None, None, None]
        for m in range(9):
            rows = slice(m * CH, (m + 1) * CH)
            got = dot(env_high[rows, :], hot) + dot(env_low[rows, :], hot)
            around.append(got)
            term = got if m == 0 else got * angular[m]
            degree = degrees[m]
            sums[degree] = term if sums[degree] is None else sums[degree] + term
        value = paired[CH : 2 * CH, here]
        invariant = jnp.concatenate([s * value for s in sums], axis=0)
        high, low = halves(invariant)
        mt = mt_ref[...]
        pre = paired[2 * CH :, here] + dot(mt, high) + dot(mt, low) + dot(mtl_ref[...], high)
        gate = 1.0 / (1.0 + jnp.exp(-pre))
        act = pre * gate
        back = ab_ref[:, 1:2]
        geo[ERAW : ERAW + 1, here] += jnp.sum(act * back, axis=0, keepdims=True)
        d_pre = (gate + act * (1.0 - gate)) * back * envelope
        d_high, d_low = halves(d_pre)
        mixed[:, here] = d_high
        mixed_low[:, here] = d_low
        mb = mb_ref[...]
        d_inv = dot(mb, d_high) + dot(mb, d_low) + dot(mbl_ref[...], d_high)
        d_inv = [d_inv[i * CH : (i + 1) * CH] for i in range(3)]
        d_value[:, here] = d_inv[0] * sums[0] + d_inv[1] * sums[1] + d_inv[2] * sums[2]
        d_sum = [d * value for d in d_inv]
        for m in range(9):
            share = d_sum[degrees[m]]
            term = share if m == 0 else share * angular[m]
            high, low = halves(term)
            rows = slice(m * CH, (m + 1) * CH)
            g_env[rows, :] += dot_nt(high, hot) + dot_nt(low, hot)
            if m:
                geo[DANG + m - 1 : DANG + m, here] = jnp.sum(share * around[m], axis=0, keepdims=True)
        return carry

    lax.fori_loop(0, blocks, second_pass, 0)
    g_high[...], g_low[...] = halves(g_env[...] * ENV_SCALE)

    def third_pass(block, carry):
        here = pl.ds(pl.multiple_of(block * EB, EB), EB)
        hot = hots[:, here]
        angular = [geo[ANG + m : ANG + m + 1, here] for m in range(9)]
        envelope = geo[ENVL : ENVL + 1, here]
        raw = paired[0:CH, here]
        weights = raw * envelope
        d_weight = None
        d_ang = [None]
        for m in range(9):
            rows = slice(m * CH, (m + 1) * CH)
            got = dot(g_high[rows, :], hot) + dot(g_low[rows, :], hot)
            term = got if m == 0 else got * angular[m]
            d_weight = term if m == 0 else d_weight + term
            if m:
                d_ang.append(
                    geo[DANG + m - 1 : DANG + m, here] + jnp.sum(weights * got, axis=0, keepdims=True)
                )
        e_raw = geo[ERAW : ERAW + 1, here]
        d_envelope = e_raw + jnp.sum(d_weight * raw, axis=0, keepdims=True)
        pair_high, pair_low = halves(
            jnp.concatenate([d_weight * envelope, d_value[:, here]], axis=0)
        )
        both_high = jnp.concatenate([pair_high, mixed[:, here]], axis=0)
        both_low = jnp.concatenate([pair_low, mixed_low[:, here]], axis=0)
        dn = dn_ref[...]
        d_act = dot(dn, both_high) + dot(dn, both_low) + dot(dnl_ref[...], both_high)
        d_act = d_act + ab_ref[:, 0:1] * envelope
        d_pre_high, d_pre_low = halves(d_act * slope[:, here])
        d_radial = dot(wr_ref[...], jnp.concatenate([d_pre_high, d_pre_low], axis=0)) + dot(
            wrl_ref[...], d_pre_high
        )
        d_soft = jnp.sum(d_radial[0:8] * geo[DRAD : DRAD + 8, here], axis=0, keepdims=True)
        d_soft = d_soft + d_envelope * geo[DENVL : DENVL + 1, here]
        unit = geo[DIR : DIR + 3, here]
        rinv = geo[RINV : RINV + 1, here]
        ux, uy, uz = unit[0:1], unit[1:2], unit[2:3]
        d_ux = root3 * d_ang[1] + root15 * (uy * d_ang[4] + uz * d_ang[7] + ux * d_ang[8]) - root5 * ux * d_ang[6]
        d_uy = root3 * d_ang[2] + root15 * (ux * d_ang[4] + uz * d_ang[5] - uy * d_ang[8]) - root5 * uy * d_ang[6]
        d_uz = root3 * d_ang[3] + root15 * (uy * d_ang[5] + ux * d_ang[7]) + 2.0 * root5 * uz * d_ang[6]
        along = d_soft - (d_ux * ux + d_uy * uy + d_uz * uz) * rinv
        pull = [d * rinv + u * along for d, u in ((d_ux, ux), (d_uy, uy), (d_uz, uz))]
        energy = e_raw * envelope
        sent = jnp.concatenate([*pull, energy, jnp.zeros((4, EB), F32)], axis=0)
        sent = jnp.concatenate([sent, sent - sent.astype(BF16).astype(F32)], axis=0).astype(BF16)
        at_centre[...] += dot_nt(sent, hot)
        code = jnp.where(
            begin_valid(block, total), edges[5:6, here], 0.0
        ).astype(I32)
        seg = lax.broadcasted_iota(I32, (16, EB), 0) == (code >> 8)
        spread = jnp.concatenate([jnp.where(seg, g, 0.0) for g in pull], axis=0)
        high, low = halves(spread)
        hot_partner = one_hot(code & 255, ATOM)
        at_partner[...] += dot_nt(high, hot_partner) + dot_nt(low, hot_partner)
        return carry

    lax.fori_loop(0, blocks, third_pass, 0)
    sums = at_centre[...]
    sums = sums[0:8] + sums[8:16]
    parts = at_partner[...]
    mine = [parts[16 * i : 16 * i + 1] for i in range(3)]
    force_ref[...] = sums[0:3] - jnp.concatenate(mine, axis=0)
    energy_ref[...] = sums[3:4]
    msg_ref[...] = jnp.zeros_like(msg_ref)
    for k in range(NBR):
        for i in range(3):
            msg_ref[k, i : i + 1, :] = parts[16 * i + 3 + k : 16 * i + 4 + k]
            ghost = parts[16 * i + 1 + k // 4 : 16 * i + 2 + k // 4]
            msg_ref[k, 3 + i : 4 + i, 0:GHOST] = ghost[:, (k % 4) * GHOST : (k % 4 + 1) * GHOST]


def begin_valid(block, total):
    return block * EB + lax.broadcasted_iota(I32, (1, EB), 1) < total


def return_kernel(msg_ref, force_ref, send_ref, out_ref, inbox, send_sem, recv_sem):
    barrier, peers = greet()
    sends = jnp.concatenate([send_ref[k : k + 1, :] for k in range(NBR)], axis=1)
    hot = one_hot(sends, ATOM)
    pl.semaphore_wait(barrier, NBR)
    copies = swap(peers, msg_ref, inbox, send_sem, recv_sem)
    for copy in copies:
        copy.wait()
    total = force_ref[...]
    for k in range(NBR):
        total = total - inbox[k, 0:3, :]
    ghosts = jnp.concatenate([inbox[k, 3:6, 0:GHOST] for k in range(NBR)], axis=1)
    split = jnp.concatenate([*thirds(ghosts), jnp.zeros((7, SLOTS), F32)], axis=0).astype(BF16)
    back = dot_nt(split, hot)
    out_ref[...] = total - joined(back)


def per_device(
    positions, species, send_list, edge_src, edge_dst, edge_count,
    w_in, w_mid, w_pair, w_mix, w_back, w_read,
):
    sends = send_list[0]
    shape = jax.ShapeDtypeStruct
    shared = pl.pallas_call(
        share_kernel,
        out_shape=(
            shape((8, LIST), F32),
            shape((16, ATOM), BF16),
            shape((NBR, 8, LIST), F32),
            shape((WIDTH, 64), BF16),
            shape((2 * WIDTH, 2 * WIDTH), BF16),
            shape((2 * WIDTH, WIDTH), BF16),
            shape((WIDTH, 2 * WIDTH), BF16),
            shape((WIDTH, 2 * WIDTH), BF16),
            shape((WIDTH, 3 * CH), BF16),
            shape((WIDTH, 3 * CH), BF16),
            shape((3 * CH, WIDTH), BF16),
            shape((3 * CH, WIDTH), BF16),
            shape((16, 2 * WIDTH), BF16),
            shape((16, WIDTH), BF16),
            shape((WIDTH, 2), F32),
        ),
        in_specs=[SMEM] + [VMEM] * 11,
        out_specs=[VMEM, VMEM, VMEM] + [VMEM] * 12,
        scratch_shapes=[
            pltpu.VMEM((NBR, 8, LIST), F32),
            pltpu.VMEM((16, PAIR), F32),
            pltpu.SemaphoreType.DMA((NBR,)),
            pltpu.SemaphoreType.DMA((NBR,)),
        ],
        compiler_params=pltpu.CompilerParams(
            collective_id=0, has_side_effects=True, vmem_limit_bytes=48 << 20
        ),
    )(
        edge_count, positions, species.reshape(1, ATOM), sends, edge_src, edge_dst,
        w_in, w_mid, w_pair, w_mix, w_back, w_read.reshape(1, WIDTH),
    )
    messages, force, energy = pl.pallas_call(
        edge_kernel,
        out_shape=(
            shape((NBR, 8, ATOM), F32),
            shape((3, ATOM), F32),
            shape((1, ATOM), F32),
        ),
        in_specs=[SMEM] + [VMEM] * 18,
        out_specs=[VMEM] * 3,
        scratch_shapes=[
            pltpu.VMEM((8, CAP + 512), F32),
            pltpu.VMEM((ATOM, CAP), BF16),
            pltpu.VMEM((2 * WIDTH, CAP), F32),
            pltpu.VMEM((WIDTH, CAP), F32),
            pltpu.VMEM((WIDTH, CAP), BF16),
            pltpu.VMEM((WIDTH, CAP), BF16),
            pltpu.VMEM((CH, CAP), F32),
            pltpu.VMEM((ROWS, CAP), F32),
            pltpu.VMEM((9 * CH, ATOM), F32),
            pltpu.VMEM((9 * CH, ATOM), F32),
            pltpu.VMEM((9 * CH, ATOM), BF16),
            pltpu.VMEM((9 * CH, ATOM), BF16),
            pltpu.VMEM((9 * CH, ATOM), BF16),
            pltpu.VMEM((9 * CH, ATOM), BF16),
            pltpu.VMEM((16, ATOM), F32),
            pltpu.VMEM((48, ATOM), F32),
        ],
        compiler_params=pltpu.CompilerParams(vmem_limit_bytes=56 << 20),
    )(edge_count, edge_src, edge_dst, sends, *shared)
    forces = pl.pallas_call(
        return_kernel,
        out_shape=shape((3, ATOM), F32),
        in_specs=[VMEM] * 3,
        out_specs=VMEM,
        scratch_shapes=[
            pltpu.VMEM((NBR, 8, ATOM), F32),
            pltpu.SemaphoreType.DMA((NBR,)),
            pltpu.SemaphoreType.DMA((NBR,)),
        ],
        compiler_params=pltpu.CompilerParams(
            collective_id=1, has_side_effects=True, vmem_limit_bytes=16 << 20
        ),
    )(messages, force, sends)
    return forces, energy.reshape(ATOM)


def solution(mesh):
    both = ("dom", "face")
    placed = (
        P(None, both), P(both), P(both, None, None), P(both, None), P(both, None), P(both),
        P(), P(), P(), P(), P(), P(),
    )
    return jax.shard_map(
        per_device,
        mesh=mesh,
        in_specs=placed,
        out_specs=(P(None, both), P(both)),
        check_vma=False,
    )
```

time: 459 us -> 73.1 us (0.16); the launches traced: 450 us -> 72.6 us
  waiting for transfers between devices: 138 us -> 0 us
  other arithmetic: 113 us -> 0 us
  local copies, waits for them, and re-layouts: 115 us -> 18.4 us
  starting transfers between devices: 56.7 us -> 0 us
  Pallas kernels: 0 us -> 52.8 us
  matrix products: 24.3 us -> 0 us
    ppermute x24 -> x0, waiting for transfers between devices: 138 us -> none  [the longest x12 76.8 us: padded_2(): lax.ppermute(head, axis, [((i + 1) % count, i) for i in range(count)])]
    scatter-add x8 -> x0, other arithmetic: 80.2 us -> none  [the longest x1 14.9 us: atom_energy(): env_in[centre]]
    gather x13 -> x0, local copies, waits for them, and re-layouts: 66.9 us -> none  [the longest x2 15.1 us: partial_env(): jax.ops.segment_sum(env_terms(paired_in, angular_in, envelope_in), centre...]
    ppermute x24 -> x0, starting transfers between devices: 56.7 us -> none  [the longest x12 30 us: padded_2(): lax.ppermute(tail, axis, [(i, (i + 1) % count) for i in range(count)])]
    pallas_call x0 -> x3, Pallas kernels: none -> 52.8 us  [the longest x1 31 us: per_device(): pl.pallas_call(edge_kernel, out_shape=(shape((NBR, 8, ATOM), F32), shape(...]
    dot_general x11 -> x0, matrix products: 24.3 us -> none  [product_of(): jnp.dot(left, right, precision=lax.Precision.HIGHEST, preferred_element_t...]
    slice x38 -> x0, local copies, waits for them, and re-layouts: 11.7 us -> none  [the longest x1 7.95 us: edge_energy(): env_rows[:, order * CHANNELS:(order + 1) * CHANNELS]]
    concatenate x26 -> x0, other arithmetic: 7.53 us -> none  [the longest x6 4.37 us: padded_2(): jnp.concatenate([lax.ppermute(tail, axis, [(i, (i + 1) % count) for i in...]
  transfers between devices with their start and end apart: 24 -> 0, of which waited for: 20 -> 0; matrix products, arithmetic and copies ran while one was open for 4% -> 0% of each run, Pallas kernels for 0% -> 0%
where the time goes in v1:
time: 73.1 us; the launch traced here: 72.6 us
  Pallas kernels  52.8 us (72%)
  local copies, waits for them, and re-layouts  18.4 us (25%)
  between operations  1.38 us (2%)
    pallas_call x1, Pallas kernels, per_device(): pl.pallas_call(edge_kernel, out_shape=(shape((NBR, 8, ATOM), F32), shape(...  31 us
    unnamed x59, local copies, waits for them, and re-layouts  18.4 us
    pallas_call x1, Pallas kernels, per_device(): pl.pallas_call(share_kernel, out_shape=(shape((8, LIST), F32), shape((16,...  15 us
    pallas_call x1, Pallas kernels, per_device(): pl.pallas_call(return_kernel, out_shape=shape((3, ATOM), F32), in_specs=[...  6.74 us

profile of v1, /device:TPU:1, one launch (start us, length us, event | category | flops | bytes accessed | tf_op | source)
XLA Modules:
  0.0 72.6 jit_solution(17659822651267966364)
XLA Ops:
  1.3 0.7 copy-done.27
  2.0 0.9 %copy-done.1 = f32[320,128]{1,0:T(8,128)S(1)} copy-done((f32[320,128]{1,0:T(8,128)S(1)}, f32[320,128]{1,0:T(8,128)}, u32[]{:S(2)}) %copy-start.1) | copy-done | bytes 163864
  2.9 0.8 %copy-done.10 = f32[128,128]{1,0:T(8,128)S(1)} copy-done((f32[128,128]{1,0:T(8,128)S(1)}, f32[128,128]{1,0:T(8,128)}, u32[]{:S(2)}) %copy-start.10) | copy-done | bytes 65560
  3.7 0.8 %copy-done.11 = f32[128,128]{1,0:T(8,128)S(1)} copy-done((f32[128,128]{1,0:T(8,128)S(1)}, f32[128,128]{1,0:T(8,128)}, u32[]{:S(2)}) %copy-start.11) | copy-done | bytes 65560
  4.6 0.8 %copy-done.12 = f32[128,128]{1,0:T(8,128)S(1)} copy-done((f32[128,128]{1,0:T(8,128)S(1)}, f32[128,128]{1,0:T(8,128)}, u32[]{:S(2)}) %copy-start.12) | copy-done | bytes 65560
  5.4 0.7 copy-done.19
  6.1 0.7 copy-done.20
  6.8 0.7 copy-done.21
  7.5 0.7 copy-done.24
  8.2 15.0 %shard_map.131 = (f32[8,1152]{1,0:T(8,128)S(1)}, bf16[16,256]{1,0:T(8,128)(2,1)S(1)}, f32[8,8,1152]{2,1,0:T(8,128)S(1)}, bf16[128,64]{1,0:T(8,128)(2,1)S(1)}, bf...) custom-call(s32[1]{0:T(128)S(6)} %copy.15.count_ref, ...), custom_call_target="tpu_custom_call" | custom-call | tf_op jit(solution)/shard_map/pallas_call | solution.py:520
  23.2 0.7 copy-done
  23.9 0.7 copy-done.2
  24.6 0.6 copy-done.3
  25.2 0.6 copy-done.4
  25.8 0.6 copy-done.5
  26.5 0.6 copy-done.6
  27.1 0.6 copy-done.7
  27.7 0.6 copy-done.8
  29.0 0.6 copy-done.14
  32.0 31.0 %shard_map.132 = (f32[8,8,256]{2,1,0:T(8,128)}, f32[3,256]{1,0:T(4,128)}, f32[1,256]{1,0:T(1,128)}) custom-call(s32[1]{0:T(128)S(6)} %copy.15.count_ref, s32[1,1024]{1,0:T(1,128)} %src_ref.3, s32[1,1024]{1,0:T(1,128)} %dst_ref.3, s32[8,64]{1,0:T(8,128)} %bitcast.4, f32[8,1152]{1,0:T(8,128)} %copy-done.17, bf16[16,256]{1,0:T(8,128)(2,1)} %copy-done.22, ...), custom_call_target="tpu_custom_call" | custom-call | tf_op jit(solution)/shard_map/pallas_call | solution.py:554
  63.0 0.7 copy-done.16
  63.7 0.8 %copy-done.9 = f32[8,8,256]{2,1,0:T(8,128)S(1)} copy-done((f32[8,8,256]{2,1,0:T(8,128)S(1)}, f32[8,8,256]{2,1,0:T(8,128)}, u32[]{:S(2)}) %copy-start.9) | copy-done | bytes 65560
  64.5 0.7 copy-done.26
  65.2 6.7 %shard_map.133 = f32[3,256]{1,0:T(4,128)S(1)} custom-call(f32[8,8,256]{2,1,0:T(8,128)S(1)} %copy-done.9, f32[3,256]{1,0:T(4,128)S(1)} %copy-done.26, s32[8,64]{1,0:T(8,128)S(1)} %bitcast.6), custom_call_target="tpu_custom_call" | custom-call | tf_op jit(solution)/shard_map/pallas_call | solution.py:583
  (38 shorter events, 3.7 us)
Async XLA Ops:
  0.6 0.7 copy-start.15
  1.3 0.7 copy-start.27
  1.3 0.7 copy-start.28
  2.0 0.9 %copy-start.1 = (f32[320,128]{1,0:T(8,128)S(1)}, f32[320,128]{1,0:T(8,128)}, u32[]{:S(2)}) copy-start(f32[320,128]{1,0:T(8,128)} %w_mix_ref.1) | copy-start | bytes 491524
  2.9 0.8 %copy-start.10 = (f32[128,128]{1,0:T(8,128)S(1)}, f32[128,128]{1,0:T(8,128)}, u32[]{:S(2)}) copy-start(f32[128,128]{1,0:T(8,128)} %w_mid_ref.1) | copy-start | bytes 196612
  3.7 0.8 %copy-start.11 = (f32[128,128]{1,0:T(8,128)S(1)}, f32[128,128]{1,0:T(8,128)}, u32[]{:S(2)}) copy-start(f32[128,128]{1,0:T(8,128)} %w_pair_ref.1) | copy-start | bytes 196612
  4.6 0.8 %copy-start.12 = (f32[128,128]{1,0:T(8,128)S(1)}, f32[128,128]{1,0:T(8,128)}, u32[]{:S(2)}) copy-start(f32[128,128]{1,0:T(8,128)} %w_back_ref.1) | copy-start | bytes 196612
  5.4 0.7 copy-start.19
  6.1 0.7 copy-start.20
  6.8 0.7 copy-start.21
  7.5 0.7 copy-start.24
  23.2 0.7 copy-start
  23.9 0.7 copy-start.2
  24.6 0.6 copy-start.3
  25.2 0.6 copy-start.4
  25.8 0.6 copy-start.5
  26.5 0.6 copy-start.6
  27.1 0.6 copy-start.7
  27.7 0.6 copy-start.8
  29.0 0.6 copy-start.14
  29.6 0.6 copy-start.17
  63.0 0.7 copy-start.16
  63.7 0.8 %copy-start.9 = (f32[8,8,256]{2,1,0:T(8,128)S(1)}, f32[8,8,256]{2,1,0:T(8,128)}, u32[]{:S(2)}) copy-start(f32[8,8,256]{2,1,0:T(8,128)} %get-tuple-element.35.msg_ref) | copy-start | bytes 196612
  64.5 0.7 copy-start.26
  (5 other events, 3.0 us)

commit v2 on v1

--- a/solution.py
+++ b/solution.py
@@ -22,14 +22,14 @@
 SLOTS = NBR * GHOST
 LIST = PAIR + 128
 CAP = 10 * PAIR
-EB = 512
+EB = 1024
 F32 = jnp.float32
 BF16 = jnp.bfloat16
 I32 = jnp.int32
 MESH = pl.DeviceIdType.MESH
 VMEM = pl.BlockSpec(memory_space=pltpu.VMEM)
 SMEM = pl.BlockSpec(memory_space=pltpu.SMEM)
-ANY = pl.BlockSpec(memory_space=pl.ANY)
+HBM = pl.BlockSpec(memory_space=pltpu.HBM)
 
 RAD, DRAD, ANG, ENVL, DENVL, RINV, DIR, ERAW, DANG, ROWS = 0, 8, 16, 25, 26, 27, 28, 31, 32, 40
 
@@ -106,13 +106,28 @@
 
 
 def share_kernel(
-    count_ref, pos_ref, spec_ref, send_ref, src_ref, dst_ref,
-    w_in_ref, w_mid_ref, w_pair_ref, w_mix_ref, w_back_ref, w_read_ref,
-    own_ref, table_ref, recv_ref, wx_ref, up_ref, upl_ref, dn_ref, dnl_ref,
-    mt_ref, mtl_ref, mb_ref, mbl_ref, wr_ref, wrl_ref, ab_ref,
-    out_buf, order_buf, send_sem, recv_sem,
+    count_ref, *refs,
 ):
+    sources, refs = refs[:11], refs[11:]
+    (
+        own_ref, table_ref, recv_ref, wx_ref, up_ref, upl_ref, dn_ref, dnl_ref,
+        mt_ref, mtl_ref, mb_ref, mbl_ref, wr_ref, wrl_ref, ab_ref,
+    ) = refs[:15]
+    held, refs = refs[15:26], refs[26:]
+    out_buf, order_buf, load_sem, send_sem, recv_sem = refs
+    (
+        pos_ref, spec_ref, send_ref, src_ref, dst_ref,
+        w_in_ref, w_mid_ref, w_pair_ref, w_mix_ref, w_back_ref, w_read_ref,
+    ) = held
+    loads = [
+        pltpu.make_async_copy(source, target, load_sem.at[i])
+        for i, (source, target) in enumerate(zip(sources, held))
+    ]
+    for load in loads:
+        load.start()
     barrier, peers = greet()
+    for load in loads[:5]:
+        load.wait()
     table = atom_table(pos_ref[...], spec_ref[...].astype(F32)).astype(BF16)
     table_ref[...] = table
     sends = jnp.concatenate([send_ref[k : k + 1, :] for k in range(NBR)], axis=1)
@@ -167,8 +182,14 @@
         out_buf[k, 5:6, PAIR:LIST] = jnp.broadcast_to(start[k + 1 : k + 2, :], (1, 128))
     pl.semaphore_wait(barrier, NBR)
     copies = swap(peers, out_buf, recv_ref, send_sem, recv_sem)
-    own_ref[:, 0:PAIR] = entries
-    own_ref[:, PAIR:LIST] = jnp.zeros((8, 128), F32)
+    own_ref[0:8, 0:PAIR] = entries
+    own_ref[:, PAIR:LIST] = jnp.zeros((16, 128), F32)
+    own_ref[8:9, 0:PAIR] = src.astype(F32)
+    own_ref[9:10, 0:PAIR] = dst.astype(F32)
+    own_ref[10:11, 0:SLOTS] = sends.astype(F32)
+    own_ref[11:12, PAIR:LIST] = jnp.full((1, 128), count_ref[0], I32).astype(F32)
+    for load in loads[5:]:
+        load.wait()
     own_ref[4:5, PAIR:LIST] = jnp.broadcast_to(total[0:1, :], (1, 128))
     w_in = w_in_ref[...]
     w_c = w_in[0:SPECIES].T
@@ -209,16 +230,16 @@
 
 
 def edge_kernel(
-    count_ref, src_ref, dst_ref, send_ref, own_ref, table_ref, recv_ref,
+    own_ref, table_ref, recv_ref,
     wx_ref, up_ref, upl_ref, dn_ref, dnl_ref, mt_ref, mtl_ref, mb_ref, mbl_ref,
     wr_ref, wrl_ref, ab_ref,
     msg_ref, force_ref, energy_ref,
     edges, hots, paired, slope, mixed, mixed_low, d_value, geo, env, g_env,
-    env_high, env_low, g_high, g_low, at_centre, at_partner,
+    fields, terms, around, at_centre, at_partner,
 ):
-    count = count_ref[0]
-    src = src_ref[...]
-    dst = dst_ref[...]
+    count = own_ref[11:12, PAIR : PAIR + 128][0, 0].astype(I32)
+    src = own_ref[8:9, 0:PAIR]
+    dst = own_ref[9:10, 0:PAIR].astype(I32)
     near = jnp.concatenate([recv_ref[k, 0:4, PAIR : PAIR + GHOST] for k in range(NBR)], axis=1)
     ghosts = atom_table(near[0:3], near[3:4]).astype(BF16)
     table = table_ref[...]
@@ -227,7 +248,7 @@
     part = dst >> 8
     picked = jnp.where(part == 0, found[0:16], jnp.where(part == 1, found[16:32], found[32:48]))
     edges[:, 0:PAIR] = jnp.concatenate(
-        [joined(picked), picked[9:10], src.astype(F32), dst.astype(F32), jnp.zeros((2, PAIR), F32)],
+        [joined(picked), picked[9:10], src, dst.astype(F32), jnp.zeros((2, PAIR), F32)],
         axis=0,
     )
     lane = lax.broadcasted_iota(I32, (8, 128), 1)
@@ -239,8 +260,8 @@
         turn = base & 127
         low = jnp.clip(first, 0, 8)
         high = jnp.clip(first + 1, 0, 8)
-        left = ref[:, pl.ds(pl.multiple_of(low * 128, 128), 128)]
-        right = ref[:, pl.ds(pl.multiple_of(high * 128, 128), 128)]
+        left = ref[0:8, pl.ds(pl.multiple_of(low * 128, 128), 128)]
+        right = ref[0:8, pl.ds(pl.multiple_of(high * 128, 128), 128)]
         back = lax.rem(128 - turn, 128)
         taken = jnp.where(
             lane < 128 - turn, pltpu.roll(left, back, 1), pltpu.roll(right, back, 1)
@@ -284,7 +305,7 @@
     at_centre[...] = jnp.zeros_like(at_centre)
     at_partner[...] = jnp.zeros_like(at_partner)
     root3, root5, root15 = 3.0**0.5, 5.0**0.5, 15.0**0.5
-    sends = jnp.concatenate([send_ref[k : k + 1, :] for k in range(NBR)], axis=1).astype(F32)
+    sends = own_ref[10:11, 0:SLOTS]
     own_index = lax.broadcasted_iota(I32, (1, ATOM), 1).astype(F32)
     codes = jnp.concatenate(
         [own_index, sends[:, 0:ATOM], sends[:, ATOM:SLOTS], jnp.zeros((13, ATOM), F32)], axis=0
@@ -365,13 +386,13 @@
         weights = after[0:CH] * envelope
         for m in range(9):
             term = weights if m == 0 else weights * angular[m]
-            high, low = halves(term)
             rows = slice(m * CH, (m + 1) * CH)
-            env[rows, :] += dot_nt(high, hot) + dot_nt(low, hot)
+            terms[rows, 0:EB], terms[rows, EB:] = halves(term)
+        env[...] += dot_nt(terms[...], jnp.concatenate([hot, hot], axis=1))
         return carry
 
     lax.fori_loop(0, blocks, first_pass, 0)
-    env_high[...], env_low[...] = halves(env[...] * ENV_SCALE)
+    fields[:, 0:ATOM], fields[:, ATOM:] = halves(env[...] * ENV_SCALE)
     degrees = (0, 1, 1, 1, 2, 2, 2, 2, 2)
 
     def second_pass(block, carry):
@@ -379,12 +400,10 @@
         hot = hots[:, here]
         angular = [geo[ANG + m : ANG + m + 1, here] for m in range(9)]
         envelope = geo[ENVL : ENVL + 1, here]
-        around = []
+        around[...] = dot(fields[...], jnp.concatenate([hot, hot], axis=0))
         sums = [None, None, None]
         for m in range(9):
-            rows = slice(m * CH, (m + 1) * CH)
-            got = dot(env_high[rows, :], hot) + dot(env_low[rows, :], hot)
-            around.append(got)
+            got = around[m * CH : (m + 1) * CH, :]
             term = got if m == 0 else got * angular[m]
             degree = degrees[m]
             sums[degree] = term if sums[degree] is None else sums[degree] + term
@@ -409,15 +428,15 @@
         for m in range(9):
             share = d_sum[degrees[m]]
             term = share if m == 0 else share * angular[m]
-            high, low = halves(term)
             rows = slice(m * CH, (m + 1) * CH)
-            g_env[rows, :] += dot_nt(high, hot) + dot_nt(low, hot)
+            terms[rows, 0:EB], terms[rows, EB:] = halves(term)
             if m:
-                geo[DANG + m - 1 : DANG + m, here] = jnp.sum(share * around[m], axis=0, keepdims=True)
+                geo[DANG + m - 1 : DANG + m, here] = jnp.sum(share * around[rows, :], axis=0, keepdims=True)
+        g_env[...] += dot_nt(terms[...], jnp.concatenate([hot, hot], axis=1))
         return carry
 
     lax.fori_loop(0, blocks, second_pass, 0)
-    g_high[...], g_low[...] = halves(g_env[...] * ENV_SCALE)
+    fields[:, 0:ATOM], fields[:, ATOM:] = halves(g_env[...] * ENV_SCALE)
 
     def third_pass(block, carry):
         here = pl.ds(pl.multiple_of(block * EB, EB), EB)
@@ -428,9 +447,9 @@
         weights = raw * envelope
         d_weight = None
         d_ang = [None]
+        around[...] = dot(fields[...], jnp.concatenate([hot, hot], axis=0))
         for m in range(9):
-            rows = slice(m * CH, (m + 1) * CH)
-            got = dot(g_high[rows, :], hot) + dot(g_low[rows, :], hot)
+            got = around[m * CH : (m + 1) * CH, :]
             term = got if m == 0 else got * angular[m]
             d_weight = term if m == 0 else d_weight + term
             if m:
@@ -494,9 +513,9 @@
     return block * EB + lax.broadcasted_iota(I32, (1, EB), 1) < total
 
 
-def return_kernel(msg_ref, force_ref, send_ref, out_ref, inbox, send_sem, recv_sem):
+def return_kernel(msg_ref, force_ref, own_ref, out_ref, inbox, send_sem, recv_sem):
     barrier, peers = greet()
-    sends = jnp.concatenate([send_ref[k : k + 1, :] for k in range(NBR)], axis=1)
+    sends = own_ref[10:11, 0:SLOTS].astype(I32)
     hot = one_hot(sends, ATOM)
     pl.semaphore_wait(barrier, NBR)
     copies = swap(peers, msg_ref, inbox, send_sem, recv_sem)
@@ -511,6 +530,38 @@
     out_ref[...] = total - joined(back)
 
 
+def edge_call(*operands):
+    shape = jax.ShapeDtypeStruct
+    return pl.pallas_call(
+        edge_kernel,
+        out_shape=(
+            shape((NBR, 8, ATOM), F32),
+            shape((3, ATOM), F32),
+            shape((1, ATOM), F32),
+        ),
+        in_specs=[VMEM] * 15,
+        out_specs=[VMEM] * 3,
+        scratch_shapes=[
+            pltpu.VMEM((8, CAP + 512), F32),
+            pltpu.VMEM((ATOM, CAP), BF16),
+            pltpu.VMEM((2 * WIDTH, CAP), F32),
+            pltpu.VMEM((WIDTH, CAP), F32),
+            pltpu.VMEM((WIDTH, CAP), BF16),
+            pltpu.VMEM((WIDTH, CAP), BF16),
+            pltpu.VMEM((CH, CAP), F32),
+            pltpu.VMEM((ROWS, CAP), F32),
+            pltpu.VMEM((9 * CH, ATOM), F32),
+            pltpu.VMEM((9 * CH, ATOM), F32),
+            pltpu.VMEM((9 * CH, 2 * ATOM), BF16),
+            pltpu.VMEM((9 * CH, 2 * EB), BF16),
+            pltpu.VMEM((9 * CH, EB), F32),
+            pltpu.VMEM((16, ATOM), F32),
+            pltpu.VMEM((48, ATOM), F32),
+        ],
+        compiler_params=pltpu.CompilerParams(vmem_limit_bytes=48 << 20),
+    )(*operands)
+
+
 def per_device(
     positions, species, send_list, edge_src, edge_dst, edge_count,
     w_in, w_mid, w_pair, w_mix, w_back, w_read,
@@ -520,7 +571,7 @@
     shared = pl.pallas_call(
         share_kernel,
         out_shape=(
-            shape((8, LIST), F32),
+            shape((16, LIST), F32),
             shape((16, ATOM), BF16),
             shape((NBR, 8, LIST), F32),
             shape((WIDTH, 64), BF16),
@@ -536,50 +587,40 @@
             shape((16, WIDTH), BF16),
             shape((WIDTH, 2), F32),
         ),
-        in_specs=[SMEM] + [VMEM] * 11,
-        out_specs=[VMEM, VMEM, VMEM] + [VMEM] * 12,
+        in_specs=[SMEM] + [HBM] * 11,
+        out_specs=[VMEM] * 15,
         scratch_shapes=[
+            pltpu.VMEM((3, ATOM), F32),
+            pltpu.VMEM((1, ATOM), I32),
+            pltpu.VMEM((NBR, GHOST), I32),
+            pltpu.VMEM((1, PAIR), I32),
+            pltpu.VMEM((1, PAIR), I32),
+            pltpu.VMEM((2 * SPECIES + BASIS, WIDTH), F32),
+            pltpu.VMEM((WIDTH, WIDTH), F32),
+            pltpu.VMEM((WIDTH, WIDTH), F32),
+            pltpu.VMEM((WIDTH + 3 * CH, WIDTH), F32),
+            pltpu.VMEM((WIDTH, WIDTH), F32),
+            pltpu.VMEM((1, WIDTH), F32),
             pltpu.VMEM((NBR, 8, LIST), F32),
             pltpu.VMEM((16, PAIR), F32),
+            pltpu.SemaphoreType.DMA((11,)),
             pltpu.SemaphoreType.DMA((NBR,)),
             pltpu.SemaphoreType.DMA((NBR,)),
         ],
         compiler_params=pltpu.CompilerParams(
-            collective_id=0, has_side_effects=True, vmem_limit_bytes=48 << 20
+            collective_id=0, has_side_effects=True, vmem_limit_bytes=8 << 20
         ),
     )(
-        edge_count, positions, species.reshape(1, ATOM), sends, edge_src, edge_dst,
-        w_in, w_mid, w_pair, w_mix, w_back, w_read.reshape(1, WIDTH),
+        edge_count,
+        *(
+            pltpu.with_memory_space_constraint(x, pltpu.HBM)
+            for x in (
+                positions, species.reshape(1, ATOM), sends, edge_src, edge_dst,
+                w_in, w_mid, w_pair, w_mix, w_back, w_read.reshape(1, WIDTH),
+            )
+        ),
     )
-    messages, force, energy = pl.pallas_call(
-        edge_kernel,
-        out_shape=(
-            shape((NBR, 8, ATOM), F32),
-            shape((3, ATOM), F32),
-            shape((1, ATOM), F32),
-        ),
-        in_specs=[SMEM] + [VMEM] * 18,
-        out_specs=[VMEM] * 3,
-        scratch_shapes=[
-            pltpu.VMEM((8, CAP + 512), F32),
-            pltpu.VMEM((ATOM, CAP), BF16),
-            pltpu.VMEM((2 * WIDTH, CAP), F32),
-            pltpu.VMEM((WIDTH, CAP), F32),
-            pltpu.VMEM((WIDTH, CAP), BF16),
-            pltpu.VMEM((WIDTH, CAP), BF16),
-            pltpu.VMEM((CH, CAP), F32),
-            pltpu.VMEM((ROWS, CAP), F32),
-            pltpu.VMEM((9 * CH, ATOM), F32),
-            pltpu.VMEM((9 * CH, ATOM), F32),
-            pltpu.VMEM((9 * CH, ATOM), BF16),
-            pltpu.VMEM((9 * CH, ATOM), BF16),
-            pltpu.VMEM((9 * CH, ATOM), BF16),
-            pltpu.VMEM((9 * CH, ATOM), BF16),
-            pltpu.VMEM((16, ATOM), F32),
-            pltpu.VMEM((48, ATOM), F32),
-        ],
-        compiler_params=pltpu.CompilerParams(vmem_limit_bytes=56 << 20),
-    )(edge_count, edge_src, edge_dst, sends, *shared)
+    messages, force, energy = edge_call(*shared)
     forces = pl.pallas_call(
         return_kernel,
         out_shape=shape((3, ATOM), F32),
@@ -591,9 +632,9 @@
             pltpu.SemaphoreType.DMA((NBR,)),
         ],
         compiler_params=pltpu.CompilerParams(
-            collective_id=1, has_side_effects=True, vmem_limit_bytes=16 << 20
+            collective_id=1, has_side_effects=True, vmem_limit_bytes=4 << 20
         ),
-    )(messages, force, sends)
+    )(messages, force, shared[0])
     return forces, energy.reshape(ATOM)
 
 

time: 73.1 us -> 43 us (0.59)
  local copies, waits for them, and re-layouts: 18.4 us -> 0.6 us
  Pallas kernels: 52.8 us -> 41 us
    unnamed x59 -> x1, local copies, waits for them, and re-layouts: 18.4 us -> 0.6 us
    pallas_call x2, Pallas kernels: 46 us -> 32.6 us  [the longest x1 17.1 us: edge_call(): pl.pallas_call(edge_kernel, out_shape=(shape((NBR, 8, ATOM), F32), shape(...]
    pallas_call x1, Pallas kernels: 6.74 us -> 8.4 us  [per_device(): pl.pallas_call(return_kernel, out_shape=shape((3, ATOM), F32), in_specs=[...]
where the time goes in v2:
time: 43 us; the launch traced here: 42.9 us
  Pallas kernels  41 us (95%)
  between operations  1.3 us (3%)
  local copies, waits for them, and re-layouts  0.6 us (1%)
    pallas_call x1, Pallas kernels, edge_call(): pl.pallas_call(edge_kernel, out_shape=(shape((NBR, 8, ATOM), F32), shape(...  17.1 us
    pallas_call x1, Pallas kernels, per_device(): pl.pallas_call(share_kernel, out_shape=(shape((16, LIST), F32), shape((16...  15.5 us
    pallas_call x1, Pallas kernels, per_device(): pl.pallas_call(return_kernel, out_shape=shape((3, ATOM), F32), in_specs=[...  8.4 us

profile of v2, /device:TPU:1, one launch (start us, length us, event | category | flops | bytes accessed | tf_op | source)
XLA Modules:
  0.0 42.9 jit_solution(10164104275527129284)
XLA Ops:
  1.3 15.5 %shard_map.131 = (f32[16,1152]{1,0:T(8,128)S(1)}, bf16[16,256]{1,0:T(8,128)(2,1)S(1)}, f32[8,8,1152]{2,1,0:T(8,128)S(1)}, bf16[128,64]{1,0:T(8,128)(2,1)S(1)}, b...) custom-call(s32[1]{0:T(128)S(6)} %copy.15.count_ref, ...), custom_call_target="tpu_custom_call" | custom-call | tf_op jit(solution)/shard_map/pallas_call | solution.py:571
  16.8 17.1 %shard_map.132 = (f32[8,8,256]{2,1,0:T(8,128)S(1)}, f32[3,256]{1,0:T(4,128)S(1)}, f32[1,256]{1,0:T(1,128)}) custom-call(f32[16,1152]{1,0:T(8,128)S(1)} %get-tuple-element.20.own_ref, bf16[16,256]{1,0:T(8,128)(2,1)S(1)} %get-tuple-element.21.table_ref, f32[8,8,1152]{2,1,0:T(8,128)S(1)} %get-tuple-element.22.recv_ref, ...), custom_call_target="tpu_custom_call" | custom-call | tf_op jit(solution)/shard_map/pallas_call | solution.py:535
  33.9 8.4 %shard_map.133 = f32[3,256]{1,0:T(4,128)S(1)} custom-call(f32[8,8,256]{2,1,0:T(8,128)S(1)} %get-tuple-element.35.msg_ref, f32[3,256]{1,0:T(4,128)S(1)} %get-tuple-element.36.force_ref, f32[16,1152]{1,0:T(8,128)S(1)} %get-tuple-element.20.own_ref), custom_call_target="tpu_custom_call" | custom-call | tf_op jit(solution)/shard_map/pallas_call | solution.py:624
  42.3 0.6 %copy.16 = f32[3,256]{1,0:T(4,128)} copy(f32[3,256]{1,0:T(4,128)S(1)} %shard_map.133) | data formatting | bytes 6144

commit v3 on v2

--- a/solution.py
+++ b/solution.py
@@ -22,7 +22,9 @@
 SLOTS = NBR * GHOST
 LIST = PAIR + 128
 CAP = 10 * PAIR
-EB = 1024
+EB = 2048
+SB = 2048
+NSUB = EB // SB
 F32 = jnp.float32
 BF16 = jnp.bfloat16
 I32 = jnp.int32
@@ -56,6 +58,20 @@
     rest = x - high
     mid = rest.astype(BF16).astype(F32)
     return high, mid, rest - mid
+
+
+def sigmoid(x):
+    return 0.5 * jnp.tanh(0.5 * x) + 0.5
+
+
+def triple(weight):
+    high, low = halves(weight)
+    return jnp.concatenate([high, high, low], axis=1)
+
+
+def stacked(x):
+    high, low = halves(x)
+    return jnp.concatenate([high, low, high], axis=0)
 
 
 def one_hot(row, count):
@@ -110,10 +126,9 @@
 ):
     sources, refs = refs[:11], refs[11:]
     (
-        own_ref, table_ref, recv_ref, wx_ref, up_ref, upl_ref, dn_ref, dnl_ref,
-        mt_ref, mtl_ref, mb_ref, mbl_ref, wr_ref, wrl_ref, ab_ref,
-    ) = refs[:15]
-    held, refs = refs[15:26], refs[26:]
+        own_ref, table_ref, recv_ref, wx_ref, up_ref, dn_ref, mt_ref, mb_ref, wr_ref, ab_ref,
+    ) = refs[:10]
+    held, refs = refs[10:21], refs[21:]
     out_buf, order_buf, load_sem, send_sem, recv_sem = refs
     (
         pos_ref, spec_ref, send_ref, src_ref, dst_ref,
@@ -203,8 +218,7 @@
         [first_high, first_high[:, 16:24], first_low, jnp.zeros((WIDTH, 8), F32)], axis=1
     ).astype(BF16)
     wr_high, wr_low = halves(jnp.concatenate([w_r, jnp.zeros((8, WIDTH), F32)], axis=0))
-    wr_ref[...] = jnp.concatenate([wr_high, wr_high], axis=1)
-    wrl_ref[...] = wr_low
+    wr_ref[...] = jnp.concatenate([wr_high, wr_high, wr_low], axis=1)
     w_mid = w_mid_ref[...]
     w_read = w_read_ref[...]
     down = jnp.concatenate(
@@ -213,26 +227,20 @@
     a_col = jnp.sum(w_mid * w_read, axis=1, keepdims=True)
     b_col = jnp.sum(w_back_ref[...] * w_read, axis=1, keepdims=True)
     ab_ref[...] = jnp.concatenate([a_col, b_col], axis=1)
-    dn_high, dn_low = halves(down)
-    dn_ref[...] = dn_high
-    dnl_ref[...] = dn_low
-    up = down.T
-    up_high, up_low = halves(up)
-    up_ref[...] = jnp.concatenate([up_high, up_high], axis=1)
-    upl_ref[...] = up_low
+    dn_ref[...] = triple(down)
+    up_ref[...] = triple(down.T)
     mix = jnp.concatenate(
         [w_mix_ref[pl.ds(WIDTH + degree, CH, stride=3), :] for degree in range(3)], axis=0
     )
-    mb_ref[...], mbl_ref[...] = halves(mix)
-    mt_ref[...], mtl_ref[...] = halves(mix.T)
+    mb_ref[...] = triple(mix)
+    mt_ref[...] = triple(mix.T)
     for copy in copies:
         copy.wait()
 
 
 def edge_kernel(
     own_ref, table_ref, recv_ref,
-    wx_ref, up_ref, upl_ref, dn_ref, dnl_ref, mt_ref, mtl_ref, mb_ref, mbl_ref,
-    wr_ref, wrl_ref, ab_ref,
+    wx_ref, up_ref, dn_ref, mt_ref, mb_ref, wr_ref, ab_ref,
     msg_ref, force_ref, energy_ref,
     edges, hots, paired, slope, mixed, mixed_low, d_value, geo, env, g_env,
     fields, terms, around, at_centre, at_partner,
@@ -311,10 +319,9 @@
         [own_index, sends[:, 0:ATOM], sends[:, ATOM:SLOTS], jnp.zeros((13, ATOM), F32)], axis=0
     ).astype(BF16)
 
-    def first_pass(block, carry):
-        begin = pl.multiple_of(block * EB, EB)
-        here = pl.ds(begin, EB)
-        valid = begin + lax.broadcasted_iota(I32, (1, EB), 1) < total
+    def first_geometry(begin):
+        here = pl.ds(pl.multiple_of(begin, SB), SB)
+        valid = begin + lax.broadcasted_iota(I32, (1, SB), 1) < total
         part = jnp.where(valid, edges[:, here], 0.0)
         code = part[4:5].astype(I32)
         seek = dot(codes, one_hot(code & 255, ATOM))
@@ -360,34 +367,46 @@
             geo[ANG + m : ANG + m + 1, here] = angular[m]
         inner = 1.0 - length2 * (1.0 / (CUTOFF * CUTOFF))
         alive = jnp.where(valid, 1.0, 0.0)
-        envelope = alive * inner * inner
-        geo[ENVL : ENVL + 1, here] = envelope
+        geo[ENVL : ENVL + 1, here] = alive * inner * inner
         geo[DENVL : DENVL + 1, here] = alive * inner * soft * (-4.0 / (CUTOFF * CUTOFF))
         geo[RINV : RINV + 1, here] = rinv
         geo[DIR : DIR + 3, here] = unit
         radial = geo[RAD : RAD + 8, here]
         radial_low = radial - radial.astype(BF16).astype(F32)
-        kinds = lax.broadcasted_iota(I32, (8, EB), 0)
+        kinds = lax.broadcasted_iota(I32, (8, SB), 0)
         hot_c = jnp.where(kinds == held[9:10].astype(I32), 1.0, 0.0)
         hot_p = jnp.where(kinds == part[3:4].astype(I32), 1.0, 0.0)
         inputs = jnp.concatenate(
-            [hot_c, hot_p, radial, radial_low, hot_c, hot_p, radial, jnp.zeros((8, EB), F32)], axis=0
+            [hot_c, hot_p, radial, radial_low, hot_c, hot_p, radial, jnp.zeros((8, SB), F32)], axis=0
         ).astype(BF16)
-        pre = dot(wx_ref[...], inputs)
-        gate = 1.0 / (1.0 + jnp.exp(-pre))
+        return dot(wx_ref[...], inputs)
+
+    def first_layers(begin, pre):
+        here = pl.ds(pl.multiple_of(begin, SB), SB)
+        gate = sigmoid(pre)
         act = pre * gate
         slope[:, here] = gate + act * (1.0 - gate)
-        act_high, act_low = halves(act)
-        after = dot(up_ref[...], jnp.concatenate([act_high, act_low], axis=0)) + dot(
-            upl_ref[...], act_high
-        )
+        after = dot(up_ref[...], stacked(act))
         paired[:, here] = after
         geo[ERAW : ERAW + 1, here] = jnp.sum(act * ab_ref[:, 0:1], axis=0, keepdims=True)
-        weights = after[0:CH] * envelope
+
+    def first_terms(sub, begin):
+        here = pl.ds(pl.multiple_of(begin, SB), SB)
+        weights = paired[0:CH, here] * geo[ENVL : ENVL + 1, here]
+        at = sub * SB
         for m in range(9):
-            term = weights if m == 0 else weights * angular[m]
+            term = weights if m == 0 else weights * geo[ANG + m : ANG + m + 1, here]
             rows = slice(m * CH, (m + 1) * CH)
-            terms[rows, 0:EB], terms[rows, EB:] = halves(term)
+            terms[rows, at : at + SB], terms[rows, EB + at : EB + at + SB] = halves(term)
+
+    def first_pass(block, carry):
+        begin = pl.multiple_of(block * EB, EB)
+        pres = [first_geometry(begin + i * SB) for i in range(NSUB)]
+        for i in range(NSUB):
+            first_layers(begin + i * SB, pres[i])
+        for i in range(NSUB):
+            first_terms(i, begin + i * SB)
+        hot = hots[:, pl.ds(begin, EB)]
         env[...] += dot_nt(terms[...], jnp.concatenate([hot, hot], axis=1))
         return carry
 
@@ -395,24 +414,27 @@
     fields[:, 0:ATOM], fields[:, ATOM:] = halves(env[...] * ENV_SCALE)
     degrees = (0, 1, 1, 1, 2, 2, 2, 2, 2)
 
-    def second_pass(block, carry):
-        here = pl.ds(pl.multiple_of(block * EB, EB), EB)
-        hot = hots[:, here]
-        angular = [geo[ANG + m : ANG + m + 1, here] for m in range(9)]
+    def gather(sub, begin):
+        hot = hots[:, pl.ds(pl.multiple_of(begin, SB), SB)]
+        both = jnp.concatenate([hot, hot], axis=0)
+        for lo, hi in ((0, 288), (288, 576)):
+            around[lo:hi, sub * SB : (sub + 1) * SB] = dot(fields[lo:hi, :], both)
+
+    def second_middle(sub, begin):
+        here = pl.ds(pl.multiple_of(begin, SB), SB)
+        at = sub * SB
+        there = slice(at, at + SB)
         envelope = geo[ENVL : ENVL + 1, here]
-        around[...] = dot(fields[...], jnp.concatenate([hot, hot], axis=0))
         sums = [None, None, None]
         for m in range(9):
-            got = around[m * CH : (m + 1) * CH, :]
-            term = got if m == 0 else got * angular[m]
+            got = around[m * CH : (m + 1) * CH, there]
+            term = got if m == 0 else got * geo[ANG + m : ANG + m + 1, here]
             degree = degrees[m]
             sums[degree] = term if sums[degree] is None else sums[degree] + term
         value = paired[CH : 2 * CH, here]
         invariant = jnp.concatenate([s * value for s in sums], axis=0)
-        high, low = halves(invariant)
-        mt = mt_ref[...]
-        pre = paired[2 * CH :, here] + dot(mt, high) + dot(mt, low) + dot(mtl_ref[...], high)
-        gate = 1.0 / (1.0 + jnp.exp(-pre))
+        pre = paired[2 * CH :, here] + dot(mt_ref[...], stacked(invariant))
+        gate = sigmoid(pre)
         act = pre * gate
         back = ab_ref[:, 1:2]
         geo[ERAW : ERAW + 1, here] += jnp.sum(act * back, axis=0, keepdims=True)
@@ -420,37 +442,46 @@
         d_high, d_low = halves(d_pre)
         mixed[:, here] = d_high
         mixed_low[:, here] = d_low
-        mb = mb_ref[...]
-        d_inv = dot(mb, d_high) + dot(mb, d_low) + dot(mbl_ref[...], d_high)
+        d_inv = dot(mb_ref[...], jnp.concatenate([d_high, d_low, d_high], axis=0))
         d_inv = [d_inv[i * CH : (i + 1) * CH] for i in range(3)]
         d_value[:, here] = d_inv[0] * sums[0] + d_inv[1] * sums[1] + d_inv[2] * sums[2]
         d_sum = [d * value for d in d_inv]
         for m in range(9):
             share = d_sum[degrees[m]]
-            term = share if m == 0 else share * angular[m]
+            term = share if m == 0 else share * geo[ANG + m : ANG + m + 1, here]
             rows = slice(m * CH, (m + 1) * CH)
-            terms[rows, 0:EB], terms[rows, EB:] = halves(term)
+            terms[rows, at : at + SB], terms[rows, EB + at : EB + at + SB] = halves(term)
             if m:
-                geo[DANG + m - 1 : DANG + m, here] = jnp.sum(share * around[rows, :], axis=0, keepdims=True)
-        g_env[...] += dot_nt(terms[...], jnp.concatenate([hot, hot], axis=1))
+                geo[DANG + m - 1 : DANG + m, here] = jnp.sum(share * around[rows, there], axis=0, keepdims=True)
+
+    def second_pass(block, carry):
+        begin = pl.multiple_of(block * EB, EB)
+        gather(0, begin)
+        for i in range(NSUB):
+            if i + 1 < NSUB:
+                gather(i + 1, begin + (i + 1) * SB)
+            second_middle(i, begin + i * SB)
+        hot = hots[:, pl.ds(begin, EB)]
+        both = jnp.concatenate([hot, hot], axis=1)
+        for lo, hi in ((0, 288), (288, 576)):
+            g_env[lo:hi, :] += dot_nt(terms[lo:hi, :], both)
         return carry
 
     lax.fori_loop(0, blocks, second_pass, 0)
     fields[:, 0:ATOM], fields[:, ATOM:] = halves(g_env[...] * ENV_SCALE)
 
-    def third_pass(block, carry):
-        here = pl.ds(pl.multiple_of(block * EB, EB), EB)
+    def third_middle(sub, begin):
+        here = pl.ds(pl.multiple_of(begin, SB), SB)
+        there = slice(sub * SB, (sub + 1) * SB)
         hot = hots[:, here]
-        angular = [geo[ANG + m : ANG + m + 1, here] for m in range(9)]
         envelope = geo[ENVL : ENVL + 1, here]
         raw = paired[0:CH, here]
         weights = raw * envelope
         d_weight = None
         d_ang = [None]
-        around[...] = dot(fields[...], jnp.concatenate([hot, hot], axis=0))
         for m in range(9):
-            got = around[m * CH : (m + 1) * CH, :]
-            term = got if m == 0 else got * angular[m]
+            got = around[m * CH : (m + 1) * CH, there]
+            term = got if m == 0 else got * geo[ANG + m : ANG + m + 1, here]
             d_weight = term if m == 0 else d_weight + term
             if m:
                 d_ang.append(
@@ -463,13 +494,9 @@
         )
         both_high = jnp.concatenate([pair_high, mixed[:, here]], axis=0)
         both_low = jnp.concatenate([pair_low, mixed_low[:, here]], axis=0)
-        dn = dn_ref[...]
-        d_act = dot(dn, both_high) + dot(dn, both_low) + dot(dnl_ref[...], both_high)
+        d_act = dot(dn_ref[...], jnp.concatenate([both_high, both_low, both_high], axis=0))
         d_act = d_act + ab_ref[:, 0:1] * envelope
-        d_pre_high, d_pre_low = halves(d_act * slope[:, here])
-        d_radial = dot(wr_ref[...], jnp.concatenate([d_pre_high, d_pre_low], axis=0)) + dot(
-            wrl_ref[...], d_pre_high
-        )
+        d_radial = dot(wr_ref[...], stacked(d_act * slope[:, here]))
         d_soft = jnp.sum(d_radial[0:8] * geo[DRAD : DRAD + 8, here], axis=0, keepdims=True)
         d_soft = d_soft + d_envelope * geo[DENVL : DENVL + 1, here]
         unit = geo[DIR : DIR + 3, here]
@@ -481,17 +508,24 @@
         along = d_soft - (d_ux * ux + d_uy * uy + d_uz * uz) * rinv
         pull = [d * rinv + u * along for d, u in ((d_ux, ux), (d_uy, uy), (d_uz, uz))]
         energy = e_raw * envelope
-        sent = jnp.concatenate([*pull, energy, jnp.zeros((4, EB), F32)], axis=0)
+        sent = jnp.concatenate([*pull, energy, jnp.zeros((4, SB), F32)], axis=0)
         sent = jnp.concatenate([sent, sent - sent.astype(BF16).astype(F32)], axis=0).astype(BF16)
         at_centre[...] += dot_nt(sent, hot)
-        code = jnp.where(
-            begin_valid(block, total), edges[5:6, here], 0.0
-        ).astype(I32)
-        seg = lax.broadcasted_iota(I32, (16, EB), 0) == (code >> 8)
+        valid = begin + lax.broadcasted_iota(I32, (1, SB), 1) < total
+        code = jnp.where(valid, edges[5:6, here], 0.0).astype(I32)
+        seg = lax.broadcasted_iota(I32, (16, SB), 0) == (code >> 8)
         spread = jnp.concatenate([jnp.where(seg, g, 0.0) for g in pull], axis=0)
         high, low = halves(spread)
         hot_partner = one_hot(code & 255, ATOM)
         at_partner[...] += dot_nt(high, hot_partner) + dot_nt(low, hot_partner)
+
+    def third_pass(block, carry):
+        begin = pl.multiple_of(block * EB, EB)
+        gather(0, begin)
+        for i in range(NSUB):
+            if i + 1 < NSUB:
+                gather(i + 1, begin + (i + 1) * SB)
+            third_middle(i, begin + i * SB)
         return carry
 
     lax.fori_loop(0, blocks, third_pass, 0)
@@ -507,10 +541,6 @@
             msg_ref[k, i : i + 1, :] = parts[16 * i + 3 + k : 16 * i + 4 + k]
             ghost = parts[16 * i + 1 + k // 4 : 16 * i + 2 + k // 4]
             msg_ref[k, 3 + i : 4 + i, 0:GHOST] = ghost[:, (k % 4) * GHOST : (k % 4 + 1) * GHOST]
-
-
-def begin_valid(block, total):
-    return block * EB + lax.broadcasted_iota(I32, (1, EB), 1) < total
 
 
 def return_kernel(msg_ref, force_ref, own_ref, out_ref, inbox, send_sem, recv_sem):
@@ -539,7 +569,7 @@
             shape((3, ATOM), F32),
             shape((1, ATOM), F32),
         ),
-        in_specs=[VMEM] * 15,
+        in_specs=[VMEM] * 10,
         out_specs=[VMEM] * 3,
         scratch_shapes=[
             pltpu.VMEM((8, CAP + 512), F32),
@@ -575,20 +605,15 @@
             shape((16, ATOM), BF16),
             shape((NBR, 8, LIST), F32),
             shape((WIDTH, 64), BF16),
-            shape((2 * WIDTH, 2 * WIDTH), BF16),
-            shape((2 * WIDTH, WIDTH), BF16),
-            shape((WIDTH, 2 * WIDTH), BF16),
-            shape((WIDTH, 2 * WIDTH), BF16),
-            shape((WIDTH, 3 * CH), BF16),
-            shape((WIDTH, 3 * CH), BF16),
-            shape((3 * CH, WIDTH), BF16),
-            shape((3 * CH, WIDTH), BF16),
-            shape((16, 2 * WIDTH), BF16),
-            shape((16, WIDTH), BF16),
+            shape((2 * WIDTH, 3 * WIDTH), BF16),
+            shape((WIDTH, 6 * WIDTH), BF16),
+            shape((WIDTH, 9 * CH), BF16),
+            shape((3 * CH, 3 * WIDTH), BF16),
+            shape((16, 3 * WIDTH), BF16),
             shape((WIDTH, 2), F32),
         ),
         in_specs=[SMEM] + [HBM] * 11,
-        out_specs=[VMEM] * 15,
+        out_specs=[VMEM] * 10,
         scratch_shapes=[
             pltpu.VMEM((3, ATOM), F32),
             pltpu.VMEM((1, ATOM), I32),

time: 43 us -> 39.1 us (0.909)
  Pallas kernels: 41 us -> 37.1 us
    pallas_call x1, Pallas kernels: 17.1 us -> 13.2 us  [edge_call(): pl.pallas_call(edge_kernel, out_shape=(shape((NBR, 8, ATOM), F32), shape(...]
where the time goes in v3:
time: 39.1 us; the launch traced here: 39 us
  Pallas kernels  37.1 us (95%)
  between operations  1.3 us (3%)
  local copies, waits for them, and re-layouts  0.6 us (2%)
    pallas_call x1, Pallas kernels, per_device(): pl.pallas_call(share_kernel, out_shape=(shape((16, LIST), F32), shape((16...  15.5 us
    pallas_call x1, Pallas kernels, edge_call(): pl.pallas_call(edge_kernel, out_shape=(shape((NBR, 8, ATOM), F32), shape(...  13.2 us
    pallas_call x1, Pallas kernels, per_device(): pl.pallas_call(return_kernel, out_shape=shape((3, ATOM), F32), in_specs=[...  8.39 us

profile of v3, /device:TPU:1, one launch (start us, length us, event | category | flops | bytes accessed | tf_op | source)
XLA Modules:
  0.0 39.0 jit_solution(8207146828236163321)
XLA Ops:
  1.3 15.5 %shard_map.131 = (f32[16,1152]{1,0:T(8,128)S(1)}, bf16[16,256]{1,0:T(8,128)(2,1)S(1)}, f32[8,8,1152]{2,1,0:T(8,128)S(1)}, bf16[128,64]{1,0:T(8,128)(2,1)S(1)}, b...) custom-call(s32[1]{0:T(128)S(6)} %copy.15.count_ref, ...), custom_call_target="tpu_custom_call" | custom-call | tf_op jit(solution)/shard_map/pallas_call | solution.py:601
  16.8 13.2 %shard_map.132 = (f32[8,8,256]{2,1,0:T(8,128)S(1)}, f32[3,256]{1,0:T(4,128)S(1)}, f32[1,256]{1,0:T(1,128)}) custom-call(f32[16,1152]{1,0:T(8,128)S(1)} %get-tuple-element.15.own_ref, bf16[16,256]{1,0:T(8,128)(2,1)S(1)} %get-tuple-element.16.table_ref, f32[8,8,1152]{2,1,0:T(8,128)S(1)} %get-tuple-element.17.recv_ref, ...), custom_call_target="tpu_custom_call" | custom-call | tf_op jit(solution)/shard_map/pallas_call | solution.py:565
  30.0 8.4 %shard_map.133 = f32[3,256]{1,0:T(4,128)S(1)} custom-call(f32[8,8,256]{2,1,0:T(8,128)S(1)} %get-tuple-element.25.msg_ref, f32[3,256]{1,0:T(4,128)S(1)} %get-tuple-element.26.force_ref, f32[16,1152]{1,0:T(8,128)S(1)} %get-tuple-element.15.own_ref), custom_call_target="tpu_custom_call" | custom-call | tf_op jit(solution)/shard_map/pallas_call | solution.py:649
  38.4 0.6 %copy.16 = f32[3,256]{1,0:T(4,128)} copy(f32[3,256]{1,0:T(4,128)S(1)} %shard_map.133) | data formatting | bytes 6144

commit v4 on v3

--- a/solution.py
+++ b/solution.py
@@ -22,9 +22,8 @@
 SLOTS = NBR * GHOST
 LIST = PAIR + 128
 CAP = 10 * PAIR
-EB = 2048
-SB = 2048
-NSUB = EB // SB
+MAIN = 2048
+EXTRA = 512
 F32 = jnp.float32
 BF16 = jnp.bfloat16
 I32 = jnp.int32
@@ -33,7 +32,10 @@
 SMEM = pl.BlockSpec(memory_space=pltpu.SMEM)
 HBM = pl.BlockSpec(memory_space=pltpu.HBM)
 
-RAD, DRAD, ANG, ENVL, DENVL, RINV, DIR, ERAW, DANG, ROWS = 0, 8, 16, 25, 26, 27, 28, 31, 32, 40
+RAD, DRAD, ANG, ENVL, DENVL, RINV, DIR, ERAW, DANG, CODE, ROWS = 0, 8, 16, 25, 26, 27, 28, 31, 32, 40, 48
+FIELD = 9 * CH
+ROOT3, ROOT5, ROOT15 = 3.0**0.5, 5.0**0.5, 15.0**0.5
+DEGREES = (0, 1, 1, 1, 2, 2, 2, 2, 2)
 
 
 def dot(a, b):
@@ -126,9 +128,9 @@
 ):
     sources, refs = refs[:11], refs[11:]
     (
-        own_ref, table_ref, recv_ref, wx_ref, up_ref, dn_ref, mt_ref, mb_ref, wr_ref, ab_ref,
-    ) = refs[:10]
-    held, refs = refs[10:21], refs[21:]
+        own_ref, table_ref, recv_ref, wx_ref, up_ref, dn_ref, mt_ref, mb_ref, wr_ref, ab_ref, cols_ref,
+    ) = refs[:11]
+    held, refs = refs[11:22], refs[22:]
     out_buf, order_buf, load_sem, send_sem, recv_sem = refs
     (
         pos_ref, spec_ref, send_ref, src_ref, dst_ref,
@@ -202,6 +204,7 @@
     own_ref[8:9, 0:PAIR] = src.astype(F32)
     own_ref[9:10, 0:PAIR] = dst.astype(F32)
     own_ref[10:11, 0:SLOTS] = sends.astype(F32)
+    cols_ref[...] = send_ref[...].astype(F32).T
     own_ref[11:12, PAIR:LIST] = jnp.full((1, 128), count_ref[0], I32).astype(F32)
     for load in loads[5:]:
         load.wait()
@@ -238,13 +241,84 @@
         copy.wait()
 
 
+def gather(fields, hot, around):
+    width = hot.shape[1]
+    both = jnp.concatenate([hot, hot], axis=0)
+    for lo, hi in ((0, 288), (288, FIELD)):
+        around[lo:hi, 0:width] = dot(fields[lo:hi, :], both)
+
+
+def scatter(terms, hot, total, count):
+    width = hot.shape[1]
+    both = jnp.concatenate([hot, hot], axis=1)
+    for lo, hi in ((0, 288), (288, count)):
+        total[lo:hi, :] += dot_nt(terms[lo:hi, 0 : 2 * width], both)
+
+
+def third_pass(store, begin, width, fields, around, dn_ref, wr_ref, ab_ref):
+    hots, slope, mixed, mixed_low, d_value, raw_ref, geo = store
+    here = pl.ds(begin, width)
+    gather(fields, hots[:, here], around)
+    envelope = geo[ENVL : ENVL + 1, here]
+    raw = raw_ref[:, here]
+    weights = raw * envelope
+    d_weight = None
+    d_ang = [None]
+    for m in range(9):
+        got = around[m * CH : (m + 1) * CH, 0:width]
+        term = got if m == 0 else got * geo[ANG + m : ANG + m + 1, here]
+        d_weight = term if m == 0 else d_weight + term
+        if m:
+            d_ang.append(
+                geo[DANG + m - 1 : DANG + m, here] + jnp.sum(weights * got, axis=0, keepdims=True)
+            )
+    d_envelope = geo[ERAW : ERAW + 1, here] + jnp.sum(d_weight * raw, axis=0, keepdims=True)
+    pair_high, pair_low = halves(jnp.concatenate([d_weight * envelope, d_value[:, here]], axis=0))
+    both_high = jnp.concatenate([pair_high, mixed[:, here]], axis=0)
+    both_low = jnp.concatenate([pair_low, mixed_low[:, here]], axis=0)
+    d_act = dot(dn_ref[...], jnp.concatenate([both_high, both_low, both_high], axis=0))
+    d_act = d_act + ab_ref[:, 0:1] * envelope
+    d_radial = dot(wr_ref[...], stacked(d_act * slope[:, here]))
+    d_soft = jnp.sum(d_radial[0:8] * geo[DRAD : DRAD + 8, here], axis=0, keepdims=True)
+    d_soft = d_soft + d_envelope * geo[DENVL : DENVL + 1, here]
+    unit = geo[DIR : DIR + 3, here]
+    rinv = geo[RINV : RINV + 1, here]
+    ux, uy, uz = unit[0:1], unit[1:2], unit[2:3]
+    d_ux = ROOT3 * d_ang[1] + ROOT15 * (uy * d_ang[4] + uz * d_ang[7] + ux * d_ang[8]) - ROOT5 * ux * d_ang[6]
+    d_uy = ROOT3 * d_ang[2] + ROOT15 * (ux * d_ang[4] + uz * d_ang[5] - uy * d_ang[8]) - ROOT5 * uy * d_ang[6]
+    d_uz = ROOT3 * d_ang[3] + ROOT15 * (uy * d_ang[5] + ux * d_ang[7]) + 2.0 * ROOT5 * uz * d_ang[6]
+    along = d_soft - (d_ux * ux + d_uy * uy + d_uz * uz) * rinv
+    return [d * rinv + u * along for d, u in ((d_ux, ux), (d_uy, uy), (d_uz, uz))]
+
+
+def to_partners(pull, geo, begin, width, at_partner):
+    code = geo[CODE : CODE + 1, pl.ds(begin, width)].astype(I32)
+    seg = lax.broadcasted_iota(I32, (16, width), 0) == (code >> 8)
+    high, low = halves(jnp.concatenate([jnp.where(seg, g, 0.0) for g in pull], axis=0))
+    hot = one_hot(code & 255, ATOM)
+    at_partner[...] += dot_nt(
+        jnp.concatenate([high, low], axis=1), jnp.concatenate([hot, hot], axis=1)
+    )
+
+
+def to_centres(pull, hots, begin, width, at_centre):
+    sent = jnp.concatenate([*pull, jnp.zeros((5, width), F32)], axis=0)
+    sent = jnp.concatenate([sent, sent - sent.astype(BF16).astype(F32)], axis=0).astype(BF16)
+    at_centre[...] += dot_nt(sent, hots[:, pl.ds(begin, width)])
+
+
 def edge_kernel(
     own_ref, table_ref, recv_ref,
-    wx_ref, up_ref, dn_ref, mt_ref, mb_ref, wr_ref, ab_ref,
-    msg_ref, force_ref, energy_ref,
-    edges, hots, paired, slope, mixed, mixed_low, d_value, geo, env, g_env,
-    fields, terms, around, at_centre, at_partner,
+    wx_ref, up_ref, dn_ref, mt_ref, mb_ref, wr_ref, ab_ref, cols_ref,
+    energy_ref, fields, at_centre, at_partner, hots, slope, mixed, mixed_low, d_value, raw, geo,
+    edges, value, base, more_hots, more_slope, more_mixed, more_low, more_d_value, more_raw, more_geo,
+    more_value, more_base, env, g_env, terms, around,
 ):
+    first_store = (hots, slope, mixed, mixed_low, d_value, raw, geo, value, base)
+    more_store = (
+        more_hots, more_slope, more_mixed, more_low, more_d_value, more_raw, more_geo,
+        more_value, more_base,
+    )
     count = own_ref[11:12, PAIR : PAIR + 128][0, 0].astype(I32)
     src = own_ref[8:9, 0:PAIR]
     dst = own_ref[9:10, 0:PAIR].astype(I32)
@@ -262,7 +336,7 @@
     lane = lax.broadcasted_iota(I32, (8, 128), 1)
     row = lax.broadcasted_iota(I32, (8, 128), 0)
 
-    def place(ref, size, begin, at, extra, tile):
+    def place(ref, size, begin, at, k, tile):
         base = tile * 128 - at + begin
         first = base >> 7
         turn = base & 127
@@ -274,10 +348,15 @@
         taken = jnp.where(
             lane < 128 - turn, pltpu.roll(left, back, 1), pltpu.roll(right, back, 1)
         )
+        if k is not None:
+            match = lax.broadcasted_iota(I32, (GHOST, 128), 0) == taken[4:5].astype(I32)
+            atom = jnp.sum(jnp.where(match, cols_ref[:, k : k + 1], 0.0), axis=0, keepdims=True)
+            taken = jnp.where(row == 4, atom, taken)
+            taken = jnp.where(row == 5, taken + F32(ATOM * (3 + k)), taken)
         here = pl.ds(pl.multiple_of(tile * 128, 128), 128)
         spot = tile * 128 + lane
         inside = (spot >= at) & (spot < at + size)
-        edges[:, here] = jnp.where(inside, taken + extra, edges[:, here])
+        edges[:, here] = jnp.where(inside, taken, edges[:, here])
 
     def scalar(ref, which):
         return ref[which : which + 1, PAIR : PAIR + 128][0, 0].astype(I32)
@@ -285,50 +364,41 @@
     at = count
     jobs = []
     size = scalar(own_ref, 4)
-    jobs.append((own_ref, size, 0, at, jnp.zeros((8, 128), F32), 4))
+    jobs.append((own_ref, size, 0, at, None, 4))
     at = at + size
     for k in range(NBR):
         ref = recv_ref.at[k]
         size = scalar(ref, 4)
-        extra = jnp.where(row == 4, F32(ATOM + GHOST * k), 0.0)
-        extra = jnp.where(row == 5, F32(ATOM * (3 + k)), extra)
-        jobs.append((ref, size, scalar(ref, 5), at, extra, 2))
+        jobs.append((ref, size, scalar(ref, 5), at, k, 2))
         at = at + size
     total = at
-    for ref, size, begin, at, extra, usual in jobs:
+    for ref, size, begin, at, k, usual in jobs:
         for step in range(usual):
-            place(ref, size, begin, at, extra, (at >> 7) + step)
-    for ref, size, begin, at, extra, usual in jobs:
+            place(ref, size, begin, at, k, (at >> 7) + step)
+    for ref, size, begin, at, k, usual in jobs:
         last = (at + size + 127) >> 7
 
-        def more(tile, carry, ref=ref, size=size, begin=begin, at=at, extra=extra):
-            place(ref, size, begin, at, extra, tile)
+        def more(tile, carry, ref=ref, size=size, begin=begin, at=at, k=k):
+            place(ref, size, begin, at, k, tile)
             return carry
 
         lax.fori_loop((at >> 7) + usual, last, more, 0)
-    blocks = lax.div(total + EB - 1, EB)
+    extra_blocks = lax.div(jnp.maximum(total - MAIN, 0) + EXTRA - 1, EXTRA)
 
     env[...] = jnp.zeros_like(env)
     g_env[...] = jnp.zeros_like(g_env)
+    terms[FIELD:, :] = jnp.zeros((16, 2 * MAIN), BF16)
     at_centre[...] = jnp.zeros_like(at_centre)
     at_partner[...] = jnp.zeros_like(at_partner)
-    root3, root5, root15 = 3.0**0.5, 5.0**0.5, 15.0**0.5
-    sends = own_ref[10:11, 0:SLOTS]
-    own_index = lax.broadcasted_iota(I32, (1, ATOM), 1).astype(F32)
-    codes = jnp.concatenate(
-        [own_index, sends[:, 0:ATOM], sends[:, ATOM:SLOTS], jnp.zeros((13, ATOM), F32)], axis=0
-    ).astype(BF16)
-
-    def first_geometry(begin):
-        here = pl.ds(pl.multiple_of(begin, SB), SB)
-        valid = begin + lax.broadcasted_iota(I32, (1, SB), 1) < total
-        part = jnp.where(valid, edges[:, here], 0.0)
-        code = part[4:5].astype(I32)
-        seek = dot(codes, one_hot(code & 255, ATOM))
-        kind = code >> 8
-        centre = jnp.where(kind == 0, seek[0:1], jnp.where(kind == 1, seek[1:2], seek[2:3]))
-        hot = one_hot(centre.astype(I32), ATOM)
+
+    def first_pass(store, begin, width, offset):
+        hots, slope, _, _, _, raw, geo, value, base = store
+        here = pl.ds(begin, width)
+        valid = begin + offset + lax.broadcasted_iota(I32, (1, width), 1) < total
+        part = jnp.where(valid, edges[:, pl.ds(begin + offset, width)], 0.0)
+        hot = one_hot(part[4:5].astype(I32), ATOM)
         hots[:, here] = hot
+        geo[CODE : CODE + 1, here] = part[5:6]
         held = dot(table, hot)
         delta = part[0:3] - joined(held)
         length2 = delta[0:1] * delta[0:1] + delta[1:2] * delta[1:2] + delta[2:3] * delta[2:3] + 1.0
@@ -354,90 +424,71 @@
             c_old, c_now = c_now, twice * c_now - c_old
         angular = [
             jnp.ones_like(ux),
-            root3 * ux,
-            root3 * uy,
-            root3 * uz,
-            root15 * ux * uy,
-            root15 * uy * uz,
-            0.5 * root5 * (2.0 * uz * uz - ux * ux - uy * uy),
-            root15 * ux * uz,
-            0.5 * root15 * (ux * ux - uy * uy),
+            ROOT3 * ux,
+            ROOT3 * uy,
+            ROOT3 * uz,
+            ROOT15 * ux * uy,
+            ROOT15 * uy * uz,
+            0.5 * ROOT5 * (2.0 * uz * uz - ux * ux - uy * uy),
+            ROOT15 * ux * uz,
+            0.5 * ROOT15 * (ux * ux - uy * uy),
         ]
         for m in range(9):
             geo[ANG + m : ANG + m + 1, here] = angular[m]
         inner = 1.0 - length2 * (1.0 / (CUTOFF * CUTOFF))
         alive = jnp.where(valid, 1.0, 0.0)
-        geo[ENVL : ENVL + 1, here] = alive * inner * inner
+        envelope = alive * inner * inner
+        geo[ENVL : ENVL + 1, here] = envelope
         geo[DENVL : DENVL + 1, here] = alive * inner * soft * (-4.0 / (CUTOFF * CUTOFF))
         geo[RINV : RINV + 1, here] = rinv
         geo[DIR : DIR + 3, here] = unit
         radial = geo[RAD : RAD + 8, here]
         radial_low = radial - radial.astype(BF16).astype(F32)
-        kinds = lax.broadcasted_iota(I32, (8, SB), 0)
+        kinds = lax.broadcasted_iota(I32, (8, width), 0)
         hot_c = jnp.where(kinds == held[9:10].astype(I32), 1.0, 0.0)
         hot_p = jnp.where(kinds == part[3:4].astype(I32), 1.0, 0.0)
         inputs = jnp.concatenate(
-            [hot_c, hot_p, radial, radial_low, hot_c, hot_p, radial, jnp.zeros((8, SB), F32)], axis=0
+            [hot_c, hot_p, radial, radial_low, hot_c, hot_p, radial, jnp.zeros((8, width), F32)], axis=0
         ).astype(BF16)
-        return dot(wx_ref[...], inputs)
-
-    def first_layers(begin, pre):
-        here = pl.ds(pl.multiple_of(begin, SB), SB)
+        pre = dot(wx_ref[...], inputs)
         gate = sigmoid(pre)
         act = pre * gate
         slope[:, here] = gate + act * (1.0 - gate)
         after = dot(up_ref[...], stacked(act))
-        paired[:, here] = after
+        raw[:, here] = after[0:CH]
+        value[:, here] = after[CH : 2 * CH]
+        base[:, here] = after[2 * CH :]
         geo[ERAW : ERAW + 1, here] = jnp.sum(act * ab_ref[:, 0:1], axis=0, keepdims=True)
-
-    def first_terms(sub, begin):
-        here = pl.ds(pl.multiple_of(begin, SB), SB)
-        weights = paired[0:CH, here] * geo[ENVL : ENVL + 1, here]
-        at = sub * SB
+        weights = after[0:CH] * envelope
         for m in range(9):
-            term = weights if m == 0 else weights * geo[ANG + m : ANG + m + 1, here]
+            term = weights if m == 0 else weights * angular[m]
             rows = slice(m * CH, (m + 1) * CH)
-            terms[rows, at : at + SB], terms[rows, EB + at : EB + at + SB] = halves(term)
-
-    def first_pass(block, carry):
-        begin = pl.multiple_of(block * EB, EB)
-        pres = [first_geometry(begin + i * SB) for i in range(NSUB)]
-        for i in range(NSUB):
-            first_layers(begin + i * SB, pres[i])
-        for i in range(NSUB):
-            first_terms(i, begin + i * SB)
-        hot = hots[:, pl.ds(begin, EB)]
-        env[...] += dot_nt(terms[...], jnp.concatenate([hot, hot], axis=1))
-        return carry
-
-    lax.fori_loop(0, blocks, first_pass, 0)
-    fields[:, 0:ATOM], fields[:, ATOM:] = halves(env[...] * ENV_SCALE)
-    degrees = (0, 1, 1, 1, 2, 2, 2, 2, 2)
-
-    def gather(sub, begin):
-        hot = hots[:, pl.ds(pl.multiple_of(begin, SB), SB)]
-        both = jnp.concatenate([hot, hot], axis=0)
-        for lo, hi in ((0, 288), (288, 576)):
-            around[lo:hi, sub * SB : (sub + 1) * SB] = dot(fields[lo:hi, :], both)
-
-    def second_middle(sub, begin):
-        here = pl.ds(pl.multiple_of(begin, SB), SB)
-        at = sub * SB
-        there = slice(at, at + SB)
+            terms[rows, 0:width], terms[rows, width : 2 * width] = halves(term)
+        scatter(terms, hot, env, FIELD)
+
+    def second_pass(store, begin, width):
+        hots, _, mixed, mixed_low, d_value, _, geo, value, base = store
+        here = pl.ds(begin, width)
+        hot = hots[:, here]
+        gather(fields, hot, around)
         envelope = geo[ENVL : ENVL + 1, here]
         sums = [None, None, None]
         for m in range(9):
-            got = around[m * CH : (m + 1) * CH, there]
+            got = around[m * CH : (m + 1) * CH, 0:width]
             term = got if m == 0 else got * geo[ANG + m : ANG + m + 1, here]
-            degree = degrees[m]
+            degree = DEGREES[m]
             sums[degree] = term if sums[degree] is None else sums[degree] + term
-        value = paired[CH : 2 * CH, here]
-        invariant = jnp.concatenate([s * value for s in sums], axis=0)
-        pre = paired[2 * CH :, here] + dot(mt_ref[...], stacked(invariant))
+        held = value[:, here]
+        invariant = jnp.concatenate([s * held for s in sums], axis=0)
+        pre = base[:, here] + dot(mt_ref[...], stacked(invariant))
         gate = sigmoid(pre)
         act = pre * gate
         back = ab_ref[:, 1:2]
-        geo[ERAW : ERAW + 1, here] += jnp.sum(act * back, axis=0, keepdims=True)
+        e_raw = geo[ERAW : ERAW + 1, here] + jnp.sum(act * back, axis=0, keepdims=True)
+        geo[ERAW : ERAW + 1, here] = e_raw
+        energy = e_raw * envelope
+        energy = jnp.concatenate([energy, jnp.zeros((15, width), F32)], axis=0)
+        terms[FIELD:, 0:width], terms[FIELD:, width : 2 * width] = halves(energy)
         d_pre = (gate + act * (1.0 - gate)) * back * envelope
         d_high, d_low = halves(d_pre)
         mixed[:, here] = d_high
@@ -445,113 +496,72 @@
         d_inv = dot(mb_ref[...], jnp.concatenate([d_high, d_low, d_high], axis=0))
         d_inv = [d_inv[i * CH : (i + 1) * CH] for i in range(3)]
         d_value[:, here] = d_inv[0] * sums[0] + d_inv[1] * sums[1] + d_inv[2] * sums[2]
-        d_sum = [d * value for d in d_inv]
+        d_sum = [d * held for d in d_inv]
         for m in range(9):
-            share = d_sum[degrees[m]]
+            share = d_sum[DEGREES[m]]
             term = share if m == 0 else share * geo[ANG + m : ANG + m + 1, here]
             rows = slice(m * CH, (m + 1) * CH)
-            terms[rows, at : at + SB], terms[rows, EB + at : EB + at + SB] = halves(term)
+            terms[rows, 0:width], terms[rows, width : 2 * width] = halves(term)
             if m:
-                geo[DANG + m - 1 : DANG + m, here] = jnp.sum(share * around[rows, there], axis=0, keepdims=True)
-
-    def second_pass(block, carry):
-        begin = pl.multiple_of(block * EB, EB)
-        gather(0, begin)
-        for i in range(NSUB):
-            if i + 1 < NSUB:
-                gather(i + 1, begin + (i + 1) * SB)
-            second_middle(i, begin + i * SB)
-        hot = hots[:, pl.ds(begin, EB)]
-        both = jnp.concatenate([hot, hot], axis=1)
-        for lo, hi in ((0, 288), (288, 576)):
-            g_env[lo:hi, :] += dot_nt(terms[lo:hi, :], both)
-        return carry
-
-    lax.fori_loop(0, blocks, second_pass, 0)
-    fields[:, 0:ATOM], fields[:, ATOM:] = halves(g_env[...] * ENV_SCALE)
-
-    def third_middle(sub, begin):
-        here = pl.ds(pl.multiple_of(begin, SB), SB)
-        there = slice(sub * SB, (sub + 1) * SB)
-        hot = hots[:, here]
-        envelope = geo[ENVL : ENVL + 1, here]
-        raw = paired[0:CH, here]
-        weights = raw * envelope
-        d_weight = None
-        d_ang = [None]
-        for m in range(9):
-            got = around[m * CH : (m + 1) * CH, there]
-            term = got if m == 0 else got * geo[ANG + m : ANG + m + 1, here]
-            d_weight = term if m == 0 else d_weight + term
-            if m:
-                d_ang.append(
-                    geo[DANG + m - 1 : DANG + m, here] + jnp.sum(weights * got, axis=0, keepdims=True)
+                geo[DANG + m - 1 : DANG + m, here] = jnp.sum(
+                    share * around[rows, 0:width], axis=0, keepdims=True
                 )
-        e_raw = geo[ERAW : ERAW + 1, here]
-        d_envelope = e_raw + jnp.sum(d_weight * raw, axis=0, keepdims=True)
-        pair_high, pair_low = halves(
-            jnp.concatenate([d_weight * envelope, d_value[:, here]], axis=0)
+        scatter(terms, hot, g_env, FIELD + 16)
+
+    def rest(step):
+        def body(block, carry):
+            step(pl.multiple_of(block * EXTRA, EXTRA))
+            return carry
+
+        lax.fori_loop(0, extra_blocks, body, 0)
+
+    first_pass(first_store, 0, MAIN, 0)
+    rest(lambda begin: first_pass(more_store, begin, EXTRA, MAIN))
+    fields[:, 0:ATOM], fields[:, ATOM:] = halves(env[...] * ENV_SCALE)
+    second_pass(first_store, 0, MAIN)
+    rest(lambda begin: second_pass(more_store, begin, EXTRA))
+    energy_ref[...] = g_env[FIELD : FIELD + 1, :]
+    fields[:, 0:ATOM], fields[:, ATOM:] = halves(g_env[0:FIELD, :] * ENV_SCALE)
+
+    def third(begin):
+        pull = third_pass(
+            (more_hots, more_slope, more_mixed, more_low, more_d_value, more_raw, more_geo),
+            begin, EXTRA, fields, around, dn_ref, wr_ref, ab_ref,
         )
-        both_high = jnp.concatenate([pair_high, mixed[:, here]], axis=0)
-        both_low = jnp.concatenate([pair_low, mixed_low[:, here]], axis=0)
-        d_act = dot(dn_ref[...], jnp.concatenate([both_high, both_low, both_high], axis=0))
-        d_act = d_act + ab_ref[:, 0:1] * envelope
-        d_radial = dot(wr_ref[...], stacked(d_act * slope[:, here]))
-        d_soft = jnp.sum(d_radial[0:8] * geo[DRAD : DRAD + 8, here], axis=0, keepdims=True)
-        d_soft = d_soft + d_envelope * geo[DENVL : DENVL + 1, here]
-        unit = geo[DIR : DIR + 3, here]
-        rinv = geo[RINV : RINV + 1, here]
-        ux, uy, uz = unit[0:1], unit[1:2], unit[2:3]
-        d_ux = root3 * d_ang[1] + root15 * (uy * d_ang[4] + uz * d_ang[7] + ux * d_ang[8]) - root5 * ux * d_ang[6]
-        d_uy = root3 * d_ang[2] + root15 * (ux * d_ang[4] + uz * d_ang[5] - uy * d_ang[8]) - root5 * uy * d_ang[6]
-        d_uz = root3 * d_ang[3] + root15 * (uy * d_ang[5] + ux * d_ang[7]) + 2.0 * root5 * uz * d_ang[6]
-        along = d_soft - (d_ux * ux + d_uy * uy + d_uz * uz) * rinv
-        pull = [d * rinv + u * along for d, u in ((d_ux, ux), (d_uy, uy), (d_uz, uz))]
-        energy = e_raw * envelope
-        sent = jnp.concatenate([*pull, energy, jnp.zeros((4, SB), F32)], axis=0)
-        sent = jnp.concatenate([sent, sent - sent.astype(BF16).astype(F32)], axis=0).astype(BF16)
-        at_centre[...] += dot_nt(sent, hot)
-        valid = begin + lax.broadcasted_iota(I32, (1, SB), 1) < total
-        code = jnp.where(valid, edges[5:6, here], 0.0).astype(I32)
-        seg = lax.broadcasted_iota(I32, (16, SB), 0) == (code >> 8)
-        spread = jnp.concatenate([jnp.where(seg, g, 0.0) for g in pull], axis=0)
-        high, low = halves(spread)
-        hot_partner = one_hot(code & 255, ATOM)
-        at_partner[...] += dot_nt(high, hot_partner) + dot_nt(low, hot_partner)
-
-    def third_pass(block, carry):
-        begin = pl.multiple_of(block * EB, EB)
-        gather(0, begin)
-        for i in range(NSUB):
-            if i + 1 < NSUB:
-                gather(i + 1, begin + (i + 1) * SB)
-            third_middle(i, begin + i * SB)
-        return carry
-
-    lax.fori_loop(0, blocks, third_pass, 0)
-    sums = at_centre[...]
-    sums = sums[0:8] + sums[8:16]
+        to_partners(pull, more_geo, begin, EXTRA, at_partner)
+        to_centres(pull, more_hots, begin, EXTRA, at_centre)
+
+    rest(third)
+
+
+def return_kernel(
+    own_ref, dn_ref, wr_ref, ab_ref,
+    fields, more_centre, more_partner, hots, slope, mixed, mixed_low, d_value, raw, geo,
+    out_ref, outbox, inbox, around, at_centre, at_partner, send_sem, recv_sem,
+):
+    barrier, peers = greet()
+    at_centre[...] = more_centre[...]
+    at_partner[...] = more_partner[...]
+    store = (hots, slope, mixed, mixed_low, d_value, raw, geo)
+    pull = third_pass(store, 0, MAIN, fields, around, dn_ref, wr_ref, ab_ref)
+    to_partners(pull, geo, 0, MAIN, at_partner)
     parts = at_partner[...]
-    mine = [parts[16 * i : 16 * i + 1] for i in range(3)]
-    force_ref[...] = sums[0:3] - jnp.concatenate(mine, axis=0)
-    energy_ref[...] = sums[3:4]
-    msg_ref[...] = jnp.zeros_like(msg_ref)
+    outbox[...] = jnp.zeros_like(outbox)
     for k in range(NBR):
         for i in range(3):
-            msg_ref[k, i : i + 1, :] = parts[16 * i + 3 + k : 16 * i + 4 + k]
+            outbox[k, i : i + 1, :] = parts[16 * i + 3 + k : 16 * i + 4 + k]
             ghost = parts[16 * i + 1 + k // 4 : 16 * i + 2 + k // 4]
-            msg_ref[k, 3 + i : 4 + i, 0:GHOST] = ghost[:, (k % 4) * GHOST : (k % 4 + 1) * GHOST]
-
-
-def return_kernel(msg_ref, force_ref, own_ref, out_ref, inbox, send_sem, recv_sem):
-    barrier, peers = greet()
+            outbox[k, 3 + i : 4 + i, 0:GHOST] = ghost[:, (k % 4) * GHOST : (k % 4 + 1) * GHOST]
+    pl.semaphore_wait(barrier, NBR)
+    copies = swap(peers, outbox, inbox, send_sem, recv_sem)
+    to_centres(pull, hots, 0, MAIN, at_centre)
     sends = own_ref[10:11, 0:SLOTS].astype(I32)
     hot = one_hot(sends, ATOM)
-    pl.semaphore_wait(barrier, NBR)
-    copies = swap(peers, msg_ref, inbox, send_sem, recv_sem)
+    sums = at_centre[...]
+    total = sums[0:3] + sums[8:11]
+    total = total - jnp.concatenate([parts[16 * i : 16 * i + 1] for i in range(3)], axis=0)
     for copy in copies:
         copy.wait()
-    total = force_ref[...]
     for k in range(NBR):
         total = total - inbox[k, 0:3, :]
     ghosts = jnp.concatenate([inbox[k, 3:6, 0:GHOST] for k in range(NBR)], axis=1)
@@ -562,33 +572,43 @@
 
 def edge_call(*operands):
     shape = jax.ShapeDtypeStruct
+    rest = CAP - MAIN
+
+    def store(lanes, make):
+        return [
+            make((ATOM, lanes), BF16),
+            make((WIDTH, lanes), F32),
+            make((WIDTH, lanes), BF16),
+            make((WIDTH, lanes), BF16),
+            make((CH, lanes), F32),
+            make((CH, lanes), F32),
+            make((ROWS, lanes), F32),
+        ]
+
     return pl.pallas_call(
         edge_kernel,
         out_shape=(
-            shape((NBR, 8, ATOM), F32),
-            shape((3, ATOM), F32),
             shape((1, ATOM), F32),
+            shape((FIELD, 2 * ATOM), BF16),
+            shape((16, ATOM), F32),
+            shape((48, ATOM), F32),
+            *store(MAIN, shape),
         ),
-        in_specs=[VMEM] * 10,
-        out_specs=[VMEM] * 3,
+        in_specs=[VMEM] * 11,
+        out_specs=[VMEM] * 11,
         scratch_shapes=[
             pltpu.VMEM((8, CAP + 512), F32),
-            pltpu.VMEM((ATOM, CAP), BF16),
-            pltpu.VMEM((2 * WIDTH, CAP), F32),
-            pltpu.VMEM((WIDTH, CAP), F32),
-            pltpu.VMEM((WIDTH, CAP), BF16),
-            pltpu.VMEM((WIDTH, CAP), BF16),
-            pltpu.VMEM((CH, CAP), F32),
-            pltpu.VMEM((ROWS, CAP), F32),
-            pltpu.VMEM((9 * CH, ATOM), F32),
-            pltpu.VMEM((9 * CH, ATOM), F32),
-            pltpu.VMEM((9 * CH, 2 * ATOM), BF16),
-            pltpu.VMEM((9 * CH, 2 * EB), BF16),
-            pltpu.VMEM((9 * CH, EB), F32),
-            pltpu.VMEM((16, ATOM), F32),
-            pltpu.VMEM((48, ATOM), F32),
+            pltpu.VMEM((CH, MAIN), F32),
+            pltpu.VMEM((WIDTH, MAIN), F32),
+            *store(rest, pltpu.VMEM),
+            pltpu.VMEM((CH, rest), F32),
+            pltpu.VMEM((WIDTH, rest), F32),
+            pltpu.VMEM((FIELD, ATOM), F32),
+            pltpu.VMEM((FIELD + 16, ATOM), F32),
+            pltpu.VMEM((FIELD + 16, 2 * MAIN), BF16),
+            pltpu.VMEM((FIELD, MAIN), F32),
         ],
-        compiler_params=pltpu.CompilerParams(vmem_limit_bytes=48 << 20),
+        compiler_params=pltpu.CompilerParams(vmem_limit_bytes=46 << 20),
     )(*operands)
 
 
@@ -611,9 +631,10 @@
             shape((3 * CH, 3 * WIDTH), BF16),
             shape((16, 3 * WIDTH), BF16),
             shape((WIDTH, 2), F32),
+            shape((GHOST, NBR), F32),
         ),
         in_specs=[SMEM] + [HBM] * 11,
-        out_specs=[VMEM] * 10,
+        out_specs=[VMEM] * 11,
         scratch_shapes=[
             pltpu.VMEM((3, ATOM), F32),
             pltpu.VMEM((1, ATOM), I32),
@@ -645,21 +666,26 @@
             )
         ),
     )
-    messages, force, energy = edge_call(*shared)
+    energy, *kept = edge_call(*shared)
+    own, dn, wr, ab = shared[0], shared[5], shared[8], shared[9]
     forces = pl.pallas_call(
         return_kernel,
         out_shape=shape((3, ATOM), F32),
-        in_specs=[VMEM] * 3,
+        in_specs=[VMEM] * 14,
         out_specs=VMEM,
         scratch_shapes=[
             pltpu.VMEM((NBR, 8, ATOM), F32),
+            pltpu.VMEM((NBR, 8, ATOM), F32),
+            pltpu.VMEM((FIELD, MAIN), F32),
+            pltpu.VMEM((16, ATOM), F32),
+            pltpu.VMEM((48, ATOM), F32),
             pltpu.SemaphoreType.DMA((NBR,)),
             pltpu.SemaphoreType.DMA((NBR,)),
         ],
         compiler_params=pltpu.CompilerParams(
-            collective_id=1, has_side_effects=True, vmem_limit_bytes=4 << 20
+            collective_id=1, has_side_effects=True, vmem_limit_bytes=20 << 20
         ),
-    )(messages, force, shared[0])
+    )(own, dn, wr, ab, *kept)
     return forces, energy.reshape(ATOM)
 
 

time: 39.1 us -> 35.3 us (0.903)
  Pallas kernels: 37.1 us -> 33.3 us
    pallas_call x1, Pallas kernels: 13.2 us -> 9.26 us  [edge_call(): pl.pallas_call(edge_kernel, out_shape=(shape((1, ATOM), F32), shape((FIEL...]
where the time goes in v4:
time: 35.3 us; the launch traced here: 35.2 us
  Pallas kernels  33.3 us (94%)
  between operations  1.3 us (4%)
  local copies, waits for them, and re-layouts  0.6 us (2%)
    pallas_call x1, Pallas kernels, per_device(): pl.pallas_call(share_kernel, out_shape=(shape((16, LIST), F32), shape((16...  15.5 us
    pallas_call x1, Pallas kernels, edge_call(): pl.pallas_call(edge_kernel, out_shape=(shape((1, ATOM), F32), shape((FIEL...  9.26 us
    pallas_call x1, Pallas kernels, per_device(): pl.pallas_call(return_kernel, out_shape=shape((3, ATOM), F32), in_specs=[...  8.46 us

profile of v4, /device:TPU:1, one launch (start us, length us, event | category | flops | bytes accessed | tf_op | source)
XLA Modules:
  0.0 35.2 jit_solution(5104856204490359041)
XLA Ops:
  1.3 15.5 %shard_map.131 = (f32[16,1152]{1,0:T(8,128)S(1)}, bf16[16,256]{1,0:T(8,128)(2,1)S(1)}, f32[8,8,1152]{2,1,0:T(8,128)S(1)}, bf16[128,64]{1,0:T(8,128)(2,1)S(1)}, b...) custom-call(s32[1]{0:T(128)S(6)} %copy.15.count_ref, ...), custom_call_target="tpu_custom_call" | custom-call | tf_op jit(solution)/shard_map/pallas_call | solution.py:621
  16.8 9.3 %shard_map.132 = (f32[1,256]{1,0:T(1,128)}, bf16[576,512]{1,0:T(8,128)(2,1)S(1)}, f32[16,256]{1,0:T(8,128)S(1)}, f32[48,256]{1,0:T(8,128)S(1)}, bf16[256,2048]{1...) custom-call(f32[16,1152]{1,0:T(8,128)S(1)} %get-tuple-element.24.own, ...), custom_call_target="tpu_custom_call" | custom-call | tf_op jit(solution)/shard_map/pallas_call | solution.py:588
  26.1 8.5 %shard_map.133 = f32[3,256]{1,0:T(4,128)S(1)} custom-call(f32[16,1152]{1,0:T(8,128)S(1)} %get-tuple-element.24.own_ref, bf16[128,768]{1,0:T(8,128)(2,1)S(1)} %get-tuple-element.25.dn_ref, bf16[16,384]{1,0:T(8,128)(2,1)S(1)} %get-tuple-element.26.wr_ref, f32[128,2]{1,0:T(8,128)S(1)} %get-tuple-element.27.ab_ref, ...), custom_call_target="tpu_custom_call" | custom-call | tf_op jit(solution)/shard_map/pallas_call | solution.py:671
  34.6 0.6 %copy.16 = f32[3,256]{1,0:T(4,128)} copy(f32[3,256]{1,0:T(4,128)S(1)} %shard_map.133) | data formatting | bytes 6144

commit v5 on v4

--- a/solution.py
+++ b/solution.py
@@ -20,7 +20,7 @@
 GHOST = 64
 PAIR = 1024
 SLOTS = NBR * GHOST
-LIST = PAIR + 128
+LIST = 512
 CAP = 10 * PAIR
 MAIN = 2048
 EXTRA = 512
@@ -129,8 +129,9 @@
     sources, refs = refs[:11], refs[11:]
     (
         own_ref, table_ref, recv_ref, wx_ref, up_ref, dn_ref, mt_ref, mb_ref, wr_ref, ab_ref, cols_ref,
-    ) = refs[:11]
-    held, refs = refs[11:22], refs[22:]
+        home_ref,
+    ) = refs[:12]
+    held, refs = refs[12:23], refs[23:]
     out_buf, order_buf, load_sem, send_sem, recv_sem = refs
     (
         pos_ref, spec_ref, send_ref, src_ref, dst_ref,
@@ -178,37 +179,45 @@
         offset = offset + sums[i]
     spot = jnp.concatenate(spots, axis=1)
     spot = jnp.where(live, spot, -1.0).astype(I32)
-    picked = dot(table, one_hot(src, ATOM))
     data = jnp.concatenate(
-        [picked[0:10], place.astype(F32), src.astype(F32), jnp.zeros((4, PAIR), F32)], axis=0
+        [place.astype(F32), src.astype(F32), jnp.zeros((14, PAIR), F32)], axis=0
     ).astype(BF16)
     for i in range(PAIR // ATOM):
         rows = lax.broadcasted_iota(I32, (ATOM, PAIR), 0) + i * ATOM
         chosen = jnp.where(rows == spot, 1.0, 0.0).astype(BF16)
-        order_buf[:, i * ATOM : (i + 1) * ATOM] = dot_nt(data, chosen)
-    ordered = order_buf[...]
-    entries = jnp.concatenate(
-        [joined(ordered), ordered[9:12], jnp.zeros((2, PAIR), F32)], axis=0
-    )
+        ordered = dot_nt(data, chosen)
+        for j in range(2):
+            for half in range(2):
+                order_buf[2 * i + half : 2 * i + half + 1, j * 128 : (j + 1) * 128] = ordered[
+                    j : j + 1, half * 128 : (half + 1) * 128
+                ]
+    atoms = jnp.concatenate([pos_ref[...], spec_ref[...].astype(F32)], axis=0)
+    for i in range(4):
+        for half in range(2):
+            order_buf[2 * i + half : 2 * i + half + 1, 256:384] = atoms[
+                i : i + 1, half * 128 : (half + 1) * 128
+            ]
+    entries = order_buf[...]
     none = jnp.zeros((8, GHOST), F32)
+    indices = sends.astype(F32)
     for k in range(NBR):
-        out_buf[k, :, 0:PAIR] = entries
-        mine = jnp.concatenate([ghost_rows[:, k * GHOST : (k + 1) * GHOST], none[0:4]], axis=0)
-        out_buf[k, :, PAIR:LIST] = jnp.concatenate([mine, none], axis=1)
-        out_buf[k, 4:5, PAIR:LIST] = jnp.broadcast_to(total[k + 1 : k + 2, :], (1, 128))
-        out_buf[k, 5:6, PAIR:LIST] = jnp.broadcast_to(start[k + 1 : k + 2, :], (1, 128))
+        out_buf[k, :, 0:384] = entries
+        part = slice(k * GHOST, (k + 1) * GHOST)
+        mine = jnp.concatenate([ghost_rows[:, part], none[0:2], indices[:, part], none[0:1]], axis=0)
+        out_buf[k, :, 384:LIST] = jnp.concatenate([mine, none], axis=1)
+        out_buf[k, 4:5, 384:LIST] = jnp.broadcast_to(total[k + 1 : k + 2, :], (1, 128))
+        out_buf[k, 5:6, 384:LIST] = jnp.broadcast_to(start[k + 1 : k + 2, :], (1, 128))
     pl.semaphore_wait(barrier, NBR)
     copies = swap(peers, out_buf, recv_ref, send_sem, recv_sem)
-    own_ref[0:8, 0:PAIR] = entries
-    own_ref[:, PAIR:LIST] = jnp.zeros((16, 128), F32)
-    own_ref[8:9, 0:PAIR] = src.astype(F32)
-    own_ref[9:10, 0:PAIR] = dst.astype(F32)
-    own_ref[10:11, 0:SLOTS] = sends.astype(F32)
+    home_ref[:, 0:384] = entries
+    home_ref[:, 384:LIST] = jnp.zeros((8, 128), F32)
+    home_ref[4:5, 384:LIST] = jnp.broadcast_to(total[0:1, :], (1, 128))
+    own_ref[0:1, :] = src.astype(F32)
+    own_ref[1:2, :] = dst.astype(F32)
+    own_ref[2:3, :] = jnp.full((1, PAIR), count_ref[0], I32).astype(F32)
     cols_ref[...] = send_ref[...].astype(F32).T
-    own_ref[11:12, PAIR:LIST] = jnp.full((1, 128), count_ref[0], I32).astype(F32)
     for load in loads[5:]:
         load.wait()
-    own_ref[4:5, PAIR:LIST] = jnp.broadcast_to(total[0:1, :], (1, 128))
     w_in = w_in_ref[...]
     w_c = w_in[0:SPECIES].T
     w_p = w_in[SPECIES : 2 * SPECIES].T
@@ -309,77 +318,92 @@
 
 def edge_kernel(
     own_ref, table_ref, recv_ref,
-    wx_ref, up_ref, dn_ref, mt_ref, mb_ref, wr_ref, ab_ref, cols_ref,
+    wx_ref, up_ref, dn_ref, mt_ref, mb_ref, wr_ref, ab_ref, cols_ref, home_ref,
     energy_ref, fields, at_centre, at_partner, hots, slope, mixed, mixed_low, d_value, raw, geo,
-    edges, value, base, more_hots, more_slope, more_mixed, more_low, more_d_value, more_raw, more_geo,
-    more_value, more_base, env, g_env, terms, around,
+    edges, base, more_hots, more_slope, more_mixed, more_low, more_d_value, more_raw, more_geo,
+    more_base, env, g_env, terms, around, lines,
 ):
-    first_store = (hots, slope, mixed, mixed_low, d_value, raw, geo, value, base)
+    first_store = (hots, slope, mixed, mixed_low, d_value, raw, geo, base)
     more_store = (
         more_hots, more_slope, more_mixed, more_low, more_d_value, more_raw, more_geo,
-        more_value, more_base,
+        more_base,
     )
-    count = own_ref[11:12, PAIR : PAIR + 128][0, 0].astype(I32)
-    src = own_ref[8:9, 0:PAIR]
-    dst = own_ref[9:10, 0:PAIR].astype(I32)
-    near = jnp.concatenate([recv_ref[k, 0:4, PAIR : PAIR + GHOST] for k in range(NBR)], axis=1)
-    ghosts = atom_table(near[0:3], near[3:4]).astype(BF16)
+    count = own_ref[2:3, 0:128][0, 0].astype(I32)
+    src = own_ref[0:1, :]
+    dst = own_ref[1:2, :].astype(I32)
+    near = jnp.concatenate([recv_ref[k, :, 384 : 384 + GHOST] for k in range(NBR)], axis=1)
+    ghosts = jnp.concatenate(
+        [*thirds(near[0:3]), near[3:4], near[6:7], jnp.zeros((5, SLOTS), F32)], axis=0
+    ).astype(BF16)
     table = table_ref[...]
     segments = jnp.concatenate([table, ghosts[:, 0:ATOM], ghosts[:, ATOM:SLOTS]], axis=0)
     found = dot(segments, one_hot(dst & 255, ATOM))
     part = dst >> 8
     picked = jnp.where(part == 0, found[0:16], jnp.where(part == 1, found[16:32], found[32:48]))
+    beyond = (((dst - ATOM) >> 6) + 3).astype(F32) * ATOM + picked[10:11]
+    code = jnp.where(part == 0, dst.astype(F32), beyond)
     edges[:, 0:PAIR] = jnp.concatenate(
-        [joined(picked), picked[9:10], src, dst.astype(F32), jnp.zeros((2, PAIR), F32)],
-        axis=0,
+        [joined(picked), picked[9:10], src, code, jnp.zeros((2, PAIR), F32)], axis=0
     )
     lane = lax.broadcasted_iota(I32, (8, 128), 1)
     row = lax.broadcasted_iota(I32, (8, 128), 0)
 
-    def place(ref, size, begin, at, k, tile):
+    def kept(ref):
+        halves_of = [
+            jnp.concatenate([ref[2 * i : 2 * i + 1, 256:384], ref[2 * i + 1 : 2 * i + 2, 256:384]], axis=1)
+            for i in range(4)
+        ]
+        return atom_table(jnp.concatenate(halves_of[0:3], axis=0), halves_of[3]).astype(BF16)
+
+    def place(ref, size, begin, at, k, held, tile):
         base = tile * 128 - at + begin
         first = base >> 7
         turn = base & 127
-        low = jnp.clip(first, 0, 8)
-        high = jnp.clip(first + 1, 0, 8)
-        left = ref[0:8, pl.ds(pl.multiple_of(low * 128, 128), 128)]
-        right = ref[0:8, pl.ds(pl.multiple_of(high * 128, 128), 128)]
+        low = jnp.clip(first, 0, 7)
+        high = jnp.clip(first + 1, 0, 7)
+        which = NBR if k is None else k
+        left, right = lines[which, low], lines[which, high]
         back = lax.rem(128 - turn, 128)
         taken = jnp.where(
             lane < 128 - turn, pltpu.roll(left, back, 1), pltpu.roll(right, back, 1)
         )
+        found = dot(held, one_hot(taken[5:6].astype(I32), ATOM))
+        partner = jnp.concatenate([joined(found), found[9:10], jnp.zeros((4, 128), F32)], axis=0)
         if k is not None:
             match = lax.broadcasted_iota(I32, (GHOST, 128), 0) == taken[4:5].astype(I32)
             atom = jnp.sum(jnp.where(match, cols_ref[:, k : k + 1], 0.0), axis=0, keepdims=True)
-            taken = jnp.where(row == 4, atom, taken)
-            taken = jnp.where(row == 5, taken + F32(ATOM * (3 + k)), taken)
+            taken = jnp.where(row == 4, atom, taken + F32(ATOM * (3 + k)))
+        taken = jnp.where(row < 4, partner, taken)
         here = pl.ds(pl.multiple_of(tile * 128, 128), 128)
         spot = tile * 128 + lane
         inside = (spot >= at) & (spot < at + size)
         edges[:, here] = jnp.where(inside, taken, edges[:, here])
 
     def scalar(ref, which):
-        return ref[which : which + 1, PAIR : PAIR + 128][0, 0].astype(I32)
-
+        return ref[which : which + 1, 384:LIST][0, 0].astype(I32)
+
+    for k, ref in enumerate([recv_ref.at[k] for k in range(NBR)] + [home_ref]):
+        for i in range(PAIR // 128):
+            lines[k, i] = jnp.where(row == 4, ref[i : i + 1, 0:128], ref[i : i + 1, 128:256])
     at = count
     jobs = []
-    size = scalar(own_ref, 4)
-    jobs.append((own_ref, size, 0, at, None, 4))
+    size = scalar(home_ref, 4)
+    jobs.append((home_ref, size, 0, at, None, kept(home_ref), 4))
     at = at + size
     for k in range(NBR):
         ref = recv_ref.at[k]
         size = scalar(ref, 4)
-        jobs.append((ref, size, scalar(ref, 5), at, k, 2))
+        jobs.append((ref, size, scalar(ref, 5), at, k, kept(ref), 2))
         at = at + size
     total = at
-    for ref, size, begin, at, k, usual in jobs:
+    for ref, size, begin, at, k, held, usual in jobs:
         for step in range(usual):
-            place(ref, size, begin, at, k, (at >> 7) + step)
-    for ref, size, begin, at, k, usual in jobs:
+            place(ref, size, begin, at, k, held, (at >> 7) + step)
+    for ref, size, begin, at, k, held, usual in jobs:
         last = (at + size + 127) >> 7
 
-        def more(tile, carry, ref=ref, size=size, begin=begin, at=at, k=k):
-            place(ref, size, begin, at, k, tile)
+        def more(tile, carry, ref=ref, size=size, begin=begin, at=at, k=k, held=held):
+            place(ref, size, begin, at, k, held, tile)
             return carry
 
         lax.fori_loop((at >> 7) + usual, last, more, 0)
@@ -392,7 +416,7 @@
     at_partner[...] = jnp.zeros_like(at_partner)
 
     def first_pass(store, begin, width, offset):
-        hots, slope, _, _, _, raw, geo, value, base = store
+        hots, slope, _, _, value, raw, geo, base = store
         here = pl.ds(begin, width)
         valid = begin + offset + lax.broadcasted_iota(I32, (1, width), 1) < total
         part = jnp.where(valid, edges[:, pl.ds(begin + offset, width)], 0.0)
@@ -467,7 +491,7 @@
         scatter(terms, hot, env, FIELD)
 
     def second_pass(store, begin, width):
-        hots, _, mixed, mixed_low, d_value, _, geo, value, base = store
+        hots, _, mixed, mixed_low, value, _, geo, base = store
         here = pl.ds(begin, width)
         hot = hots[:, here]
         gather(fields, hot, around)
@@ -495,7 +519,7 @@
         mixed_low[:, here] = d_low
         d_inv = dot(mb_ref[...], jnp.concatenate([d_high, d_low, d_high], axis=0))
         d_inv = [d_inv[i * CH : (i + 1) * CH] for i in range(3)]
-        d_value[:, here] = d_inv[0] * sums[0] + d_inv[1] * sums[1] + d_inv[2] * sums[2]
+        value[:, here] = d_inv[0] * sums[0] + d_inv[1] * sums[1] + d_inv[2] * sums[2]
         d_sum = [d * held for d in d_inv]
         for m in range(9):
             share = d_sum[DEGREES[m]]
@@ -535,7 +559,7 @@
 
 
 def return_kernel(
-    own_ref, dn_ref, wr_ref, ab_ref,
+    dn_ref, wr_ref, ab_ref,
     fields, more_centre, more_partner, hots, slope, mixed, mixed_low, d_value, raw, geo,
     out_ref, outbox, inbox, around, at_centre, at_partner, send_sem, recv_sem,
 ):
@@ -546,28 +570,25 @@
     pull = third_pass(store, 0, MAIN, fields, around, dn_ref, wr_ref, ab_ref)
     to_partners(pull, geo, 0, MAIN, at_partner)
     parts = at_partner[...]
-    outbox[...] = jnp.zeros_like(outbox)
     for k in range(NBR):
         for i in range(3):
-            outbox[k, i : i + 1, :] = parts[16 * i + 3 + k : 16 * i + 4 + k]
-            ghost = parts[16 * i + 1 + k // 4 : 16 * i + 2 + k // 4]
-            outbox[k, 3 + i : 4 + i, 0:GHOST] = ghost[:, (k % 4) * GHOST : (k % 4 + 1) * GHOST]
+            for half in range(2):
+                outbox[k, 3 * half + i : 3 * half + i + 1, :] = parts[
+                    16 * i + 3 + k : 16 * i + 4 + k, half * 128 : (half + 1) * 128
+                ]
+        outbox[k, 6:8, :] = jnp.zeros((2, 128), F32)
     pl.semaphore_wait(barrier, NBR)
     copies = swap(peers, outbox, inbox, send_sem, recv_sem)
     to_centres(pull, hots, 0, MAIN, at_centre)
-    sends = own_ref[10:11, 0:SLOTS].astype(I32)
-    hot = one_hot(sends, ATOM)
     sums = at_centre[...]
     total = sums[0:3] + sums[8:11]
     total = total - jnp.concatenate([parts[16 * i : 16 * i + 1] for i in range(3)], axis=0)
     for copy in copies:
         copy.wait()
-    for k in range(NBR):
-        total = total - inbox[k, 0:3, :]
-    ghosts = jnp.concatenate([inbox[k, 3:6, 0:GHOST] for k in range(NBR)], axis=1)
-    split = jnp.concatenate([*thirds(ghosts), jnp.zeros((7, SLOTS), F32)], axis=0).astype(BF16)
-    back = dot_nt(split, hot)
-    out_ref[...] = total - joined(back)
+    arrived = inbox[0]
+    for k in range(1, NBR):
+        arrived = arrived + inbox[k]
+    out_ref[...] = total - jnp.concatenate([arrived[0:3], arrived[3:6]], axis=1)
 
 
 def edge_call(*operands):
@@ -594,19 +615,18 @@
             shape((48, ATOM), F32),
             *store(MAIN, shape),
         ),
-        in_specs=[VMEM] * 11,
+        in_specs=[VMEM] * 12,
         out_specs=[VMEM] * 11,
         scratch_shapes=[
             pltpu.VMEM((8, CAP + 512), F32),
-            pltpu.VMEM((CH, MAIN), F32),
             pltpu.VMEM((WIDTH, MAIN), F32),
             *store(rest, pltpu.VMEM),
-            pltpu.VMEM((CH, rest), F32),
             pltpu.VMEM((WIDTH, rest), F32),
             pltpu.VMEM((FIELD, ATOM), F32),
             pltpu.VMEM((FIELD + 16, ATOM), F32),
             pltpu.VMEM((FIELD + 16, 2 * MAIN), BF16),
             pltpu.VMEM((FIELD, MAIN), F32),
+            pltpu.VMEM((NBR + 1, PAIR // 128, 8, 128), F32),
         ],
         compiler_params=pltpu.CompilerParams(vmem_limit_bytes=46 << 20),
     )(*operands)
@@ -621,7 +641,7 @@
     shared = pl.pallas_call(
         share_kernel,
         out_shape=(
-            shape((16, LIST), F32),
+            shape((8, PAIR), F32),
             shape((16, ATOM), BF16),
             shape((NBR, 8, LIST), F32),
             shape((WIDTH, 64), BF16),
@@ -632,9 +652,10 @@
             shape((16, 3 * WIDTH), BF16),
             shape((WIDTH, 2), F32),
             shape((GHOST, NBR), F32),
+            shape((8, LIST), F32),
         ),
         in_specs=[SMEM] + [HBM] * 11,
-        out_specs=[VMEM] * 11,
+        out_specs=[VMEM] * 12,
         scratch_shapes=[
             pltpu.VMEM((3, ATOM), F32),
             pltpu.VMEM((1, ATOM), I32),
@@ -648,7 +669,7 @@
             pltpu.VMEM((WIDTH, WIDTH), F32),
             pltpu.VMEM((1, WIDTH), F32),
             pltpu.VMEM((NBR, 8, LIST), F32),
-            pltpu.VMEM((16, PAIR), F32),
+            pltpu.VMEM((8, 384), F32),
             pltpu.SemaphoreType.DMA((11,)),
             pltpu.SemaphoreType.DMA((NBR,)),
             pltpu.SemaphoreType.DMA((NBR,)),
@@ -667,15 +688,15 @@
         ),
     )
     energy, *kept = edge_call(*shared)
-    own, dn, wr, ab = shared[0], shared[5], shared[8], shared[9]
+    dn, wr, ab = shared[5], shared[8], shared[9]
     forces = pl.pallas_call(
         return_kernel,
         out_shape=shape((3, ATOM), F32),
-        in_specs=[VMEM] * 14,
+        in_specs=[VMEM] * 13,
         out_specs=VMEM,
         scratch_shapes=[
-            pltpu.VMEM((NBR, 8, ATOM), F32),
-            pltpu.VMEM((NBR, 8, ATOM), F32),
+            pltpu.VMEM((NBR, 8, 128), F32),
+            pltpu.VMEM((NBR, 8, 128), F32),
             pltpu.VMEM((FIELD, MAIN), F32),
             pltpu.VMEM((16, ATOM), F32),
             pltpu.VMEM((48, ATOM), F32),
@@ -685,7 +706,7 @@
         compiler_params=pltpu.CompilerParams(
             collective_id=1, has_side_effects=True, vmem_limit_bytes=20 << 20
         ),
-    )(own, dn, wr, ab, *kept)
+    )(dn, wr, ab, *kept)
     return forces, energy.reshape(ATOM)
 
 

time: 35.3 us -> 34.8 us (0.986)
  Pallas kernels: 33.3 us -> 32.8 us
    pallas_call x1, Pallas kernels: 15.5 us -> 14.6 us  [per_device(): pl.pallas_call(share_kernel, out_shape=(shape((8, PAIR), F32), shape((16,...]
    pallas_call x1, Pallas kernels: 9.26 us -> 9.66 us  [edge_call(): pl.pallas_call(edge_kernel, out_shape=(shape((1, ATOM), F32), shape((FIEL...]
where the time goes in v5:
time: 34.8 us; the launch traced here: 34.7 us
  Pallas kernels  32.8 us (94%)
  between operations  1.3 us (4%)
  local copies, waits for them, and re-layouts  0.6 us (2%)
    pallas_call x1, Pallas kernels, per_device(): pl.pallas_call(share_kernel, out_shape=(shape((8, PAIR), F32), shape((16,...  14.6 us
    pallas_call x1, Pallas kernels, edge_call(): pl.pallas_call(edge_kernel, out_shape=(shape((1, ATOM), F32), shape((FIEL...  9.66 us
    pallas_call x1, Pallas kernels, per_device(): pl.pallas_call(return_kernel, out_shape=shape((3, ATOM), F32), in_specs=[...  8.54 us

profile of v5, /device:TPU:1, one launch (start us, length us, event | category | flops | bytes accessed | tf_op | source)
XLA Modules:
  0.0 34.7 jit_solution(11270569294413194409)
XLA Ops:
  1.3 14.6 %shard_map.131 = (f32[8,1024]{1,0:T(8,128)S(1)}, bf16[16,256]{1,0:T(8,128)(2,1)S(1)}, f32[8,8,512]{2,1,0:T(8,128)S(1)}, bf16[128,64]{1,0:T(8,128)(2,1)S(1)}, bf1...) custom-call(s32[1]{0:T(128)S(6)} %copy.15.count_ref, ...), custom_call_target="tpu_custom_call" | custom-call | tf_op jit(solution)/shard_map/pallas_call | solution.py:641
  15.9 9.7 %shard_map.132 = (f32[1,256]{1,0:T(1,128)}, bf16[576,512]{1,0:T(8,128)(2,1)S(1)}, f32[16,256]{1,0:T(8,128)S(1)}, f32[48,256]{1,0:T(8,128)S(1)}, bf16[256,2048]{1...) custom-call(f32[8,1024]{1,0:T(8,128)S(1)} %get-tuple-element.28.own_, ...), custom_call_target="tpu_custom_call" | custom-call | tf_op jit(solution)/shard_map/pallas_call | solution.py:609
  25.6 8.5 %shard_map.133 = f32[3,256]{1,0:T(4,128)S(1)} custom-call(bf16[128,768]{1,0:T(8,128)(2,1)S(1)} %get-tuple-element.25.dn_ref, bf16[16,384]{1,0:T(8,128)(2,1)S(1)} %get-tuple-element.26.wr_ref, f32[128,2]{1,0:T(8,128)S(1)} %get-tuple-element.27.ab_ref, bf16[576,512]{1,0:T(8,128)(2,1)S(1)} %get-tuple-element.37.fields, ...), custom_call_target="tpu_custom_call" | custom-call | tf_op jit(solution)/shard_map/pallas_call | solution.py:692
  34.1 0.6 %copy.16 = f32[3,256]{1,0:T(4,128)} copy(f32[3,256]{1,0:T(4,128)S(1)} %shard_map.133) | data formatting | bytes 6144

commit v6 on v5

--- a/solution.py
+++ b/solution.py
@@ -77,8 +77,9 @@
 
 
 def one_hot(row, count):
-    rows = lax.broadcasted_iota(I32, (count, row.shape[1]), 0)
-    return jnp.where(rows == row, 1.0, 0.0).astype(BF16)
+    rows = lax.broadcasted_iota(I32, (count, row.shape[1]), 0).astype(F32).astype(BF16)
+    match = rows == row.astype(F32).astype(BF16)
+    return jnp.where(match, jnp.ones_like(rows), jnp.zeros_like(rows))
 
 
 def atom_table(coords, kinds):
@@ -252,16 +253,13 @@
 
 def gather(fields, hot, around):
     width = hot.shape[1]
-    both = jnp.concatenate([hot, hot], axis=0)
-    for lo, hi in ((0, 288), (288, FIELD)):
-        around[lo:hi, 0:width] = dot(fields[lo:hi, :], both)
+    around[:, 0:width] = dot(fields[...], jnp.concatenate([hot, hot], axis=0))
 
 
 def scatter(terms, hot, total, count):
     width = hot.shape[1]
-    both = jnp.concatenate([hot, hot], axis=1)
-    for lo, hi in ((0, 288), (288, count)):
-        total[lo:hi, :] += dot_nt(terms[lo:hi, 0 : 2 * width], both)
+    for part in (slice(0, width), slice(width, 2 * width)):
+        total[0:count, :] += dot_nt(terms[0:count, part], hot)
 
 
 def third_pass(store, begin, width, fields, around, dn_ref, wr_ref, ab_ref):
@@ -305,9 +303,8 @@
     seg = lax.broadcasted_iota(I32, (16, width), 0) == (code >> 8)
     high, low = halves(jnp.concatenate([jnp.where(seg, g, 0.0) for g in pull], axis=0))
     hot = one_hot(code & 255, ATOM)
-    at_partner[...] += dot_nt(
-        jnp.concatenate([high, low], axis=1), jnp.concatenate([hot, hot], axis=1)
-    )
+    sums = dot_nt(jnp.concatenate([high, low], axis=0), hot)
+    at_partner[...] += sums[0:48] + sums[48:96]
 
 
 def to_centres(pull, hots, begin, width, at_centre):

time: 34.8 us -> 34.3 us (0.986)
  Pallas kernels: 32.8 us -> 32.3 us
where the time goes in v6:
time: 34.3 us; the launch traced here: 34.1 us
  Pallas kernels  32.3 us (94%)
  between operations  1.3 us (4%)
  local copies, waits for them, and re-layouts  0.6 us (2%)
    pallas_call x1, Pallas kernels, per_device(): pl.pallas_call(share_kernel, out_shape=(shape((8, PAIR), F32), shape((16,...  14.6 us
    pallas_call x1, Pallas kernels, edge_call(): pl.pallas_call(edge_kernel, out_shape=(shape((1, ATOM), F32), shape((FIEL...  9.4 us
    pallas_call x1, Pallas kernels, per_device(): pl.pallas_call(return_kernel, out_shape=shape((3, ATOM), F32), in_specs=[...  8.25 us

profile of v6, /device:TPU:1, one launch (start us, length us, event | category | flops | bytes accessed | tf_op | source)
XLA Modules:
  0.0 34.1 jit_solution(9233054594704856037)
XLA Ops:
  1.3 14.6 %shard_map.131 = (f32[8,1024]{1,0:T(8,128)S(1)}, bf16[16,256]{1,0:T(8,128)(2,1)S(1)}, f32[8,8,512]{2,1,0:T(8,128)S(1)}, bf16[128,64]{1,0:T(8,128)(2,1)S(1)}, bf1...) custom-call(s32[1]{0:T(128)S(6)} %copy.15.count_ref, ...), custom_call_target="tpu_custom_call" | custom-call | tf_op jit(solution)/shard_map/pallas_call | solution.py:638
  15.9 9.4 %shard_map.132 = (f32[1,256]{1,0:T(1,128)}, bf16[576,512]{1,0:T(8,128)(2,1)S(1)}, f32[16,256]{1,0:T(8,128)S(1)}, f32[48,256]{1,0:T(8,128)S(1)}, bf16[256,2048]{1...) custom-call(f32[8,1024]{1,0:T(8,128)S(1)} %get-tuple-element.28.own_, ...), custom_call_target="tpu_custom_call" | custom-call | tf_op jit(solution)/shard_map/pallas_call | solution.py:606
  25.3 8.3 %shard_map.133 = f32[3,256]{1,0:T(4,128)S(1)} custom-call(bf16[128,768]{1,0:T(8,128)(2,1)S(1)} %get-tuple-element.25.dn_ref, bf16[16,384]{1,0:T(8,128)(2,1)S(1)} %get-tuple-element.26.wr_ref, f32[128,2]{1,0:T(8,128)S(1)} %get-tuple-element.27.ab_ref, bf16[576,512]{1,0:T(8,128)(2,1)S(1)} %get-tuple-element.37.fields, ...), custom_call_target="tpu_custom_call" | custom-call | tf_op jit(solution)/shard_map/pallas_call | solution.py:689
  33.6 0.6 %copy.16 = f32[3,256]{1,0:T(4,128)} copy(f32[3,256]{1,0:T(4,128)S(1)} %shard_map.133) | data formatting | bytes 6144

commit v7 on v6

--- a/solution.py
+++ b/solution.py
@@ -23,6 +23,7 @@
 LIST = 512
 CAP = 10 * PAIR
 MAIN = 2048
+LATE = 768
 EXTRA = 512
 F32 = jnp.float32
 BF16 = jnp.bfloat16
@@ -130,10 +131,10 @@
     sources, refs = refs[:11], refs[11:]
     (
         own_ref, table_ref, recv_ref, wx_ref, up_ref, dn_ref, mt_ref, mb_ref, wr_ref, ab_ref, cols_ref,
-        home_ref,
-    ) = refs[:12]
-    held, refs = refs[12:23], refs[23:]
-    out_buf, order_buf, load_sem, send_sem, recv_sem = refs
+        home_ref, hots_ref, slope_ref, value_ref, raw_ref, geo_ref, base_ref, env_ref,
+    ) = refs[:19]
+    held, refs = refs[19:30], refs[30:]
+    out_buf, order_buf, terms, load_sem, send_sem, recv_sem = refs
     (
         pos_ref, spec_ref, send_ref, src_ref, dst_ref,
         w_in_ref, w_mid_ref, w_pair_ref, w_mix_ref, w_back_ref, w_read_ref,
@@ -181,12 +182,19 @@
     spot = jnp.concatenate(spots, axis=1)
     spot = jnp.where(live, spot, -1.0).astype(I32)
     data = jnp.concatenate(
-        [place.astype(F32), src.astype(F32), jnp.zeros((14, PAIR), F32)], axis=0
+        [
+            place.astype(F32), src.astype(F32), (dst >> 8).astype(F32), (dst & 255).astype(F32),
+            jnp.zeros((12, PAIR), F32),
+        ],
+        axis=0,
     ).astype(BF16)
     for i in range(PAIR // ATOM):
         rows = lax.broadcasted_iota(I32, (ATOM, PAIR), 0) + i * ATOM
         chosen = jnp.where(rows == spot, 1.0, 0.0).astype(BF16)
         ordered = dot_nt(data, chosen)
+        span = slice(i * ATOM, (i + 1) * ATOM)
+        own_ref[0:1, span] = ordered[1:2]
+        own_ref[1:2, span] = ordered[2:3] * ATOM + ordered[3:4]
         for j in range(2):
             for half in range(2):
                 order_buf[2 * i + half : 2 * i + half + 1, j * 128 : (j + 1) * 128] = ordered[
@@ -213,8 +221,6 @@
     home_ref[:, 0:384] = entries
     home_ref[:, 384:LIST] = jnp.zeros((8, 128), F32)
     home_ref[4:5, 384:LIST] = jnp.broadcast_to(total[0:1, :], (1, 128))
-    own_ref[0:1, :] = src.astype(F32)
-    own_ref[1:2, :] = dst.astype(F32)
     own_ref[2:3, :] = jnp.full((1, PAIR), count_ref[0], I32).astype(F32)
     cols_ref[...] = send_ref[...].astype(F32).T
     for load in loads[5:]:
@@ -247,6 +253,19 @@
     )
     mb_ref[...] = triple(mix)
     mt_ref[...] = triple(mix.T)
+    half = LATE // 2
+    ends = [own_ref[i : i + 1, 0:half] for i in range(2)]
+    centre = jnp.concatenate(ends, axis=1)
+    mate = jnp.concatenate(ends[::-1], axis=1)
+    found = dot(table, one_hot(mate.astype(I32), ATOM))
+    partner = jnp.concatenate([joined(found), found[9:10]], axis=0)
+    index = lax.broadcasted_iota(I32, (1, half), 1).astype(F32)
+    valid = jnp.concatenate([index, index], axis=1) < total[0:1, :]
+    env_ref[...] = jnp.zeros_like(env_ref)
+    store = (hots_ref, slope_ref, None, None, value_ref, raw_ref, geo_ref, base_ref)
+    first_pass(
+        centre.astype(I32), partner, mate, valid, table, store, 0, terms, env_ref, wx_ref, up_ref, ab_ref
+    )
     for copy in copies:
         copy.wait()
 
@@ -260,6 +279,81 @@
     width = hot.shape[1]
     for part in (slice(0, width), slice(width, 2 * width)):
         total[0:count, :] += dot_nt(terms[0:count, part], hot)
+
+
+def first_pass(centre, partner, code, valid, table, store, begin, terms, env, wx_ref, up_ref, ab_ref):
+    hots, slope, _, _, value, raw, geo, base = store
+    width = centre.shape[1]
+    here = pl.ds(begin, width)
+    hot = one_hot(centre, ATOM)
+    hots[:, here] = hot
+    geo[CODE : CODE + 1, here] = code
+    held = dot(table, hot)
+    delta = partner[0:3] - joined(held)
+    length2 = delta[0:1] * delta[0:1] + delta[1:2] * delta[1:2] + delta[2:3] * delta[2:3] + 1.0
+    soft = jnp.sqrt(length2)
+    rinv = 1.0 / soft
+    unit = delta * rinv
+    ux, uy, uz = unit[0:1], unit[1:2], unit[2:3]
+    turn = soft * (PI / CUTOFF) - PI / 2
+    t2 = turn * turn
+    cosine = -turn * (
+        1 + t2 * (-1 / 6 + t2 * (1 / 120 + t2 * (-1 / 5040 + t2 * (1 / 362880 - t2 / 39916800))))
+    )
+    sine = 1 + t2 * (
+        -1 / 2 + t2 * (1 / 24 + t2 * (-1 / 720 + t2 * (1 / 40320 + t2 * (-1 / 3628800 + t2 / 479001600))))
+    )
+    twice = 2 * cosine
+    s_old, s_now = jnp.zeros_like(sine), sine
+    c_old, c_now = jnp.ones_like(sine), cosine
+    for b in range(BASIS):
+        geo[RAD + b : RAD + b + 1, here] = s_now * rinv
+        geo[DRAD + b : DRAD + b + 1, here] = (c_now * ((b + 1) * PI / CUTOFF) - s_now * rinv) * rinv
+        s_old, s_now = s_now, twice * s_now - s_old
+        c_old, c_now = c_now, twice * c_now - c_old
+    angular = [
+        jnp.ones_like(ux),
+        ROOT3 * ux,
+        ROOT3 * uy,
+        ROOT3 * uz,
+        ROOT15 * ux * uy,
+        ROOT15 * uy * uz,
+        0.5 * ROOT5 * (2.0 * uz * uz - ux * ux - uy * uy),
+        ROOT15 * ux * uz,
+        0.5 * ROOT15 * (ux * ux - uy * uy),
+    ]
+    for m in range(9):
+        geo[ANG + m : ANG + m + 1, here] = angular[m]
+    inner = 1.0 - length2 * (1.0 / (CUTOFF * CUTOFF))
+    alive = jnp.where(valid, 1.0, 0.0)
+    envelope = alive * inner * inner
+    geo[ENVL : ENVL + 1, here] = envelope
+    geo[DENVL : DENVL + 1, here] = alive * inner * soft * (-4.0 / (CUTOFF * CUTOFF))
+    geo[RINV : RINV + 1, here] = rinv
+    geo[DIR : DIR + 3, here] = unit
+    radial = geo[RAD : RAD + 8, here]
+    radial_low = radial - radial.astype(BF16).astype(F32)
+    kinds = lax.broadcasted_iota(I32, (8, width), 0)
+    hot_c = jnp.where(kinds == held[9:10].astype(I32), 1.0, 0.0)
+    hot_p = jnp.where(kinds == partner[3:4].astype(I32), 1.0, 0.0)
+    inputs = jnp.concatenate(
+        [hot_c, hot_p, radial, radial_low, hot_c, hot_p, radial, jnp.zeros((8, width), F32)], axis=0
+    ).astype(BF16)
+    pre = dot(wx_ref[...], inputs)
+    gate = sigmoid(pre)
+    act = pre * gate
+    slope[:, here] = gate + act * (1.0 - gate)
+    after = dot(up_ref[...], stacked(act))
+    raw[:, here] = after[0:CH]
+    value[:, here] = after[CH : 2 * CH]
+    base[:, here] = after[2 * CH :]
+    geo[ERAW : ERAW + 1, here] = jnp.sum(act * ab_ref[:, 0:1], axis=0, keepdims=True)
+    weights = after[0:CH] * envelope
+    for m in range(9):
+        term = weights if m == 0 else weights * angular[m]
+        rows = slice(m * CH, (m + 1) * CH)
+        terms[rows, 0:width], terms[rows, width : 2 * width] = halves(term)
+    scatter(terms, hot, env, FIELD)
 
 
 def third_pass(store, begin, width, fields, around, dn_ref, wr_ref, ab_ref):
@@ -307,18 +401,19 @@
     at_partner[...] += sums[0:48] + sums[48:96]
 
 
-def to_centres(pull, hots, begin, width, at_centre):
-    sent = jnp.concatenate([*pull, jnp.zeros((5, width), F32)], axis=0)
+def settled(pull, hot):
+    sent = jnp.concatenate([*pull, jnp.zeros((5, hot.shape[1]), F32)], axis=0)
     sent = jnp.concatenate([sent, sent - sent.astype(BF16).astype(F32)], axis=0).astype(BF16)
-    at_centre[...] += dot_nt(sent, hots[:, pl.ds(begin, width)])
+    return dot_nt(sent, hot)
 
 
 def edge_kernel(
     own_ref, table_ref, recv_ref,
     wx_ref, up_ref, dn_ref, mt_ref, mb_ref, wr_ref, ab_ref, cols_ref, home_ref,
+    late_hots, late_slope, late_value, late_raw, late_geo, late_base, late_env,
     energy_ref, fields, at_centre, at_partner, hots, slope, mixed, mixed_low, d_value, raw, geo,
     edges, base, more_hots, more_slope, more_mixed, more_low, more_d_value, more_raw, more_geo,
-    more_base, env, g_env, terms, around, lines,
+    more_base, env, g_env, terms, around, lines, forward,
 ):
     first_store = (hots, slope, mixed, mixed_low, d_value, raw, geo, base)
     more_store = (
@@ -339,7 +434,7 @@
     picked = jnp.where(part == 0, found[0:16], jnp.where(part == 1, found[16:32], found[32:48]))
     beyond = (((dst - ATOM) >> 6) + 3).astype(F32) * ATOM + picked[10:11]
     code = jnp.where(part == 0, dst.astype(F32), beyond)
-    edges[:, 0:PAIR] = jnp.concatenate(
+    forward[...] = jnp.concatenate(
         [joined(picked), picked[9:10], src, code, jnp.zeros((2, PAIR), F32)], axis=0
     )
     lane = lax.broadcasted_iota(I32, (8, 128), 1)
@@ -352,25 +447,29 @@
         ]
         return atom_table(jnp.concatenate(halves_of[0:3], axis=0), halves_of[3]).astype(BF16)
 
-    def place(ref, size, begin, at, k, held, tile):
+    def place(size, begin, at, k, held, tile):
         base = tile * 128 - at + begin
         first = base >> 7
         turn = base & 127
         low = jnp.clip(first, 0, 7)
         high = jnp.clip(first + 1, 0, 7)
-        which = NBR if k is None else k
-        left, right = lines[which, low], lines[which, high]
+        if k is None:
+            left, right = [forward[:, pl.ds(pl.multiple_of(i * 128, 128), 128)] for i in (low, high)]
+        else:
+            left, right = lines[k, low], lines[k, high]
         back = lax.rem(128 - turn, 128)
         taken = jnp.where(
             lane < 128 - turn, pltpu.roll(left, back, 1), pltpu.roll(right, back, 1)
         )
-        found = dot(held, one_hot(taken[5:6].astype(I32), ATOM))
-        partner = jnp.concatenate([joined(found), found[9:10], jnp.zeros((4, 128), F32)], axis=0)
         if k is not None:
+            found = dot(held, one_hot(taken[5:6].astype(I32), ATOM))
+            partner = jnp.concatenate([joined(found), found[9:10], jnp.zeros((4, 128), F32)], axis=0)
+        if k is not None and k < NBR:
             match = lax.broadcasted_iota(I32, (GHOST, 128), 0) == taken[4:5].astype(I32)
             atom = jnp.sum(jnp.where(match, cols_ref[:, k : k + 1], 0.0), axis=0, keepdims=True)
             taken = jnp.where(row == 4, atom, taken + F32(ATOM * (3 + k)))
-        taken = jnp.where(row < 4, partner, taken)
+        if k is not None:
+            taken = jnp.where(row < 4, partner, taken)
         here = pl.ds(pl.multiple_of(tile * 128, 128), 128)
         spot = tile * 128 + lane
         inside = (spot >= at) & (spot < at + size)
@@ -382,110 +481,42 @@
     for k, ref in enumerate([recv_ref.at[k] for k in range(NBR)] + [home_ref]):
         for i in range(PAIR // 128):
             lines[k, i] = jnp.where(row == 4, ref[i : i + 1, 0:128], ref[i : i + 1, 128:256])
-    at = count
-    jobs = []
-    size = scalar(home_ref, 4)
-    jobs.append((home_ref, size, 0, at, None, kept(home_ref), 4))
+    inner = scalar(home_ref, 4)
+    early = jnp.minimum(inner, LATE // 2)
+    jobs = [(count - early, early, jnp.int32(0), None, None, PAIR // 128)]
+    at = count - early
+    size = inner - early
+    jobs.append((size, LATE // 2, at, NBR, kept(home_ref), 0))
     at = at + size
     for k in range(NBR):
         ref = recv_ref.at[k]
         size = scalar(ref, 4)
-        jobs.append((ref, size, scalar(ref, 5), at, k, kept(ref), 2))
+        jobs.append((size, scalar(ref, 5), at, k, kept(ref), 2))
         at = at + size
     total = at
-    for ref, size, begin, at, k, held, usual in jobs:
+    for size, begin, at, k, held, usual in jobs:
         for step in range(usual):
-            place(ref, size, begin, at, k, held, (at >> 7) + step)
-    for ref, size, begin, at, k, held, usual in jobs:
+            place(size, begin, at, k, held, (at >> 7) + step)
+    for size, begin, at, k, held, usual in jobs:
         last = (at + size + 127) >> 7
 
-        def more(tile, carry, ref=ref, size=size, begin=begin, at=at, k=k, held=held):
-            place(ref, size, begin, at, k, held, tile)
+        def more(tile, carry, size=size, begin=begin, at=at, k=k, held=held):
+            place(size, begin, at, k, held, tile)
             return carry
 
         lax.fori_loop((at >> 7) + usual, last, more, 0)
-    extra_blocks = lax.div(jnp.maximum(total - MAIN, 0) + EXTRA - 1, EXTRA)
-
-    env[...] = jnp.zeros_like(env)
+    extra_blocks = lax.div(jnp.maximum(total - (MAIN - LATE), 0) + EXTRA - 1, EXTRA)
+
+    for target, source in zip(
+        (hots, slope, d_value, raw, geo, base),
+        (late_hots, late_slope, late_value, late_raw, late_geo, late_base),
+    ):
+        target[:, 0:LATE] = source[...]
+    env[...] = late_env[...]
     g_env[...] = jnp.zeros_like(g_env)
     terms[FIELD:, :] = jnp.zeros((16, 2 * MAIN), BF16)
     at_centre[...] = jnp.zeros_like(at_centre)
     at_partner[...] = jnp.zeros_like(at_partner)
-
-    def first_pass(store, begin, width, offset):
-        hots, slope, _, _, value, raw, geo, base = store
-        here = pl.ds(begin, width)
-        valid = begin + offset + lax.broadcasted_iota(I32, (1, width), 1) < total
-        part = jnp.where(valid, edges[:, pl.ds(begin + offset, width)], 0.0)
-        hot = one_hot(part[4:5].astype(I32), ATOM)
-        hots[:, here] = hot
-        geo[CODE : CODE + 1, here] = part[5:6]
-        held = dot(table, hot)
-        delta = part[0:3] - joined(held)
-        length2 = delta[0:1] * delta[0:1] + delta[1:2] * delta[1:2] + delta[2:3] * delta[2:3] + 1.0
-        soft = jnp.sqrt(length2)
-        rinv = 1.0 / soft
-        unit = delta * rinv
-        ux, uy, uz = unit[0:1], unit[1:2], unit[2:3]
-        turn = soft * (PI / CUTOFF) - PI / 2
-        t2 = turn * turn
-        cosine = -turn * (
-            1 + t2 * (-1 / 6 + t2 * (1 / 120 + t2 * (-1 / 5040 + t2 * (1 / 362880 - t2 / 39916800))))
-        )
-        sine = 1 + t2 * (
-            -1 / 2 + t2 * (1 / 24 + t2 * (-1 / 720 + t2 * (1 / 40320 + t2 * (-1 / 3628800 + t2 / 479001600))))
-        )
-        twice = 2 * cosine
-        s_old, s_now = jnp.zeros_like(sine), sine
-        c_old, c_now = jnp.ones_like(sine), cosine
-        for b in range(BASIS):
-            geo[RAD + b : RAD + b + 1, here] = s_now * rinv
-            geo[DRAD + b : DRAD + b + 1, here] = (c_now * ((b + 1) * PI / CUTOFF) - s_now * rinv) * rinv
-            s_old, s_now = s_now, twice * s_now - s_old
-            c_old, c_now = c_now, twice * c_now - c_old
-        angular = [
-            jnp.ones_like(ux),
-            ROOT3 * ux,
-            ROOT3 * uy,
-            ROOT3 * uz,
-            ROOT15 * ux * uy,
-            ROOT15 * uy * uz,
-            0.5 * ROOT5 * (2.0 * uz * uz - ux * ux - uy * uy),
-            ROOT15 * ux * uz,
-            0.5 * ROOT15 * (ux * ux - uy * uy),
-        ]
-        for m in range(9):
-            geo[ANG + m : ANG + m + 1, here] = angular[m]
-        inner = 1.0 - length2 * (1.0 / (CUTOFF * CUTOFF))
-        alive = jnp.where(valid, 1.0, 0.0)
-        envelope = alive * inner * inner
-        geo[ENVL : ENVL + 1, here] = envelope
-        geo[DENVL : DENVL + 1, here] = alive * inner * soft * (-4.0 / (CUTOFF * CUTOFF))
-        geo[RINV : RINV + 1, here] = rinv
-        geo[DIR : DIR + 3, here] = unit
-        radial = geo[RAD : RAD + 8, here]
-        radial_low = radial - radial.astype(BF16).astype(F32)
-        kinds = lax.broadcasted_iota(I32, (8, width), 0)
-        hot_c = jnp.where(kinds == held[9:10].astype(I32), 1.0, 0.0)
-        hot_p = jnp.where(kinds == part[3:4].astype(I32), 1.0, 0.0)
-        inputs = jnp.concatenate(
-            [hot_c, hot_p, radial, radial_low, hot_c, hot_p, radial, jnp.zeros((8, width), F32)], axis=0
-        ).astype(BF16)
-        pre = dot(wx_ref[...], inputs)
-        gate = sigmoid(pre)
-        act = pre * gate
-        slope[:, here] = gate + act * (1.0 - gate)
-        after = dot(up_ref[...], stacked(act))
-        raw[:, here] = after[0:CH]
-        value[:, here] = after[CH : 2 * CH]
-        base[:, here] = after[2 * CH :]
-        geo[ERAW : ERAW + 1, here] = jnp.sum(act * ab_ref[:, 0:1], axis=0, keepdims=True)
-        weights = after[0:CH] * envelope
-        for m in range(9):
-            term = weights if m == 0 else weights * angular[m]
-            rows = slice(m * CH, (m + 1) * CH)
-            terms[rows, 0:width], terms[rows, width : 2 * width] = halves(term)
-        scatter(terms, hot, env, FIELD)
 
     def second_pass(store, begin, width):
         hots, _, mixed, mixed_low, value, _, geo, base = store
@@ -536,8 +567,16 @@
 
         lax.fori_loop(0, extra_blocks, body, 0)
 
-    first_pass(first_store, 0, MAIN, 0)
-    rest(lambda begin: first_pass(more_store, begin, EXTRA, MAIN))
+    def listed(store, begin, start, width):
+        valid = start + lax.broadcasted_iota(I32, (1, width), 1) < total
+        part = jnp.where(valid, edges[:, pl.ds(start, width)], 0.0)
+        first_pass(
+            part[4:5].astype(I32), part[0:4], part[5:6], valid, table, store, begin, terms, env,
+            wx_ref, up_ref, ab_ref,
+        )
+
+    listed(first_store, LATE, 0, MAIN - LATE)
+    rest(lambda begin: listed(more_store, begin, pl.multiple_of(begin + (MAIN - LATE), 256), EXTRA))
     fields[:, 0:ATOM], fields[:, ATOM:] = halves(env[...] * ENV_SCALE)
     second_pass(first_store, 0, MAIN)
     rest(lambda begin: second_pass(more_store, begin, EXTRA))
@@ -550,7 +589,7 @@
             begin, EXTRA, fields, around, dn_ref, wr_ref, ab_ref,
         )
         to_partners(pull, more_geo, begin, EXTRA, at_partner)
-        to_centres(pull, more_hots, begin, EXTRA, at_centre)
+        at_centre[...] += settled(pull, more_hots[:, pl.ds(begin, EXTRA)])
 
     rest(third)
 
@@ -558,14 +597,14 @@
 def return_kernel(
     dn_ref, wr_ref, ab_ref,
     fields, more_centre, more_partner, hots, slope, mixed, mixed_low, d_value, raw, geo,
-    out_ref, outbox, inbox, around, at_centre, at_partner, send_sem, recv_sem,
+    out_ref, outbox, inbox, around, at_partner, send_sem, recv_sem,
 ):
     barrier, peers = greet()
-    at_centre[...] = more_centre[...]
     at_partner[...] = more_partner[...]
     store = (hots, slope, mixed, mixed_low, d_value, raw, geo)
-    pull = third_pass(store, 0, MAIN, fields, around, dn_ref, wr_ref, ab_ref)
-    to_partners(pull, geo, 0, MAIN, at_partner)
+    weights = (fields, around, dn_ref, wr_ref, ab_ref)
+    pull = third_pass(store, LATE, MAIN - LATE, *weights)
+    to_partners(pull, geo, LATE, MAIN - LATE, at_partner)
     parts = at_partner[...]
     for k in range(NBR):
         for i in range(3):
@@ -576,8 +615,10 @@
         outbox[k, 6:8, :] = jnp.zeros((2, 128), F32)
     pl.semaphore_wait(barrier, NBR)
     copies = swap(peers, outbox, inbox, send_sem, recv_sem)
-    to_centres(pull, hots, 0, MAIN, at_centre)
-    sums = at_centre[...]
+    sums = more_centre[...] + settled(pull, hots[:, LATE:MAIN])
+    pull = third_pass(store, 0, LATE, *weights)
+    mates = one_hot(geo[CODE : CODE + 1, 0:LATE].astype(I32), ATOM)
+    sums = sums + settled(pull, hots[:, 0:LATE]) - settled(pull, mates)
     total = sums[0:3] + sums[8:11]
     total = total - jnp.concatenate([parts[16 * i : 16 * i + 1] for i in range(3)], axis=0)
     for copy in copies:
@@ -590,7 +631,7 @@
 
 def edge_call(*operands):
     shape = jax.ShapeDtypeStruct
-    rest = CAP - MAIN
+    rest = NBR * PAIR
 
     def store(lanes, make):
         return [
@@ -612,7 +653,7 @@
             shape((48, ATOM), F32),
             *store(MAIN, shape),
         ),
-        in_specs=[VMEM] * 12,
+        in_specs=[VMEM] * 19,
         out_specs=[VMEM] * 11,
         scratch_shapes=[
             pltpu.VMEM((8, CAP + 512), F32),
@@ -624,8 +665,9 @@
             pltpu.VMEM((FIELD + 16, 2 * MAIN), BF16),
             pltpu.VMEM((FIELD, MAIN), F32),
             pltpu.VMEM((NBR + 1, PAIR // 128, 8, 128), F32),
+            pltpu.VMEM((8, PAIR), F32),
         ],
-        compiler_params=pltpu.CompilerParams(vmem_limit_bytes=46 << 20),
+        compiler_params=pltpu.CompilerParams(vmem_limit_bytes=43 << 20),
     )(*operands)
 
 
@@ -650,9 +692,16 @@
             shape((WIDTH, 2), F32),
             shape((GHOST, NBR), F32),
             shape((8, LIST), F32),
+            shape((ATOM, LATE), BF16),
+            shape((WIDTH, LATE), F32),
+            shape((CH, LATE), F32),
+            shape((CH, LATE), F32),
+            shape((ROWS, LATE), F32),
+            shape((WIDTH, LATE), F32),
+            shape((FIELD, ATOM), F32),
         ),
         in_specs=[SMEM] + [HBM] * 11,
-        out_specs=[VMEM] * 12,
+        out_specs=[VMEM] * 19,
         scratch_shapes=[
             pltpu.VMEM((3, ATOM), F32),
             pltpu.VMEM((1, ATOM), I32),
@@ -667,12 +716,13 @@
             pltpu.VMEM((1, WIDTH), F32),
             pltpu.VMEM((NBR, 8, LIST), F32),
             pltpu.VMEM((8, 384), F32),
+            pltpu.VMEM((FIELD, 2 * LATE), BF16),
             pltpu.SemaphoreType.DMA((11,)),
             pltpu.SemaphoreType.DMA((NBR,)),
             pltpu.SemaphoreType.DMA((NBR,)),
         ],
         compiler_params=pltpu.CompilerParams(
-            collective_id=0, has_side_effects=True, vmem_limit_bytes=8 << 20
+            collective_id=0, has_side_effects=True, vmem_limit_bytes=14 << 20
         ),
     )(
         edge_count,
@@ -694,8 +744,7 @@
         scratch_shapes=[
             pltpu.VMEM((NBR, 8, 128), F32),
             pltpu.VMEM((NBR, 8, 128), F32),
-            pltpu.VMEM((FIELD, MAIN), F32),
-            pltpu.VMEM((16, ATOM), F32),
+            pltpu.VMEM((FIELD, MAIN - LATE), F32),
             pltpu.VMEM((48, ATOM), F32),
             pltpu.SemaphoreType.DMA((NBR,)),
             pltpu.SemaphoreType.DMA((NBR,)),

time: 34.3 us -> 33.8 us (0.985)
  Pallas kernels: 32.3 us -> 31.8 us
    pallas_call x1, Pallas kernels: 9.4 us -> 8.9 us  [edge_call(): pl.pallas_call(edge_kernel, out_shape=(shape((1, ATOM), F32), shape((FIEL...]
where the time goes in v7:
time: 33.8 us; the launch traced here: 33.7 us
  Pallas kernels  31.8 us (94%)
  between operations  1.3 us (4%)
  local copies, waits for them, and re-layouts  0.6 us (2%)
    pallas_call x1, Pallas kernels, per_device(): pl.pallas_call(share_kernel, out_shape=(shape((8, PAIR), F32), shape((16,...  14.6 us
    pallas_call x1, Pallas kernels, edge_call(): pl.pallas_call(edge_kernel, out_shape=(shape((1, ATOM), F32), shape((FIEL...  8.9 us
    pallas_call x1, Pallas kernels, per_device(): pl.pallas_call(return_kernel, out_shape=shape((3, ATOM), F32), in_specs=[...  8.24 us

profile of v7, /device:TPU:1, one launch (start us, length us, event | category | flops | bytes accessed | tf_op | source)
XLA Modules:
  0.0 33.7 jit_solution(17145654431659720167)
XLA Ops:
  1.3 14.6 %shard_map.131 = (f32[8,1024]{1,0:T(8,128)S(1)}, bf16[16,256]{1,0:T(8,128)(2,1)S(1)}, f32[8,8,512]{2,1,0:T(8,128)S(1)}, bf16[128,64]{1,0:T(8,128)(2,1)S(1)}, bf1...) custom-call(s32[1]{0:T(128)S(6)} %copy.15.count_ref, ...), custom_call_target="tpu_custom_call" | custom-call | tf_op jit(solution)/shard_map/pallas_call | solution.py:680
  15.9 8.9 %shard_map.132 = (f32[1,256]{1,0:T(1,128)}, bf16[576,512]{1,0:T(8,128)(2,1)S(1)}, f32[16,256]{1,0:T(8,128)S(1)}, f32[48,256]{1,0:T(8,128)S(1)}, bf16[256,2048]{1...) custom-call(f32[8,1024]{1,0:T(8,128)S(1)} %get-tuple-element.35.own_, ...), custom_call_target="tpu_custom_call" | custom-call | tf_op jit(solution)/shard_map/pallas_call | solution.py:647
  24.8 8.2 %shard_map.133 = f32[3,256]{1,0:T(4,128)S(1)} custom-call(bf16[128,768]{1,0:T(8,128)(2,1)S(1)} %get-tuple-element.32.dn_ref, bf16[16,384]{1,0:T(8,128)(2,1)S(1)} %get-tuple-element.33.wr_ref, f32[128,2]{1,0:T(8,128)S(1)} %get-tuple-element.34.ab_ref, bf16[576,512]{1,0:T(8,128)(2,1)S(1)} %get-tuple-element.51.fields, ...), custom_call_target="tpu_custom_call" | custom-call | tf_op jit(solution)/shard_map/pallas_call | solution.py:739
  33.1 0.6 %copy.16 = f32[3,256]{1,0:T(4,128)} copy(f32[3,256]{1,0:T(4,128)S(1)} %shard_map.133) | data formatting | bytes 6144

commit v8 on v7

--- a/solution.py
+++ b/solution.py
@@ -16,6 +16,7 @@
 PI = 3.141592653589793
 DIRECTIONS = ((-1, -1), (-1, 0), (-1, 1), (0, -1), (0, 1), (1, -1), (1, 0), (1, 1))
 NBR = 8
+FAR_FIRST = (0, 7, 2, 5, 3, 4, 1, 6)
 ATOM = 256
 GHOST = 64
 PAIR = 1024
@@ -102,8 +103,8 @@
             tuple(lax.rem(at + by + size, size) for at, by, size in zip(here, shift, sizes))
         )
     barrier = pltpu.get_barrier_semaphore()
-    for peer in peers:
-        pl.semaphore_signal(barrier, inc=1, device_id=peer, device_id_type=MESH)
+    for k in FAR_FIRST:
+        pl.semaphore_signal(barrier, inc=1, device_id=peers[k], device_id_type=MESH)
     return barrier, peers
 
 
@@ -120,8 +121,8 @@
                 device_id_type=MESH,
             )
         )
-    for copy in copies:
-        copy.start()
+    for k in FAR_FIRST:
+        copies[k].start()
     return copies
 
 
@@ -143,9 +144,9 @@
         pltpu.make_async_copy(source, target, load_sem.at[i])
         for i, (source, target) in enumerate(zip(sources, held))
     ]
+    barrier, peers = greet()
     for load in loads:
         load.start()
-    barrier, peers = greet()
     for load in loads[:5]:
         load.wait()
     table = atom_table(pos_ref[...], spec_ref[...].astype(F32)).astype(BF16)
@@ -447,7 +448,7 @@
         ]
         return atom_table(jnp.concatenate(halves_of[0:3], axis=0), halves_of[3]).astype(BF16)
 
-    def place(size, begin, at, k, held, tile):
+    def place(size, begin, at, k, held, tile, whole=False):
         base = tile * 128 - at + begin
         first = base >> 7
         turn = base & 127
@@ -471,6 +472,9 @@
         if k is not None:
             taken = jnp.where(row < 4, partner, taken)
         here = pl.ds(pl.multiple_of(tile * 128, 128), 128)
+        if whole:
+            edges[:, here] = taken
+            return
         spot = tile * 128 + lane
         inside = (spot >= at) & (spot < at + size)
         edges[:, here] = jnp.where(inside, taken, edges[:, here])
@@ -496,22 +500,23 @@
     total = at
     for size, begin, at, k, held, usual in jobs:
         for step in range(usual):
-            place(size, begin, at, k, held, (at >> 7) + step)
+            place(size, begin, at, k, held, (at >> 7) + step, k is None or step > 0)
+    left_over = jnp.int32(0)
     for size, begin, at, k, held, usual in jobs:
-        last = (at + size + 127) >> 7
-
-        def more(tile, carry, size=size, begin=begin, at=at, k=k, held=held):
-            place(size, begin, at, k, held, tile)
-            return carry
-
-        lax.fori_loop((at >> 7) + usual, last, more, 0)
+        left_over = left_over + jnp.maximum(((at + size + 127) >> 7) - (at >> 7) - usual, 0)
+
+    @pl.when(left_over > 0)
+    def _():
+        for size, begin, at, k, held, usual in jobs:
+
+            def more(tile, carry, size=size, begin=begin, at=at, k=k, held=held):
+                place(size, begin, at, k, held, tile)
+                return carry
+
+            lax.fori_loop((at >> 7) + usual, (at + size + 127) >> 7, more, 0)
+
     extra_blocks = lax.div(jnp.maximum(total - (MAIN - LATE), 0) + EXTRA - 1, EXTRA)
 
-    for target, source in zip(
-        (hots, slope, d_value, raw, geo, base),
-        (late_hots, late_slope, late_value, late_raw, late_geo, late_base),
-    ):
-        target[:, 0:LATE] = source[...]
     env[...] = late_env[...]
     g_env[...] = jnp.zeros_like(g_env)
     terms[FIELD:, :] = jnp.zeros((16, 2 * MAIN), BF16)
@@ -576,6 +581,11 @@
         )
 
     listed(first_store, LATE, 0, MAIN - LATE)
+    for target, source in zip(
+        (hots, slope, d_value, raw, geo, base),
+        (late_hots, late_slope, late_value, late_raw, late_geo, late_base),
+    ):
+        target[:, 0:LATE] = source[...]
     rest(lambda begin: listed(more_store, begin, pl.multiple_of(begin + (MAIN - LATE), 256), EXTRA))
     fields[:, 0:ATOM], fields[:, ATOM:] = halves(env[...] * ENV_SCALE)
     second_pass(first_store, 0, MAIN)

time: 33.8 us -> 33.5 us (level)
    pallas_call x1, Pallas kernels: 14.6 us -> 14.1 us  [per_device(): pl.pallas_call(share_kernel, out_shape=(shape((8, PAIR), F32), shape((16,...]
    pallas_call x1, Pallas kernels: 8.24 us -> 8.61 us  [per_device(): pl.pallas_call(return_kernel, out_shape=shape((3, ATOM), F32), in_specs=[...]
where the time goes in v8:
time: 33.5 us; the launch traced here: 33.4 us
  Pallas kernels  31.5 us (94%)
  between operations  1.3 us (4%)
  local copies, waits for them, and re-layouts  0.6 us (2%)
    pallas_call x1, Pallas kernels, per_device(): pl.pallas_call(share_kernel, out_shape=(shape((8, PAIR), F32), shape((16,...  14.1 us
    pallas_call x1, Pallas kernels, edge_call(): pl.pallas_call(edge_kernel, out_shape=(shape((1, ATOM), F32), shape((FIEL...  8.81 us
    pallas_call x1, Pallas kernels, per_device(): pl.pallas_call(return_kernel, out_shape=shape((3, ATOM), F32), in_specs=[...  8.61 us

profile of v8, /device:TPU:1, one launch (start us, length us, event | category | flops | bytes accessed | tf_op | source)
XLA Modules:
  0.0 33.4 jit_solution(4953381592131829327)
XLA Ops:
  1.3 14.1 %shard_map.131 = (f32[8,1024]{1,0:T(8,128)S(1)}, bf16[16,256]{1,0:T(8,128)(2,1)S(1)}, f32[8,8,512]{2,1,0:T(8,128)S(1)}, bf16[128,64]{1,0:T(8,128)(2,1)S(1)}, bf1...) custom-call(s32[1]{0:T(128)S(6)} %copy.15.count_ref, ...), custom_call_target="tpu_custom_call" | custom-call | tf_op jit(solution)/shard_map/pallas_call | solution.py:690
  15.4 8.8 %shard_map.132 = (f32[1,256]{1,0:T(1,128)}, bf16[576,512]{1,0:T(8,128)(2,1)S(1)}, f32[16,256]{1,0:T(8,128)S(1)}, f32[48,256]{1,0:T(8,128)S(1)}, bf16[256,2048]{1...) custom-call(f32[8,1024]{1,0:T(8,128)S(1)} %get-tuple-element.35.own_, ...), custom_call_target="tpu_custom_call" | custom-call | tf_op jit(solution)/shard_map/pallas_call | solution.py:657
  24.2 8.6 %shard_map.133 = f32[3,256]{1,0:T(4,128)S(1)} custom-call(bf16[128,768]{1,0:T(8,128)(2,1)S(1)} %get-tuple-element.32.dn_ref, bf16[16,384]{1,0:T(8,128)(2,1)S(1)} %get-tuple-element.33.wr_ref, f32[128,2]{1,0:T(8,128)S(1)} %get-tuple-element.34.ab_ref, bf16[576,512]{1,0:T(8,128)(2,1)S(1)} %get-tuple-element.51.fields, ...), custom_call_target="tpu_custom_call" | custom-call | tf_op jit(solution)/shard_map/pallas_call | solution.py:749
  32.8 0.6 %copy.16 = f32[3,256]{1,0:T(4,128)} copy(f32[3,256]{1,0:T(4,128)S(1)} %shard_map.133) | data formatting | bytes 6144

commit v9 on v8

--- a/solution.py
+++ b/solution.py
@@ -144,8 +144,10 @@
         pltpu.make_async_copy(source, target, load_sem.at[i])
         for i, (source, target) in enumerate(zip(sources, held))
     ]
+    for load in loads[:5]:
+        load.start()
     barrier, peers = greet()
-    for load in loads:
+    for load in loads[5:]:
         load.start()
     for load in loads[:5]:
         load.wait()
@@ -190,9 +192,7 @@
         axis=0,
     ).astype(BF16)
     for i in range(PAIR // ATOM):
-        rows = lax.broadcasted_iota(I32, (ATOM, PAIR), 0) + i * ATOM
-        chosen = jnp.where(rows == spot, 1.0, 0.0).astype(BF16)
-        ordered = dot_nt(data, chosen)
+        ordered = dot_nt(data, one_hot(spot - i * ATOM, ATOM))
         span = slice(i * ATOM, (i + 1) * ATOM)
         own_ref[0:1, span] = ordered[1:2]
         own_ref[1:2, span] = ordered[2:3] * ATOM + ordered[3:4]

time: 33.5 us -> 33.5 us (level)
  no operation moved by 1% of the time
where the time goes in v9:
time: 33.5 us; the launch traced here: 33.4 us
  Pallas kernels  31.5 us (94%)
  between operations  1.3 us (4%)
  local copies, waits for them, and re-layouts  0.6 us (2%)
    pallas_call x1, Pallas kernels, per_device(): pl.pallas_call(share_kernel, out_shape=(shape((8, PAIR), F32), shape((16,...  14.1 us
    pallas_call x1, Pallas kernels, edge_call(): pl.pallas_call(edge_kernel, out_shape=(shape((1, ATOM), F32), shape((FIEL...  8.8 us
    pallas_call x1, Pallas kernels, per_device(): pl.pallas_call(return_kernel, out_shape=shape((3, ATOM), F32), in_specs=[...  8.6 us

profile of v9, /device:TPU:1, one launch (start us, length us, event | category | flops | bytes accessed | tf_op | source)
XLA Modules:
  0.0 33.4 jit_solution(4049081357627435043)
XLA Ops:
  1.3 14.1 %shard_map.131 = (f32[8,1024]{1,0:T(8,128)S(1)}, bf16[16,256]{1,0:T(8,128)(2,1)S(1)}, f32[8,8,512]{2,1,0:T(8,128)S(1)}, bf16[128,64]{1,0:T(8,128)(2,1)S(1)}, bf1...) custom-call(s32[1]{0:T(128)S(6)} %copy.15.count_ref, ...), custom_call_target="tpu_custom_call" | custom-call | tf_op jit(solution)/shard_map/pallas_call | solution.py:690
  15.4 8.8 %shard_map.132 = (f32[1,256]{1,0:T(1,128)}, bf16[576,512]{1,0:T(8,128)(2,1)S(1)}, f32[16,256]{1,0:T(8,128)S(1)}, f32[48,256]{1,0:T(8,128)S(1)}, bf16[256,2048]{1...) custom-call(f32[8,1024]{1,0:T(8,128)S(1)} %get-tuple-element.35.own_, ...), custom_call_target="tpu_custom_call" | custom-call | tf_op jit(solution)/shard_map/pallas_call | solution.py:657
  24.2 8.6 %shard_map.133 = f32[3,256]{1,0:T(4,128)S(1)} custom-call(bf16[128,768]{1,0:T(8,128)(2,1)S(1)} %get-tuple-element.32.dn_ref, bf16[16,384]{1,0:T(8,128)(2,1)S(1)} %get-tuple-element.33.wr_ref, f32[128,2]{1,0:T(8,128)S(1)} %get-tuple-element.34.ab_ref, bf16[576,512]{1,0:T(8,128)(2,1)S(1)} %get-tuple-element.51.fields, ...), custom_call_target="tpu_custom_call" | custom-call | tf_op jit(solution)/shard_map/pallas_call | solution.py:749
  32.8 0.6 %copy.16 = f32[3,256]{1,0:T(4,128)} copy(f32[3,256]{1,0:T(4,128)S(1)} %shard_map.133) | data formatting | bytes 6144

commit v10 on v9

--- a/solution.py
+++ b/solution.py
@@ -16,7 +16,7 @@
 PI = 3.141592653589793
 DIRECTIONS = ((-1, -1), (-1, 0), (-1, 1), (0, -1), (0, 1), (1, -1), (1, 0), (1, 1))
 NBR = 8
-FAR_FIRST = (0, 7, 2, 5, 3, 4, 1, 6)
+ORDER = tuple(range(NBR))
 ATOM = 256
 GHOST = 64
 PAIR = 1024
@@ -103,7 +103,7 @@
             tuple(lax.rem(at + by + size, size) for at, by, size in zip(here, shift, sizes))
         )
     barrier = pltpu.get_barrier_semaphore()
-    for k in FAR_FIRST:
+    for k in ORDER:
         pl.semaphore_signal(barrier, inc=1, device_id=peers[k], device_id_type=MESH)
     return barrier, peers
 
@@ -121,7 +121,7 @@
                 device_id_type=MESH,
             )
         )
-    for k in FAR_FIRST:
+    for k in ORDER:
         copies[k].start()
     return copies
 
@@ -278,8 +278,8 @@
 
 def scatter(terms, hot, total, count):
     width = hot.shape[1]
-    for part in (slice(0, width), slice(width, 2 * width)):
-        total[0:count, :] += dot_nt(terms[0:count, part], hot)
+    high = dot_nt(terms[0:count, 0:width], hot)
+    total[0:count, :] += high + dot_nt(terms[0:count, width : 2 * width], hot)
 
 
 def first_pass(centre, partner, code, valid, table, store, begin, terms, env, wx_ref, up_ref, ab_ref):

time: 33.5 us -> 33.6 us (level)
    pallas_call x1, Pallas kernels: 14.1 us -> 14.6 us  [per_device(): pl.pallas_call(share_kernel, out_shape=(shape((8, PAIR), F32), shape((16,...]
where the time goes in v10:
time: 33.6 us; the launch traced here: 33.5 us
  Pallas kernels  31.6 us (94%)
  between operations  1.3 us (4%)
  local copies, waits for them, and re-layouts  0.6 us (2%)
    pallas_call x1, Pallas kernels, per_device(): pl.pallas_call(share_kernel, out_shape=(shape((8, PAIR), F32), shape((16,...  14.6 us
    pallas_call x1, Pallas kernels, edge_call(): pl.pallas_call(edge_kernel, out_shape=(shape((1, ATOM), F32), shape((FIEL...  8.74 us
    pallas_call x1, Pallas kernels, per_device(): pl.pallas_call(return_kernel, out_shape=shape((3, ATOM), F32), in_specs=[...  8.27 us

profile of v10, /device:TPU:1, one launch (start us, length us, event | category | flops | bytes accessed | tf_op | source)
XLA Modules:
  0.0 33.5 jit_solution(11115260826828571076)
XLA Ops:
  1.3 14.6 %shard_map.131 = (f32[8,1024]{1,0:T(8,128)S(1)}, bf16[16,256]{1,0:T(8,128)(2,1)S(1)}, f32[8,8,512]{2,1,0:T(8,128)S(1)}, bf16[128,64]{1,0:T(8,128)(2,1)S(1)}, bf1...) custom-call(s32[1]{0:T(128)S(6)} %copy.15.count_ref, ...), custom_call_target="tpu_custom_call" | custom-call | tf_op jit(solution)/shard_map/pallas_call | solution.py:690
  15.9 8.7 %shard_map.132 = (f32[1,256]{1,0:T(1,128)}, bf16[576,512]{1,0:T(8,128)(2,1)S(1)}, f32[16,256]{1,0:T(8,128)S(1)}, f32[48,256]{1,0:T(8,128)S(1)}, bf16[256,2048]{1...) custom-call(f32[8,1024]{1,0:T(8,128)S(1)} %get-tuple-element.35.own_, ...), custom_call_target="tpu_custom_call" | custom-call | tf_op jit(solution)/shard_map/pallas_call | solution.py:657
  24.7 8.3 %shard_map.133 = f32[3,256]{1,0:T(4,128)S(1)} custom-call(bf16[128,768]{1,0:T(8,128)(2,1)S(1)} %get-tuple-element.32.dn_ref, bf16[16,384]{1,0:T(8,128)(2,1)S(1)} %get-tuple-element.33.wr_ref, f32[128,2]{1,0:T(8,128)S(1)} %get-tuple-element.34.ab_ref, bf16[576,512]{1,0:T(8,128)(2,1)S(1)} %get-tuple-element.51.fields, ...), custom_call_target="tpu_custom_call" | custom-call | tf_op jit(solution)/shard_map/pallas_call | solution.py:749
  32.9 0.6 %copy.16 = f32[3,256]{1,0:T(4,128)} copy(f32[3,256]{1,0:T(4,128)S(1)} %shard_map.133) | data formatting | bytes 6144
